TPU v7x, 128 devices: a whole 4x4x4 slice. The times are simulated.
128 devices in a mesh: slab: 8 (over x, core), tile: 16 (over z, y).
Axes of the slice: x: 4, y: 4, z: 4, core: 2. Of those that a mesh axis runs over, the one named last changes fastest.
Arguments:
- soil_diag: float32 [4096, 128, 128], P(('slab', 'tile'))
- soil_off: float32 [4096, 4, 128, 128], P(('slab', 'tile')), may hold values from -0.3125 to 0.3125
- soil_pre: float32 [4096, 128, 128], P(('slab', 'tile'))
- own_cols: int32 [4096, 2], P(('slab', 'tile')), may hold values from 0 to 31
- margin_slot: int32 [4096], P(('slab', 'tile')), may hold values from 0 to 31
- vertical_col: int32 [4096], P(('slab', 'tile')), may hold values from 0 to 63, as said below
- fetch_rows: int32 [128, 16, 2], P(('slab', 'tile')), may hold values from 0 to 31
- soil_rhs: float32 [4096, 128], P(('slab', 'tile')), may hold values from -6 to 6
- root_diag: float32 [1024, 128, 128], P(('slab', 'tile'))
- root_pre: float32 [1024, 128, 128], P(('slab', 'tile'))
- root_up: float32 [1024, 128, 128], P(('slab', 'tile')), may hold values from -0.3125 to 0.3125
- root_down: float32 [1024, 128, 128], P(('slab', 'tile')), may hold values from -0.3125 to 0.3125
- root_cell: int32 [1024], P(('slab', 'tile')), may hold values from 0 to 31
- root_count: int32 [128], P(('slab', 'tile')), may hold values from 1 to 8, as said below
- root_rhs: float32 [1024, 128], P(('slab', 'tile')), may hold values from -6 to 6
Outputs:
- soil_solution: float32 [4096, 128], P(('slab', 'tile'))
- root_solution: float32 [1024, 128], P(('slab', 'tile'))
- soil_residual: float32 [4096, 128], P(('slab', 'tile'))
Inputs may be any that keep to these rules, and one draw needn't show every extreme that they name: `fetch_rows`: entry [d, p, c] names a block of the brick in the same slab at tile p. `vertical_col`: values below 32 couple to the slab beneath, others to the slab above; rows of the first slab always couple upward and of the last slab downward. `root_count`: some brick has all 8 slots live.
All inputs are finite; a program needn't handle non-finite values.
Results may differ from a plain program's by a relative error of at most 0.00014.
Values sent between devices are 32-bit elements; how exact they have to be, the bound alone decides.
No kernel may reach another device: no remote copies, remote signals or barrier semaphores. Data moves between devices by JAX's collectives and lax.ppermute only.
A program may use at most 64 MiB of HBM per device.

v0:
```python
import functools

import jax
import jax.numpy as jnp
from jax import lax
from jax.experimental import pallas as pl
from jax.experimental.pallas import tpu as pltpu
from jax.sharding import PartitionSpec as P

SWEEPS = 3
LOW_BOUND = 0.25
HIGH_BOUND = 2.0
THETA = (HIGH_BOUND + LOW_BOUND) / 2.0
DELTA = (HIGH_BOUND - LOW_BOUND) / 2.0
SIGMA = THETA / DELTA

B = 128
NBD = 32
RCAP = 8
TILES = 16
CAP = 2
SLOTS = TILES * CAP
PIECE = NBD + 8
F32 = jnp.float32

VMEM = pl.BlockSpec(memory_space=pltpu.VMEM)
SMEM = pl.BlockSpec(memory_space=pltpu.SMEM)


def row_sum(acc):
    lane = lax.broadcasted_iota(jnp.int32, (8, B), 1)
    sub = lax.broadcasted_iota(jnp.int32, (8, B), 0)
    ahead = lane - sub
    sums = jnp.sum(acc.reshape(B // 8, 8, B), axis=2, keepdims=True)
    out = jnp.zeros((8, B), F32)
    for k in range(B // 8):
        out = jnp.where(ahead == 8 * k, sums[k], out)
    return jnp.sum(out, axis=0, keepdims=True)


def product(*pairs):
    acc = None
    for mat, vec in pairs:
        term = mat * vec
        acc = term if acc is None else acc + term
    return row_sum(acc)


def row(ref, index):
    return ref[pl.ds(index, 1), :]


def pick(choice, values):
    return jnp.dot(
        choice[:, :NBD], values, precision=lax.Precision.HIGHEST, preferred_element_type=F32
    )


def first_kernel(fetch, pre, rhs, t_out, send):
    for g in range(NBD):
        t_out[g : g + 1, :] = product((pre[g], rhs[g : g + 1, :]))
    t = t_out[...]
    sub = lax.broadcasted_iota(jnp.int32, (8, B), 0)
    for p in range(TILES):
        send[p, :NBD, :] = t
        asked = jnp.where(sub == 0, fetch[0, p, 0], fetch[0, p, 1])
        send[p, NBD:, :] = asked.astype(F32)


def extended_rows(own, near_row, diag, off, pre, t, res, w):
    for g in range(NBD):
        w[g : g + 1, :] = res[g : g + 1, :] - product(
            (diag[g], t[g : g + 1, :]),
            (off[g, 0], row(t, own[g, 0])),
            (off[g, 1], row(t, own[g, 1])),
            (off[g, 2], near_row(g)),
        )


def first_step_kernel(
    own, margin, fetch, count, diag, off, pre, t, table, rhs, root_pre, root_rhs,
    s_out, send, choice, ur_out, w,
):
    def near_row(g):
        slot = margin[g]
        peer = slot // CAP
        return table[peer, pl.ds(fetch[0, peer, slot % CAP], 1), :]

    extended_rows(own, near_row, diag, off, pre, t, rhs, w)
    for g in range(NBD):
        z = t[g : g + 1, :] + product((pre[g], w[g : g + 1, :]))
        s_out[g : g + 1, :] = z * (1.0 / THETA)
    lane = lax.broadcasted_iota(jnp.int32, (CAP, B), 1).astype(F32)
    for p in range(TILES):
        choice[CAP * p : CAP * (p + 1), :] = (table[p, NBD : NBD + CAP, :] == lane).astype(F32)
    send[...] = pick(choice[...], s_out[...])
    for r in range(RCAP):
        z = product((root_pre[r], root_rhs[r : r + 1, :]))
        ur_out[r : r + 1, :] = jnp.where(r < count[0], z * (1.0 / THETA), 0.0)


def step_kernel(
    keep, gain, own, margin, diag, off, pre, t, table, res, s_in, x_in, choice,
    s_out, x_out, send, w,
):
    extended_rows(own, lambda g: row(table, margin[g]), diag, off, pre, t, res, w)
    for g in range(NBD):
        z = t[g : g + 1, :] + product((pre[g], w[g : g + 1, :]))
        s = keep * s_in[g : g + 1, :] + gain * z
        s_out[g : g + 1, :] = s
        x_out[g : g + 1, :] = x_in[g : g + 1, :] + s
    send[...] = pick(choice[...], s_out[...])


def residual_rows(own, margin, vert, odd, cell, diag, off, down, s, table, core, chip, res, ur, r_out):
    r_out[...] = res[...]
    for r in range(RCAP):
        at = pl.ds(cell[r], 1)
        r_out[at, :] = r_out[at, :] - product((down[r], ur[r : r + 1, :]))
    for g in range(NBD):
        place = vert[g] % NBD
        below = (vert[g] < NBD).astype(jnp.int32)
        over = jnp.where(below == odd[0], row(core, place), row(chip, place))
        r_out[g : g + 1, :] = r_out[g : g + 1, :] - product(
            (diag[g], s[g : g + 1, :]),
            (off[g, 0], row(s, own[g, 0])),
            (off[g, 1], row(s, own[g, 1])),
            (off[g, 2], row(table, margin[g])),
            (off[g, 3], over),
        )


def residual_kernel(
    keep, gain, own, margin, vert, odd, cell, count,
    diag, off, pre, root_diag, root_pre, root_up, down,
    s, table, core, chip, res, ur, rr, root_x, choice,
    t_out, r_out, ur_out, rr_out, root_x_out, send,
):
    residual_rows(own, margin, vert, odd, cell, diag, off, down, s, table, core, chip, res, ur, r_out)
    for g in range(NBD):
        t_out[g : g + 1, :] = product((pre[g], r_out[g : g + 1, :]))
    send[...] = pick(choice[...], t_out[...])
    for r in range(RCAP):
        change = product((root_diag[r], ur[r : r + 1, :]), (root_up[r], row(s, cell[r])))
        rr_out[r : r + 1, :] = rr[r : r + 1, :] - change
    for r in range(RCAP):
        z = product((root_pre[r], rr_out[r : r + 1, :]))
        new = jnp.where(r < count[0], keep * ur[r : r + 1, :] + gain * z, 0.0)
        ur_out[r : r + 1, :] = new
        root_x_out[r : r + 1, :] = root_x[r : r + 1, :] + new


def last_kernel(
    own, margin, vert, odd, cell, diag, off, down, s, table, core, chip, res, ur, r_out
):
    residual_rows(own, margin, vert, odd, cell, diag, off, down, s, table, core, chip, res, ur, r_out)


def call(kernel, name, scalars, arrays, outs, scratch=()):
    return pl.pallas_call(
        kernel,
        out_shape=tuple(jax.ShapeDtypeStruct(shape, F32) for shape in outs),
        in_specs=[SMEM] * len(scalars) + [VMEM] * len(arrays),
        out_specs=(VMEM,) * len(outs),
        scratch_shapes=[pltpu.VMEM(shape, F32) for shape in scratch],
        compiler_params=pltpu.CompilerParams(vmem_limit_bytes=4 * 2**20),
        name=name,
    )(*scalars, *arrays)


def body(
    soil_diag, soil_off, soil_pre, own_cols, margin_slot, vertical_col, fetch_rows, soil_rhs,
    root_diag, root_pre, root_up, root_down, root_cell, root_count, root_rhs,
):
    slabs = lax.axis_size("slab")
    odd = (lax.axis_index("slab") % 2).astype(jnp.int32).reshape(1)
    soil, root, table = (NBD, B), (RCAP, B), (SLOTS, B)

    def exchange(rows):
        got = lax.all_to_all(rows.reshape(TILES, CAP, B), "tile", 0, 0)
        return got.reshape(SLOTS, B)

    def vertical(s):
        core = lax.ppermute(s, "slab", [(i, i ^ 1) for i in range(slabs)])
        up = [(i, i + 1) for i in range(1, slabs - 1, 2)]
        chip = lax.ppermute(s, "slab", up + [(j, i) for i, j in up])
        return core, chip

    t, send = call(
        first_kernel, "first", (fetch_rows,), (soil_pre, soil_rhs), (soil, (TILES, PIECE, B))
    )
    got = lax.all_to_all(send, "tile", 0, 0)
    s, send, choice, ur = call(
        first_step_kernel, "step0",
        (own_cols, margin_slot, fetch_rows, root_count),
        (soil_diag, soil_off, soil_pre, t, got, soil_rhs, root_pre, root_rhs),
        (soil, table, table, root), (soil,),
    )
    x, r, rr, root_x = s, soil_rhs, root_rhs, ur
    rho = 1.0 / SIGMA
    for sweep in range(SWEEPS):
        core, chip = vertical(s)
        got = exchange(send)
        scalars = (own_cols, margin_slot, vertical_col, odd, root_cell)
        if sweep + 1 == SWEEPS:
            (r,) = call(
                last_kernel, "last", scalars,
                (soil_diag, soil_off, root_down, s, got, core, chip, r, ur), (soil,),
            )
            break
        rho_new = 1.0 / (2.0 * SIGMA - rho)
        keep, gain = rho_new * rho, 2.0 * rho_new / DELTA
        rho = rho_new
        t, r, ur, rr, root_x, send = call(
            functools.partial(residual_kernel, keep, gain), f"residual{sweep}",
            scalars + (root_count,),
            (soil_diag, soil_off, soil_pre, root_diag, root_pre, root_up, root_down,
             s, got, core, chip, r, ur, rr, root_x, choice),
            (soil, soil, root, root, root, table),
        )
        got = exchange(send)
        s, x, send = call(
            functools.partial(step_kernel, keep, gain), f"step{sweep + 1}",
            (own_cols, margin_slot),
            (soil_diag, soil_off, soil_pre, t, got, r, s, x, choice),
            (soil, soil, table), (soil,),
        )
    return x, root_x, r


def solution(mesh):
    split = P(("slab", "tile"))
    return jax.shard_map(
        body, mesh=mesh, in_specs=(split,) * 15, out_specs=(split,) * 3, check_vma=False
    )
```

profile of v0, /device:TPU:1, one launch (start us, length us, event | category | flops | bytes accessed | tf_op | source)
XLA Modules:
  0.0 119.7 jit_solution(9429985429539461347)
XLA Ops:
  0.6 0.0 copy-start.27
  0.6 0.0 copy-start.16
  0.7 0.0 copy-start.20
  0.7 0.8 copy.20.fetch
  1.4 1.6 %copy-done.3 = f32[32,128,128]{2,1,0:T(8,128)S(1)} copy-done((f32[32,128,128]{2,1,0:T(8,128)S(1)}, f32[32,128,128]{2,1,0:T(8,128)}, u32[]{:S(2)}) %copy-start.3) | copy-done | bytes 2097176
  3.0 0.7 copy-done.14
  3.8 2.0 %first.1 = (f32[32,128]{1,0:T(8,128)S(1)}, f32[16,40,128]{2,1,0:T(8,128)}) custom-call(s32[1,16,2]{2,1,0:T(8,128)S(1)} %copy.20.fetch, f32[32,128,128]{2,1,0:T(8,128)S(1)} %copy-done.3, f32[32,128]{1,0:T(8,128)S(1)} %copy-done.14), custom_call_target="tpu_custom_call" | custom-call | tf_op jit(solution)/shard_map/first/pallas_call | solution.py:160
  5.8 0.6 copy-done.17
  6.4 8.6 %all-to-all-start = ((f32[16,40,128]{2,1,0:T(8,128)}), f32[16,40,128]{2,1,0:T(8,128)S(1)}, u32[]{:S(2)}, u32[]{:S(2)}) async-start(f32[16,40,128]{2,1,0:T(8,128)} %get-tuple-element.27), calls=%async_computation | async-start | bytes 655360 | tf_op jit(solution)/shard_map/all_to_all | solution.py:192
  15.0 0.0 copy-done.27
  15.0 0.1 copy.24.own
  15.7 7.7 %all-to-all-done.table = f32[16,40,128]{2,1,0:T(8,128)S(1)} async-done(((f32[16,40,128]{2,1,0:T(8,128)}), f32[16,40,128]{2,1,0:T(8,128)S(1)}, u32[]{:S(2)}, u32[]{:S(2)}) %all-to-all-start) | async-done | bytes 327712 | tf_op jit(solution)/shard_map/all_to_all | solution.py:192
  23.5 0.0 copy-done.16
  23.5 0.0 copy-done.20
  23.5 0.0 copy-done.4
  23.5 0.0 copy-done.8
  23.5 0.0 copy-done.15
  23.5 0.0 copy-start
  23.5 3.4 %copy-done = f32[32,4,128,128]{3,2,1,0:T(8,128)S(1)} copy-done((f32[32,4,128,128]{3,2,1,0:T(8,128)S(1)}, f32[32,4,128,128]{3,2,1,0:T(8,128)}, u32[]{:S(2)}) %copy-start) | copy-done | bytes 8388632
  26.9 1.6 %copy-done.5 = f32[32,128,128]{2,1,0:T(8,128)S(1)} copy-done((f32[32,128,128]{2,1,0:T(8,128)S(1)}, f32[32,128,128]{2,1,0:T(8,128)}, u32[]{:S(2)}) %copy-start.5) | copy-done | bytes 2097176
  28.5 0.7 copy-done.18
  29.2 2.3 %step0.1 = (f32[32,128]{1,0:T(8,128)S(1)}, f32[32,128]{1,0:T(8,128)S(1)}, f32[32,128]{1,0:T(8,128)S(1)}, f32[8,128]{1,0:T(8,128)S(1)}) custom-call(s32[32,2]{1,0:T(8,128)S(1)} %copy.24.own, s32[32]{0:T(128)S(1)} %copy-done.16, s32[1,16,2]{2,1,0:T(8,128)S(1)} %copy.20.fetch, s32[1]{0:T(128)S(6)} %copy.26.count, f32[32,128,128]{2,1,0:T(8,128)S(1)} %copy-done.5, ...), custom_call_target="tpu_custom_call" | custom-call | tf_op jit(solution)/shard_map/step0/pallas_call | solution.py:160
  31.5 0.0 copy-start.19
  31.5 0.6 copy-done.19
  32.1 0.6 copy-done.21
  32.7 1.9 %collective-permute-start = (f32[32,128]{1,0:T(8,128)S(1)}, f32[32,128]{1,0:T(8,128)S(1)}, u32[]{:S(2)}, u32[]{:S(2)}) collective-permute-start(f32[32,128]{1,0:T(8,128)S(1)} %get-tuple-element.28.s.s_in.x_in), channel_id=1, source_target_pairs={{0,16},{16,0},{32,48},{48,32},{64,80},{80,64},{96,112},{112,96},{1... | collective-permute-start | bytes 49160 | tf_op jit(solution)/shard_map/ppermute | solution.py:184
  34.5 3.0 %collective-permute-start.1 = (f32[32,128]{1,0:T(8,128)S(1)}, f32[32,128]{1,0:T(8,128)S(1)}, u32[]{:S(2)}, u32[]{:S(2)}) collective-permute-start(f32[32,128]{1,0:T(8,128)S(1)} %get-tuple-element.28.s.s_in.x_in), channel_id=1, source_target_pairs={{16,32},{48,64},{80,96},{32,16},{64,48},{96,80},{17,33},{49,65},{8... | collective-permute-start | bytes 49160 | tf_op jit(solution)/shard_map/ppermute | solution.py:186
  37.6 3.5 %all-to-all-start.1 = ((f32[16,2,128]{2,1,0:T(2,128)}), f32[16,2,128]{2,1,0:T(2,128)S(1)}, u32[]{:S(2)}, u32[]{:S(2)}) async-start(f32[16,2,128]{2,1,0:T(2,128)} %bitcast.18), calls=%async_computation.1 | async-start | bytes 32768 | tf_op jit(solution)/shard_map/all_to_all | solution.py:180
  41.1 6.4 %all-to-all-done.1 = f32[16,2,128]{2,1,0:T(2,128)S(1)} async-done(((f32[16,2,128]{2,1,0:T(2,128)}), f32[16,2,128]{2,1,0:T(2,128)S(1)}, u32[]{:S(2)}, u32[]{:S(2)}) %all-to-all-start.1) | async-done | bytes 16416 | tf_op jit(solution)/shard_map/all_to_all | solution.py:180
  47.4 0.0 collective-permute-done.core
  47.4 0.0 collective-permute-done.1.chip
  47.4 0.0 copy-done.9
  47.5 0.0 copy-start.1
  47.5 3.4 %copy-done.1 = f32[32,4,128,128]{3,2,1,0:T(8,128)S(1)} copy-done((f32[32,4,128,128]{3,2,1,0:T(8,128)S(1)}, f32[32,4,128,128]{3,2,1,0:T(8,128)}, u32[]{:S(2)}) %copy-start.1) | copy-done | bytes 8388632
  50.8 1.6 %copy-done.6 = f32[32,128,128]{2,1,0:T(8,128)S(1)} copy-done((f32[32,128,128]{2,1,0:T(8,128)S(1)}, f32[32,128,128]{2,1,0:T(8,128)}, u32[]{:S(2)}) %copy-start.6) | copy-done | bytes 2097176
  52.4 1.0 copy-done.10
  53.5 1.0 copy-done.12
  54.5 0.7 copy-done.22
  55.2 0.7 copy-done.23
  55.9 0.7 copy-done.25
  56.5 2.6 %residual0.1 = (f32[32,128]{1,0:T(8,128)S(1)}, f32[32,128]{1,0:T(8,128)S(1)}, f32[8,128]{1,0:T(8,128)S(1)}, f32[8,128]{1,0:T(8,128)S(1)}, f32[8,128]{1,0:T(8,128)S(1)}, /*index=5*/f32[32,128]{1,0:T(8,128)S(1)}) custom-call(s32[32,2]{1,0:T(8,128)S(1)} %copy.24.own, s32[32]{0:T(128)S(1)} %copy-done.16, s32[32]{0:T(128)S(1)} %copy-done.23, s32[1]{0:T(128)} %bitcast.odd, ...), custom_call_target="tpu_custom_call" | custom-call | tf_op jit(solution)/shard_map/residual0/pallas_call | solution.py:160
  59.1 9.2 %all_to_all.30 = f32[16,2,128]{2,1,0:T(2,128)S(1)} all-to-all(f32[16,2,128]{2,1,0:T(2,128)S(1)} %bitcast.22), channel_id=1, replica_groups=mesh['slab'=8,'tile'=16] {'tile'}, dimensions={0} | all-to-all | bytes 32768 | tf_op jit(solution)/shard_map/all_to_all | solution.py:180
  68.3 3.4 %copy-done.2 = f32[32,4,128,128]{3,2,1,0:T(8,128)S(1)} copy-done((f32[32,4,128,128]{3,2,1,0:T(8,128)S(1)}, f32[32,4,128,128]{3,2,1,0:T(8,128)}, u32[]{:S(2)}) %copy-start.2) | copy-done | bytes 8388632
  71.7 2.1 %step1.1 = (f32[32,128]{1,0:T(8,128)S(1)}, f32[32,128]{1,0:T(8,128)S(1)}, f32[32,128]{1,0:T(8,128)S(1)}) custom-call(s32[32,2]{1,0:T(8,128)S(1)} %copy.24.own, s32[32]{0:T(128)S(1)} %copy-done.16, f32[32,128,128]{2,1,0:T(8,128)S(1)} %copy-done.6, f32[32,4,128,128]{3,2,1,0:T(8,128)S(1)} %copy-done.2, f32[32,128,128]{2,1,0:T(8,128)S(1)} %copy-done.4, ...), custom_call_target="tpu_custom_call" | custom-call | tf_op jit(solution)/shard_map/step1/pallas_call | solution.py:160
  73.9 0.3 collective-permute-start.2
  74.1 4.9 %collective-permute-start.3 = (f32[32,128]{1,0:T(8,128)S(1)}, f32[32,128]{1,0:T(8,128)S(1)}, u32[]{:S(2)}, u32[]{:S(2)}) collective-permute-start(f32[32,128]{1,0:T(8,128)S(1)} %get-tuple-element.35.s.s_in), channel_id=1, source_target_pairs={{16,32},{48,64},{80,96},{32,16},{64,48},{96,80},{17,33},{49,65},{8... | collective-permute-start | bytes 49160 | tf_op jit(solution)/shard_map/ppermute | solution.py:186
  79.1 9.2 %all_to_all.31 = f32[16,2,128]{2,1,0:T(2,128)S(1)} all-to-all(f32[16,2,128]{2,1,0:T(2,128)S(1)} %bitcast.20), channel_id=1, replica_groups=mesh['slab'=8,'tile'=16] {'tile'}, dimensions={0} | all-to-all | bytes 32768 | tf_op jit(solution)/shard_map/all_to_all | solution.py:180
  88.2 0.0 collective-permute-done.2.core
  88.2 0.0 collective-permute-done.3.chip
  88.2 0.0 copy-done.11
  88.3 0.0 copy-done.13
  88.3 0.0 copy-done.24
  88.3 0.0 slice-start.1
  88.3 3.2 %residual1.1 = (f32[32,128]{1,0:T(8,128)S(1)}, f32[32,128]{1,0:T(8,128)S(1)}, f32[8,128]{1,0:T(8,128)S(1)}, f32[8,128]{1,0:T(8,128)}, f32[8,128]{1,0:T(8,128)}, /*index=5*/f32[32,128]{1,0:T(8,128)S(1)}) custom-call(s32[32,2]{1,0:T(8,128)S(1)} %copy.24.own, s32[32]{0:T(128)S(1)} %copy-done.16, s32[32]{0:T(128)S(1)} %copy-done.24, s32[1]{0:T(128)} %bitcast.odd, ...), custom_call_target="tpu_custom_call" | custom-call | tf_op jit(solution)/shard_map/residual1/pallas_call | solution.py:160
  91.5 9.2 %all_to_all.32 = f32[16,2,128]{2,1,0:T(2,128)S(1)} all-to-all(f32[16,2,128]{2,1,0:T(2,128)S(1)} %bitcast.21), channel_id=1, replica_groups=mesh['slab'=8,'tile'=16] {'tile'}, dimensions={0} | all-to-all | bytes 32768 | tf_op jit(solution)/shard_map/all_to_all | solution.py:180
  100.7 2.6 %step2.1 = (f32[32,128]{1,0:T(8,128)S(1)}, f32[32,128]{1,0:T(8,128)}, f32[32,128]{1,0:T(8,128)S(1)}) custom-call(s32[32,2]{1,0:T(8,128)S(1)} %copy.24.own, s32[32]{0:T(128)S(1)} %copy-done.16, f32[32,128,128]{2,1,0:T(8,128)S(1)} %copy-done.6, f32[32,4,128,128]{3,2,1,0:T(8,128)S(1)} %copy-done.2, f32[32,128,128]{2,1,0:T(8,128)S(1)} %copy-done.4, ...), custom_call_target="tpu_custom_call" | custom-call | tf_op jit(solution)/shard_map/step2/pallas_call | solution.py:160
  103.3 0.0 collective-permute-start.4
  103.3 4.8 %collective-permute-start.5 = (f32[32,128]{1,0:T(8,128)S(1)}, f32[32,128]{1,0:T(8,128)S(1)}, u32[]{:S(2)}, u32[]{:S(2)}) collective-permute-start(f32[32,128]{1,0:T(8,128)S(1)} %get-tuple-element.46.s), channel_id=1, source_target_pairs={{16,32},{48,64},{80,96},{32,16},{64,48},{96,80},{17,33},{49,65},{8... | collective-permute-start | bytes 49160 | tf_op jit(solution)/shard_map/ppermute | solution.py:186
  108.1 9.2 %all_to_all.33 = f32[16,2,128]{2,1,0:T(2,128)S(1)} all-to-all(f32[16,2,128]{2,1,0:T(2,128)S(1)} %bitcast.19), channel_id=1, replica_groups=mesh['slab'=8,'tile'=16] {'tile'}, dimensions={0} | all-to-all | bytes 32768 | tf_op jit(solution)/shard_map/all_to_all | solution.py:180
  117.2 0.0 collective-permute-done.4.core
  117.2 0.0 collective-permute-done.5.chip
  117.2 0.0 slice-done.1
  117.3 0.0 copy-done.7
  117.3 2.4 %last.1 = f32[32,128]{1,0:T(8,128)} custom-call(s32[32,2]{1,0:T(8,128)S(1)} %copy.24.own, s32[32]{0:T(128)S(1)} %copy-done.16, s32[32]{0:T(128)S(1)} %copy-done.24, s32[1]{0:T(128)} %bitcast.odd, s32[8]{0:T(128)S(1)} %copy-done.26, f32[32,128,128]{2,1,0:T(8,128)S(1)} %copy-done.7, f32[32,4,128,128]{3,2,1,0:T(8,128)S(1)} %bitcast.12, ...), custom_call_target="tpu_custom_call" | custom-call | tf_op jit(solution)/shard_map/last/pallas_call | solution.py:160
  (26 shorter events, 0.0 us)
Async XLA Ops:
  0.6 14.3 %copy-start.27 = (s32[32,2]{0,1:T(2,128)S(1)}, s32[32,2]{0,1:T(2,128)}, u32[]{:S(2)}) copy-start(s32[32,2]{0,1:T(2,128)} %param.18) | copy-start | bytes 772
  0.6 22.8 %copy-start.16 = (s32[32]{0:T(128)S(1)}, s32[32]{0:T(128)}, u32[]{:S(2)}) copy-start(s32[32]{0:T(128)} %margin.11) | copy-start | bytes 388
  0.7 22.8 %copy-start.20 = (f32[8,128]{1,0:T(8,128)S(1)}, f32[8,128]{1,0:T(8,128)}, u32[]{:S(2)}) copy-start(f32[8,128]{1,0:T(8,128)} %rr.1) | copy-start | bytes 12292
  1.4 1.6 %copy-start.3 = (f32[32,128,128]{2,1,0:T(8,128)S(1)}, f32[32,128,128]{2,1,0:T(8,128)}, u32[]{:S(2)}) copy-start(f32[32,128,128]{2,1,0:T(8,128)} %pre.11) | copy-start | bytes 6291460
  3.0 0.7 copy-start.14
  3.7 19.7 %copy-start.4 = (f32[32,128,128]{2,1,0:T(8,128)S(1)}, f32[32,128,128]{2,1,0:T(8,128)}, u32[]{:S(2)}) copy-start(f32[32,128,128]{2,1,0:T(8,128)} %pre.11) | copy-start | bytes 6291460
  3.7 19.7 %copy-start.8 = (f32[8,128,128]{2,1,0:T(8,128)S(1)}, f32[8,128,128]{2,1,0:T(8,128)}, u32[]{:S(2)}) copy-start(f32[8,128,128]{2,1,0:T(8,128)} %root_pre.5) | copy-start | bytes 1572868
  3.7 19.7 %copy-start.15 = (f32[32,128]{1,0:T(8,128)S(1)}, f32[32,128]{1,0:T(8,128)}, u32[]{:S(2)}) copy-start(f32[32,128]{1,0:T(8,128)} %res.1) | copy-start | bytes 49156
  5.8 0.6 copy-start.17
  6.4 17.1 %all-to-all-start = ((f32[16,40,128]{2,1,0:T(8,128)}), f32[16,40,128]{2,1,0:T(8,128)S(1)}, u32[]{:S(2)}, u32[]{:S(2)}) async-start(f32[16,40,128]{2,1,0:T(8,128)} %get-tuple-element.27), calls=%async_computation | async-start | bytes 655360 | tf_op jit(solution)/shard_map/all_to_all | solution.py:192
  23.5 3.4 %copy-start = (f32[32,4,128,128]{3,2,1,0:T(8,128)S(1)}, f32[32,4,128,128]{3,2,1,0:T(8,128)}, u32[]{:S(2)}) copy-start(f32[32,4,128,128]{3,2,1,0:T(8,128)} %off.11) | copy-start | bytes 25165828
  26.9 1.6 %copy-start.5 = (f32[32,128,128]{2,1,0:T(8,128)S(1)}, f32[32,128,128]{2,1,0:T(8,128)}, u32[]{:S(2)}) copy-start(f32[32,128,128]{2,1,0:T(8,128)} %diag.11) | copy-start | bytes 6291460
  28.5 0.7 copy-start.18
  29.2 18.3 %copy-start.9 = (f32[8,128,128]{2,1,0:T(8,128)S(1)}, f32[8,128,128]{2,1,0:T(8,128)}, u32[]{:S(2)}) copy-start(f32[8,128,128]{2,1,0:T(8,128)} %down.5) | copy-start | bytes 1572868
  31.5 0.6 copy-start.19
  32.1 0.6 copy-start.21
  32.7 14.8 %collective-permute-start = (f32[32,128]{1,0:T(8,128)S(1)}, f32[32,128]{1,0:T(8,128)S(1)}, u32[]{:S(2)}, u32[]{:S(2)}) collective-permute-start(f32[32,128]{1,0:T(8,128)S(1)} %get-tuple-element.28.s.s_in.x_in), channel_id=1, source_target_pairs={{0,16},{16,0},{32,48},{48,32},{64,80},{80,64},{96,112},{112,96},{1... | collective-permute-start | bytes 49160 | tf_op jit(solution)/shard_map/ppermute | solution.py:184
  34.5 12.9 %collective-permute-start.1 = (f32[32,128]{1,0:T(8,128)S(1)}, f32[32,128]{1,0:T(8,128)S(1)}, u32[]{:S(2)}, u32[]{:S(2)}) collective-permute-start(f32[32,128]{1,0:T(8,128)S(1)} %get-tuple-element.28.s.s_in.x_in), channel_id=1, source_target_pairs={{16,32},{48,64},{80,96},{32,16},{64,48},{96,80},{17,33},{49,65},{8... | collective-permute-start | bytes 49160 | tf_op jit(solution)/shard_map/ppermute | solution.py:186
  37.6 9.9 %all-to-all-start.1 = ((f32[16,2,128]{2,1,0:T(2,128)}), f32[16,2,128]{2,1,0:T(2,128)S(1)}, u32[]{:S(2)}, u32[]{:S(2)}) async-start(f32[16,2,128]{2,1,0:T(2,128)} %bitcast.18), calls=%async_computation.1 | async-start | bytes 32768 | tf_op jit(solution)/shard_map/all_to_all | solution.py:180
  47.5 3.4 %copy-start.1 = (f32[32,4,128,128]{3,2,1,0:T(8,128)S(1)}, f32[32,4,128,128]{3,2,1,0:T(8,128)}, u32[]{:S(2)}) copy-start(f32[32,4,128,128]{3,2,1,0:T(8,128)} %off.11) | copy-start | bytes 25165828
  50.8 1.6 %copy-start.6 = (f32[32,128,128]{2,1,0:T(8,128)S(1)}, f32[32,128,128]{2,1,0:T(8,128)}, u32[]{:S(2)}) copy-start(f32[32,128,128]{2,1,0:T(8,128)} %diag.11) | copy-start | bytes 6291460
  52.4 1.0 copy-start.10
  53.5 1.0 copy-start.12
  54.5 0.7 copy-start.22
  55.2 0.7 copy-start.23
  55.9 0.7 copy-start.25
  68.3 3.4 %copy-start.2 = (f32[32,4,128,128]{3,2,1,0:T(8,128)S(1)}, f32[32,4,128,128]{3,2,1,0:T(8,128)}, u32[]{:S(2)}) copy-start(f32[32,4,128,128]{3,2,1,0:T(8,128)} %off.11) | copy-start | bytes 25165828
  71.7 16.6 %copy-start.11 = (f32[8,128,128]{2,1,0:T(8,128)S(1)}, f32[8,128,128]{2,1,0:T(8,128)}, u32[]{:S(2)}) copy-start(f32[8,128,128]{2,1,0:T(8,128)} %root_diag.3) | copy-start | bytes 1572868
  71.7 16.6 %copy-start.13 = (f32[8,128,128]{2,1,0:T(8,128)S(1)}, f32[8,128,128]{2,1,0:T(8,128)}, u32[]{:S(2)}) copy-start(f32[8,128,128]{2,1,0:T(8,128)} %root_up.3) | copy-start | bytes 1572868
  71.7 16.6 %copy-start.24 = (s32[32]{0:T(128)S(1)}, s32[32]{0:T(128)}, u32[]{:S(2)}) copy-start(s32[32]{0:T(128)} %vert.5) | copy-start | bytes 388
  71.7 16.6 %copy-start.26 = (s32[8]{0:T(128)S(1)}, s32[8]{0:T(128)}, u32[]{:S(2)}) copy-start(s32[8]{0:T(128)} %cell.5) | copy-start | bytes 100
  73.9 14.4 %collective-permute-start.2 = (f32[32,128]{1,0:T(8,128)S(1)}, f32[32,128]{1,0:T(8,128)S(1)}, u32[]{:S(2)}, u32[]{:S(2)}) collective-permute-start(f32[32,128]{1,0:T(8,128)S(1)} %get-tuple-element.35.s.s_in), channel_id=1, source_target_pairs={{0,16},{16,0},{32,48},{48,32},{64,80},{80,64},{96,112},{112,96},{1... | collective-permute-start | bytes 49160 | tf_op jit(solution)/shard_map/ppermute | solution.py:184
  74.1 14.1 %collective-permute-start.3 = (f32[32,128]{1,0:T(8,128)S(1)}, f32[32,128]{1,0:T(8,128)S(1)}, u32[]{:S(2)}, u32[]{:S(2)}) collective-permute-start(f32[32,128]{1,0:T(8,128)S(1)} %get-tuple-element.35.s.s_in), channel_id=1, source_target_pairs={{16,32},{48,64},{80,96},{32,16},{64,48},{96,80},{17,33},{49,65},{8... | collective-permute-start | bytes 49160 | tf_op jit(solution)/shard_map/ppermute | solution.py:186
  88.2 29.0 %slice-start = ((s8[8388608]{0:T(1024)(128)(4,1)}), s8[4194304]{0:T(1024)(128)(4,1)S(1)}, s32[]{:S(2)}) async-start(s8[8388608]{0:T(1024)(128)(4,1)} %bitcast.11), calls=%async_computation.6 | async-start | bytes 8388608
  88.3 29.0 %slice-start.1 = ((s8[8388608]{0:T(1024)(128)(4,1)}), s8[4194304]{0:T(1024)(128)(4,1)S(1)}, s32[]{:S(2)}) async-start(s8[8388608]{0:T(1024)(128)(4,1)} %bitcast.11), calls=%async_computation.7 | async-start | bytes 8388608
  100.7 16.6 %copy-start.7 = (f32[32,128,128]{2,1,0:T(8,128)S(1)}, f32[32,128,128]{2,1,0:T(8,128)}, u32[]{:S(2)}) copy-start(f32[32,128,128]{2,1,0:T(8,128)} %diag.11) | copy-start | bytes 6291460
  103.3 13.9 %collective-permute-start.4 = (f32[32,128]{1,0:T(8,128)S(1)}, f32[32,128]{1,0:T(8,128)S(1)}, u32[]{:S(2)}, u32[]{:S(2)}) collective-permute-start(f32[32,128]{1,0:T(8,128)S(1)} %get-tuple-element.46.s), channel_id=1, source_target_pairs={{0,16},{16,0},{32,48},{48,32},{64,80},{80,64},{96,112},{112,96},{1... | collective-permute-start | bytes 49160 | tf_op jit(solution)/shard_map/ppermute | solution.py:184
  103.3 13.9 %collective-permute-start.5 = (f32[32,128]{1,0:T(8,128)S(1)}, f32[32,128]{1,0:T(8,128)S(1)}, u32[]{:S(2)}, u32[]{:S(2)}) collective-permute-start(f32[32,128]{1,0:T(8,128)S(1)} %get-tuple-element.46.s), channel_id=1, source_target_pairs={{16,32},{48,64},{80,96},{32,16},{64,48},{96,80},{17,33},{49,65},{8... | collective-permute-start | bytes 49160 | tf_op jit(solution)/shard_map/ppermute | solution.py:186
where the time goes:
time: 121 us; the launch traced here: 120 us
  blocking collectives  36.7 us (30%)
  starting transfers between devices  26.9 us (22%)
  local copies, waits for them, and re-layouts  23.1 us (19%)
  Pallas kernels  17.3 us (14%)
  waiting for transfers between devices  14.1 us (12%)
  between operations  1.53 us (1%)
    all_to_all x4, blocking collectives, exchange(): got = lax.all_to_all(rows.reshape(TILES, CAP, B), 'tile', 0, 0)  36.7 us
    unnamed x62, local copies, waits for them, and re-layouts  23.1 us
    pallas_call x7, Pallas kernels, call(): pl.pallas_call(kernel, out_shape=tuple((jax.ShapeDtypeStruct(shape, F32)...  17.3 us
    ppermute x3, starting transfers between devices, vertical(): chip = lax.ppermute(s, 'slab', up + [(j, i) for i, j in up])  12.7 us
    all_to_all x1, starting transfers between devices, body(): got = lax.all_to_all(send, 'tile', 0, 0)  8.6 us
    all_to_all x1, waiting for transfers between devices, body(): got = lax.all_to_all(send, 'tile', 0, 0)  7.72 us
    all_to_all x1, waiting for transfers between devices, exchange(): got = lax.all_to_all(rows.reshape(TILES, CAP, B), 'tile', 0, 0)  6.36 us
    all_to_all x1, starting transfers between devices, exchange(): got = lax.all_to_all(rows.reshape(TILES, CAP, B), 'tile', 0, 0)  3.51 us
  transfers between devices with their start and end apart: 8, of which 2 were waited for; matrix products, arithmetic and copies ran while one was open for 0% of the time, Pallas kernels for 0%

commit v1 on v0

--- a/solution.py
+++ b/solution.py
@@ -63,7 +63,7 @@
     sub = lax.broadcasted_iota(jnp.int32, (8, B), 0)
     for p in range(TILES):
         send[p, :NBD, :] = t
-        asked = jnp.where(sub == 0, fetch[0, p, 0], fetch[0, p, 1])
+        asked = jnp.where(sub == 0, fetch[0, 0, p], fetch[0, 1, p])
         send[p, NBD:, :] = asked.astype(F32)
 
 
@@ -71,8 +71,8 @@
     for g in range(NBD):
         w[g : g + 1, :] = res[g : g + 1, :] - product(
             (diag[g], t[g : g + 1, :]),
-            (off[g, 0], row(t, own[g, 0])),
-            (off[g, 1], row(t, own[g, 1])),
+            (off[g, 0], row(t, own[0, g])),
+            (off[g, 1], row(t, own[1, g])),
             (off[g, 2], near_row(g)),
         )
 
@@ -84,7 +84,7 @@
     def near_row(g):
         slot = margin[g]
         peer = slot // CAP
-        return table[peer, pl.ds(fetch[0, peer, slot % CAP], 1), :]
+        return table[peer, pl.ds(fetch[0, slot % CAP, peer], 1), :]
 
     extended_rows(own, near_row, diag, off, pre, t, rhs, w)
     for g in range(NBD):
@@ -123,8 +123,8 @@
         over = jnp.where(below == odd[0], row(core, place), row(chip, place))
         r_out[g : g + 1, :] = r_out[g : g + 1, :] - product(
             (diag[g], s[g : g + 1, :]),
-            (off[g, 0], row(s, own[g, 0])),
-            (off[g, 1], row(s, own[g, 1])),
+            (off[g, 0], row(s, own[0, g])),
+            (off[g, 1], row(s, own[1, g])),
             (off[g, 2], row(table, margin[g])),
             (off[g, 3], over),
         )
@@ -162,8 +162,11 @@
         out_shape=tuple(jax.ShapeDtypeStruct(shape, F32) for shape in outs),
         in_specs=[SMEM] * len(scalars) + [VMEM] * len(arrays),
         out_specs=(VMEM,) * len(outs),
-        scratch_shapes=[pltpu.VMEM(shape, F32) for shape in scratch],
+        scratch_shapes=list(scratch),
         compiler_params=pltpu.CompilerParams(vmem_limit_bytes=4 * 2**20),
+        cost_estimate=pl.CostEstimate(
+            flops=20_000_000_000, transcendentals=0, bytes_accessed=40_000_000
+        ),
         name=name,
     )(*scalars, *arrays)
 
@@ -174,6 +177,7 @@
 ):
     slabs = lax.axis_size("slab")
     odd = (lax.axis_index("slab") % 2).astype(jnp.int32).reshape(1)
+    own_cols, fetch_rows = own_cols.T, jnp.swapaxes(fetch_rows, 1, 2)
     soil, root, table = (NBD, B), (RCAP, B), (SLOTS, B)
 
     def exchange(rows):
@@ -194,7 +198,7 @@
         first_step_kernel, "step0",
         (own_cols, margin_slot, fetch_rows, root_count),
         (soil_diag, soil_off, soil_pre, t, got, soil_rhs, root_pre, root_rhs),
-        (soil, table, table, root), (soil,),
+        (soil, table, table, root), (pltpu.VMEM(soil, F32),),
     )
     x, r, rr, root_x = s, soil_rhs, root_rhs, ur
     rho = 1.0 / SIGMA
@@ -223,7 +227,7 @@
             functools.partial(step_kernel, keep, gain), f"step{sweep + 1}",
             (own_cols, margin_slot),
             (soil_diag, soil_off, soil_pre, t, got, r, s, x, choice),
-            (soil, soil, table), (soil,),
+            (soil, soil, table), (pltpu.VMEM(soil, F32),),
         )
     return x, root_x, r
 

time: 121 us -> 113 us (0.934)
  local copies, waits for them, and re-layouts: 23.1 us -> 16.4 us
    unnamed x62 -> x50, local copies, waits for them, and re-layouts: 23.1 us -> 16.4 us
where the time goes in v1:
time: 113 us; the launch traced here: 112 us
  blocking collectives  36.7 us (32%)
  starting transfers between devices  26.9 us (24%)
  Pallas kernels  16.5 us (15%)
  local copies, waits for them, and re-layouts  16.4 us (15%)
  waiting for transfers between devices  14.2 us (13%)
  between operations  1.49 us (1%)
    all_to_all x4, blocking collectives, exchange(): got = lax.all_to_all(rows.reshape(TILES, CAP, B), 'tile', 0, 0)  36.7 us
    pallas_call x7, Pallas kernels, call(): pl.pallas_call(kernel, out_shape=tuple((jax.ShapeDtypeStruct(shape, F32)...  16.5 us
    unnamed x50, local copies, waits for them, and re-layouts  16.4 us
    ppermute x3, starting transfers between devices, vertical(): chip = lax.ppermute(s, 'slab', up + [(j, i) for i, j in up])  12.7 us
    all_to_all x1, starting transfers between devices, body(): got = lax.all_to_all(send, 'tile', 0, 0)  8.6 us
    all_to_all x1, waiting for transfers between devices, body(): got = lax.all_to_all(send, 'tile', 0, 0)  7.83 us
    all_to_all x1, waiting for transfers between devices, exchange(): got = lax.all_to_all(rows.reshape(TILES, CAP, B), 'tile', 0, 0)  6.36 us
    all_to_all x1, starting transfers between devices, exchange(): got = lax.all_to_all(rows.reshape(TILES, CAP, B), 'tile', 0, 0)  3.51 us
  transfers between devices with their start and end apart: 8, of which 2 were waited for; matrix products, arithmetic and copies ran while one was open for 0% of the time, Pallas kernels for 0%

profile of v1, /device:TPU:1, one launch (start us, length us, event | category | flops | bytes accessed | tf_op | source)
XLA Modules:
  0.0 112.2 jit_solution(7445608315745559996)
XLA Ops:
  0.6 0.0 copy-start.3
  0.6 1.6 %copy-done.3 = f32[32,128,128]{2,1,0:T(8,128)S(1)} copy-done((f32[32,128,128]{2,1,0:T(8,128)S(1)}, f32[32,128,128]{2,1,0:T(8,128)}, u32[]{:S(2)}) %copy-start.3) | copy-done | bytes 2097176
  2.2 0.0 copy-start.14
  2.2 0.7 copy-done.14
  2.9 0.0 copy-start.17
  2.9 0.7 copy-done.17
  3.6 0.0 copy-start.4
  3.6 0.0 copy-start.15
  3.6 0.0 copy-start.16
  3.6 0.0 copy-start.18
  3.6 0.0 copy-start.19
  3.7 0.0 copy-start.20
  3.7 1.9 %first.1 = (f32[32,128]{1,0:T(8,128)S(1)}, f32[16,40,128]{2,1,0:T(8,128)}) custom-call(s32[1,2,16]{2,1,0:T(2,128)S(1)} %bitcast.22, f32[32,128,128]{2,1,0:T(8,128)S(1)} %copy-done.3, f32[32,128]{1,0:T(8,128)S(1)} %copy-done.14), custom_call_target="tpu_custom_call" | custom-call | flops 20000000000 | bytes 40000000 | tf_op jit(solution)/shard_map/first/pallas_call | solution.py:160
  5.6 0.0 copy-start.23
  5.6 0.6 copy-done.23
  6.2 8.6 %all-to-all-start = ((f32[16,40,128]{2,1,0:T(8,128)}), f32[16,40,128]{2,1,0:T(8,128)S(1)}, u32[]{:S(2)}, u32[]{:S(2)}) async-start(f32[16,40,128]{2,1,0:T(8,128)} %get-tuple-element.27), calls=%async_computation | async-start | bytes 655360 | tf_op jit(solution)/shard_map/all_to_all | solution.py:196
  15.4 7.8 %all-to-all-done.table = f32[16,40,128]{2,1,0:T(8,128)S(1)} async-done(((f32[16,40,128]{2,1,0:T(8,128)}), f32[16,40,128]{2,1,0:T(8,128)S(1)}, u32[]{:S(2)}, u32[]{:S(2)}) %all-to-all-start) | async-done | bytes 327712 | tf_op jit(solution)/shard_map/all_to_all | solution.py:196
  23.3 0.0 copy-done.4
  23.3 0.0 copy-done.9
  23.3 0.0 copy-done.15
  23.3 0.0 copy-done.16
  23.3 0.0 copy-done.18
  23.3 0.0 copy-done.19
  23.3 0.0 copy-done.20
  23.3 0.0 copy-start
  23.3 3.4 %copy-done = f32[32,4,128,128]{3,2,1,0:T(8,128)S(1)} copy-done((f32[32,4,128,128]{3,2,1,0:T(8,128)S(1)}, f32[32,4,128,128]{3,2,1,0:T(8,128)}, u32[]{:S(2)}) %copy-start) | copy-done | bytes 8388632
  26.7 1.6 %copy-done.5 = f32[32,128,128]{2,1,0:T(8,128)S(1)} copy-done((f32[32,128,128]{2,1,0:T(8,128)S(1)}, f32[32,128,128]{2,1,0:T(8,128)}, u32[]{:S(2)}) %copy-start.5) | copy-done | bytes 2097176
  28.3 0.7 copy-done.24
  29.0 2.6 %step0.1 = (f32[32,128]{1,0:T(8,128)S(1)}, f32[32,128]{1,0:T(8,128)}, f32[32,128]{1,0:T(8,128)S(1)}, f32[8,128]{1,0:T(8,128)S(1)}) custom-call(s32[2,32]{1,0:T(2,128)S(1)} %bitcast.24, s32[32]{0:T(128)S(1)} %copy-done.20, s32[1,2,16]{2,1,0:T(2,128)S(1)} %bitcast.23, s32[1]{0:T(128)S(6)} %copy.18.count, f32[32,128,128]{2,1,0:T(8,128)S(1)} %copy-done.5, ...), custom_call_target="tpu_custom_call" | custom-call | flops 20000000000 | bytes 40000000 | tf_op jit(solution)/shard_map/step0/pallas_call | solution.py:160
  31.6 1.9 %collective-permute-start = (f32[32,128]{1,0:T(8,128)S(1)}, f32[32,128]{1,0:T(8,128)S(1)}, u32[]{:S(2)}, u32[]{:S(2)}) collective-permute-start(f32[32,128]{1,0:T(8,128)S(1)} %get-tuple-element.28.s.s_in.x_in), channel_id=1, source_target_pairs={{0,16},{16,0},{32,48},{48,32},{64,80},{80,64},{96,112},{112,96},{1... | collective-permute-start | bytes 49160 | tf_op jit(solution)/shard_map/ppermute | solution.py:188
  33.5 3.0 %collective-permute-start.1 = (f32[32,128]{1,0:T(8,128)S(1)}, f32[32,128]{1,0:T(8,128)S(1)}, u32[]{:S(2)}, u32[]{:S(2)}) collective-permute-start(f32[32,128]{1,0:T(8,128)S(1)} %get-tuple-element.28.s.s_in.x_in), channel_id=1, source_target_pairs={{16,32},{48,64},{80,96},{32,16},{64,48},{96,80},{17,33},{49,65},{8... | collective-permute-start | bytes 49160 | tf_op jit(solution)/shard_map/ppermute | solution.py:190
  36.5 3.5 %all-to-all-start.1 = ((f32[16,2,128]{2,1,0:T(2,128)}), f32[16,2,128]{2,1,0:T(2,128)S(1)}, u32[]{:S(2)}, u32[]{:S(2)}) async-start(f32[16,2,128]{2,1,0:T(2,128)} %bitcast.3), calls=%async_computation.1 | async-start | bytes 32768 | tf_op jit(solution)/shard_map/all_to_all | solution.py:184
  40.0 6.4 %all-to-all-done.1 = f32[16,2,128]{2,1,0:T(2,128)S(1)} async-done(((f32[16,2,128]{2,1,0:T(2,128)}), f32[16,2,128]{2,1,0:T(2,128)S(1)}, u32[]{:S(2)}, u32[]{:S(2)}) %all-to-all-start.1) | async-done | bytes 16416 | tf_op jit(solution)/shard_map/all_to_all | solution.py:184
  46.4 0.0 collective-permute-done.core
  46.4 0.0 collective-permute-done.1.chip
  46.4 0.0 copy-done.8
  46.4 0.0 copy-done.21
  46.4 0.0 copy-done.22
  46.4 0.0 copy-start.1
  46.4 3.4 %copy-done.1 = f32[32,4,128,128]{3,2,1,0:T(8,128)S(1)} copy-done((f32[32,4,128,128]{3,2,1,0:T(8,128)S(1)}, f32[32,4,128,128]{3,2,1,0:T(8,128)}, u32[]{:S(2)}) %copy-start.1) | copy-done | bytes 8388632
  49.8 1.6 %copy-done.6 = f32[32,128,128]{2,1,0:T(8,128)S(1)} copy-done((f32[32,128,128]{2,1,0:T(8,128)S(1)}, f32[32,128,128]{2,1,0:T(8,128)}, u32[]{:S(2)}) %copy-start.6) | copy-done | bytes 2097176
  51.4 1.0 copy-done.10
  52.4 1.0 copy-done.12
  53.5 2.4 %residual0.1 = (f32[32,128]{1,0:T(8,128)S(1)}, f32[32,128]{1,0:T(8,128)S(1)}, f32[8,128]{1,0:T(8,128)S(1)}, f32[8,128]{1,0:T(8,128)S(1)}, f32[8,128]{1,0:T(8,128)S(1)}, /*index=5*/f32[32,128]{1,0:T(8,128)S(1)}) custom-call(s32[2,32]{1,0:T(2,128)S(1)} %bitcast.25, s32[32]{0:T(128)S(1)} %copy-done.20, s32[32]{0:T(128)S(1)} %copy-done.21, s32[1]{0:T(128)} %bitcast.1.odd, ...), custom_call_target="tpu_custom_call" | custom-call | flops 20000000000 | bytes 40000000 | tf_op jit(solution)/shard_map/residual0/pallas_call | solution.py:160
  55.9 9.2 %all_to_all.30 = f32[16,2,128]{2,1,0:T(2,128)S(1)} all-to-all(f32[16,2,128]{2,1,0:T(2,128)S(1)} %bitcast.19), channel_id=1, replica_groups=mesh['slab'=8,'tile'=16] {'tile'}, dimensions={0} | all-to-all | bytes 32768 | tf_op jit(solution)/shard_map/all_to_all | solution.py:184
  65.1 0.0 copy-done.2
  65.1 2.0 %step1.1 = (f32[32,128]{1,0:T(8,128)S(1)}, f32[32,128]{1,0:T(8,128)S(1)}, f32[32,128]{1,0:T(8,128)S(1)}) custom-call(s32[2,32]{1,0:T(2,128)S(1)} %bitcast.26, s32[32]{0:T(128)S(1)} %copy-done.20, f32[32,128,128]{2,1,0:T(8,128)S(1)} %copy-done.6, f32[32,4,128,128]{3,2,1,0:T(8,128)S(1)} %copy-done.2, f32[32,128,128]{2,1,0:T(8,128)S(1)} %copy-done.4, ...), custom_call_target="tpu_custom_call" | custom-call | flops 20000000000 | bytes 40000000 | tf_op jit(solution)/shard_map/step1/pallas_call | solution.py:160
  67.1 0.3 collective-permute-start.2
  67.3 5.0 %collective-permute-start.3 = (f32[32,128]{1,0:T(8,128)S(1)}, f32[32,128]{1,0:T(8,128)S(1)}, u32[]{:S(2)}, u32[]{:S(2)}) collective-permute-start(f32[32,128]{1,0:T(8,128)S(1)} %get-tuple-element.35.s.s_in), channel_id=1, source_target_pairs={{16,32},{48,64},{80,96},{32,16},{64,48},{96,80},{17,33},{49,65},{8... | collective-permute-start | bytes 49160 | tf_op jit(solution)/shard_map/ppermute | solution.py:190
  72.3 9.2 %all_to_all.31 = f32[16,2,128]{2,1,0:T(2,128)S(1)} all-to-all(f32[16,2,128]{2,1,0:T(2,128)S(1)} %bitcast.16), channel_id=1, replica_groups=mesh['slab'=8,'tile'=16] {'tile'}, dimensions={0} | all-to-all | bytes 32768 | tf_op jit(solution)/shard_map/all_to_all | solution.py:184
  81.5 0.0 collective-permute-done.2.core
  81.5 0.0 collective-permute-done.3.chip
  81.5 0.0 copy-done.11
  81.5 0.0 copy-done.13
  81.5 3.0 %residual1.1 = (f32[32,128]{1,0:T(8,128)S(1)}, f32[32,128]{1,0:T(8,128)S(1)}, f32[8,128]{1,0:T(8,128)S(1)}, f32[8,128]{1,0:T(8,128)}, f32[8,128]{1,0:T(8,128)}, /*index=5*/f32[32,128]{1,0:T(8,128)S(1)}) custom-call(s32[2,32]{1,0:T(2,128)S(1)} %bitcast.27, s32[32]{0:T(128)S(1)} %copy-done.20, s32[32]{0:T(128)S(1)} %copy-done.21, s32[1]{0:T(128)} %bitcast.1.odd, ...), custom_call_target="tpu_custom_call" | custom-call | flops 20000000000 | bytes 40000000 | tf_op jit(solution)/shard_map/residual1/pallas_call | solution.py:160
  84.5 9.2 %all_to_all.32 = f32[16,2,128]{2,1,0:T(2,128)S(1)} all-to-all(f32[16,2,128]{2,1,0:T(2,128)S(1)} %bitcast.17), channel_id=1, replica_groups=mesh['slab'=8,'tile'=16] {'tile'}, dimensions={0} | all-to-all | bytes 32768 | tf_op jit(solution)/shard_map/all_to_all | solution.py:184
  93.7 2.4 %step2.1 = (f32[32,128]{1,0:T(8,128)S(1)}, f32[32,128]{1,0:T(8,128)}, f32[32,128]{1,0:T(8,128)S(1)}) custom-call(s32[2,32]{1,0:T(2,128)S(1)} %bitcast.28, s32[32]{0:T(128)S(1)} %copy-done.20, f32[32,128,128]{2,1,0:T(8,128)S(1)} %copy-done.6, f32[32,4,128,128]{3,2,1,0:T(8,128)S(1)} %copy-done.2, f32[32,128,128]{2,1,0:T(8,128)S(1)} %copy-done.4, ...), custom_call_target="tpu_custom_call" | custom-call | flops 20000000000 | bytes 40000000 | tf_op jit(solution)/shard_map/step2/pallas_call | solution.py:160
  96.1 0.0 collective-permute-start.4
  96.1 4.8 %collective-permute-start.5 = (f32[32,128]{1,0:T(8,128)S(1)}, f32[32,128]{1,0:T(8,128)S(1)}, u32[]{:S(2)}, u32[]{:S(2)}) collective-permute-start(f32[32,128]{1,0:T(8,128)S(1)} %get-tuple-element.46.s), channel_id=1, source_target_pairs={{16,32},{48,64},{80,96},{32,16},{64,48},{96,80},{17,33},{49,65},{8... | collective-permute-start | bytes 49160 | tf_op jit(solution)/shard_map/ppermute | solution.py:190
  100.9 9.2 %all_to_all.33 = f32[16,2,128]{2,1,0:T(2,128)S(1)} all-to-all(f32[16,2,128]{2,1,0:T(2,128)S(1)} %bitcast.15), channel_id=1, replica_groups=mesh['slab'=8,'tile'=16] {'tile'}, dimensions={0} | all-to-all | bytes 32768 | tf_op jit(solution)/shard_map/all_to_all | solution.py:184
  110.1 0.0 collective-permute-done.4.core
  110.1 0.0 collective-permute-done.5.chip
  110.1 0.0 copy-done.7
  110.1 2.1 %last.1 = f32[32,128]{1,0:T(8,128)} custom-call(s32[2,32]{1,0:T(2,128)S(1)} %bitcast.29, s32[32]{0:T(128)S(1)} %copy-done.20, s32[32]{0:T(128)S(1)} %copy-done.21, s32[1]{0:T(128)} %bitcast.1.odd, s32[8]{0:T(128)S(1)} %copy-done.22, f32[32,128,128]{2,1,0:T(8,128)S(1)} %copy-done.7, f32[32,4,128,128]{3,2,1,0:T(8,128)S(1)} %copy-done.2, ...), custom_call_target="tpu_custom_call" | custom-call | flops 20000000000 | bytes 40000000 | tf_op jit(solution)/shard_map/last/pallas_call | solution.py:160
  (13 shorter events, 0.0 us)
Async XLA Ops:
  0.6 1.6 %copy-start.3 = (f32[32,128,128]{2,1,0:T(8,128)S(1)}, f32[32,128,128]{2,1,0:T(8,128)}, u32[]{:S(2)}) copy-start(f32[32,128,128]{2,1,0:T(8,128)} %pre.11) | copy-start | bytes 6291460
  2.2 0.7 copy-start.14
  2.9 0.7 copy-start.17
  3.6 19.6 %copy-start.4 = (f32[32,128,128]{2,1,0:T(8,128)S(1)}, f32[32,128,128]{2,1,0:T(8,128)}, u32[]{:S(2)}) copy-start(f32[32,128,128]{2,1,0:T(8,128)} %pre.11) | copy-start | bytes 6291460
  3.6 19.6 %copy-start.9 = (f32[8,128,128]{2,1,0:T(8,128)S(1)}, f32[8,128,128]{2,1,0:T(8,128)}, u32[]{:S(2)}) copy-start(f32[8,128,128]{2,1,0:T(8,128)} %root_pre.5) | copy-start | bytes 1572868
  3.6 19.6 %copy-start.15 = (f32[32,128]{1,0:T(8,128)S(1)}, f32[32,128]{1,0:T(8,128)}, u32[]{:S(2)}) copy-start(f32[32,128]{1,0:T(8,128)} %res.1) | copy-start | bytes 49156
  3.6 19.6 %copy-start.16 = (f32[8,128]{1,0:T(8,128)S(1)}, f32[8,128]{1,0:T(8,128)}, u32[]{:S(2)}) copy-start(f32[8,128]{1,0:T(8,128)} %rr.1) | copy-start | bytes 12292
  3.6 19.6 %copy-start.18 = (s32[1,16,2]{1,2,0:T(2,128)S(1)}, s32[1,16,2]{1,2,0:T(2,128)}, u32[]{:S(2)}) copy-start(s32[1,16,2]{1,2,0:T(2,128)} %param.21) | copy-start | bytes 388
  3.6 19.6 %copy-start.19 = (s32[32,2]{0,1:T(2,128)S(1)}, s32[32,2]{0,1:T(2,128)}, u32[]{:S(2)}) copy-start(s32[32,2]{0,1:T(2,128)} %param.18) | copy-start | bytes 772
  3.7 19.6 %copy-start.20 = (s32[32]{0:T(128)S(1)}, s32[32]{0:T(128)}, u32[]{:S(2)}) copy-start(s32[32]{0:T(128)} %margin.11) | copy-start | bytes 388
  5.6 0.6 copy-start.23
  6.2 17.1 %all-to-all-start = ((f32[16,40,128]{2,1,0:T(8,128)}), f32[16,40,128]{2,1,0:T(8,128)S(1)}, u32[]{:S(2)}, u32[]{:S(2)}) async-start(f32[16,40,128]{2,1,0:T(8,128)} %get-tuple-element.27), calls=%async_computation | async-start | bytes 655360 | tf_op jit(solution)/shard_map/all_to_all | solution.py:196
  23.3 3.4 %copy-start = (f32[32,4,128,128]{3,2,1,0:T(8,128)S(1)}, f32[32,4,128,128]{3,2,1,0:T(8,128)}, u32[]{:S(2)}) copy-start(f32[32,4,128,128]{3,2,1,0:T(8,128)} %off.11) | copy-start | bytes 25165828
  26.7 1.6 %copy-start.5 = (f32[32,128,128]{2,1,0:T(8,128)S(1)}, f32[32,128,128]{2,1,0:T(8,128)}, u32[]{:S(2)}) copy-start(f32[32,128,128]{2,1,0:T(8,128)} %diag.11) | copy-start | bytes 6291460
  28.3 0.7 copy-start.24
  29.0 17.4 %copy-start.8 = (f32[8,128,128]{2,1,0:T(8,128)S(1)}, f32[8,128,128]{2,1,0:T(8,128)}, u32[]{:S(2)}) copy-start(f32[8,128,128]{2,1,0:T(8,128)} %root_diag.3) | copy-start | bytes 1572868
  29.0 17.4 %copy-start.21 = (s32[32]{0:T(128)S(1)}, s32[32]{0:T(128)}, u32[]{:S(2)}) copy-start(s32[32]{0:T(128)} %vert.5) | copy-start | bytes 388
  29.0 17.4 %copy-start.22 = (s32[8]{0:T(128)S(1)}, s32[8]{0:T(128)}, u32[]{:S(2)}) copy-start(s32[8]{0:T(128)} %cell.5) | copy-start | bytes 100
  31.6 14.8 %collective-permute-start = (f32[32,128]{1,0:T(8,128)S(1)}, f32[32,128]{1,0:T(8,128)S(1)}, u32[]{:S(2)}, u32[]{:S(2)}) collective-permute-start(f32[32,128]{1,0:T(8,128)S(1)} %get-tuple-element.28.s.s_in.x_in), channel_id=1, source_target_pairs={{0,16},{16,0},{32,48},{48,32},{64,80},{80,64},{96,112},{112,96},{1... | collective-permute-start | bytes 49160 | tf_op jit(solution)/shard_map/ppermute | solution.py:188
  33.5 12.9 %collective-permute-start.1 = (f32[32,128]{1,0:T(8,128)S(1)}, f32[32,128]{1,0:T(8,128)S(1)}, u32[]{:S(2)}, u32[]{:S(2)}) collective-permute-start(f32[32,128]{1,0:T(8,128)S(1)} %get-tuple-element.28.s.s_in.x_in), channel_id=1, source_target_pairs={{16,32},{48,64},{80,96},{32,16},{64,48},{96,80},{17,33},{49,65},{8... | collective-permute-start | bytes 49160 | tf_op jit(solution)/shard_map/ppermute | solution.py:190
  36.5 9.9 %all-to-all-start.1 = ((f32[16,2,128]{2,1,0:T(2,128)}), f32[16,2,128]{2,1,0:T(2,128)S(1)}, u32[]{:S(2)}, u32[]{:S(2)}) async-start(f32[16,2,128]{2,1,0:T(2,128)} %bitcast.3), calls=%async_computation.1 | async-start | bytes 32768 | tf_op jit(solution)/shard_map/all_to_all | solution.py:184
  46.4 3.4 %copy-start.1 = (f32[32,4,128,128]{3,2,1,0:T(8,128)S(1)}, f32[32,4,128,128]{3,2,1,0:T(8,128)}, u32[]{:S(2)}) copy-start(f32[32,4,128,128]{3,2,1,0:T(8,128)} %off.11) | copy-start | bytes 25165828
  49.8 1.6 %copy-start.6 = (f32[32,128,128]{2,1,0:T(8,128)S(1)}, f32[32,128,128]{2,1,0:T(8,128)}, u32[]{:S(2)}) copy-start(f32[32,128,128]{2,1,0:T(8,128)} %diag.11) | copy-start | bytes 6291460
  51.4 1.0 copy-start.10
  52.4 1.0 copy-start.12
  53.5 11.6 %copy-start.2 = (f32[32,4,128,128]{3,2,1,0:T(8,128)S(1)}, f32[32,4,128,128]{3,2,1,0:T(8,128)}, u32[]{:S(2)}) copy-start(f32[32,4,128,128]{3,2,1,0:T(8,128)} %off.11) | copy-start | bytes 25165828
  65.1 16.4 %copy-start.11 = (f32[8,128,128]{2,1,0:T(8,128)S(1)}, f32[8,128,128]{2,1,0:T(8,128)}, u32[]{:S(2)}) copy-start(f32[8,128,128]{2,1,0:T(8,128)} %root_up.3) | copy-start | bytes 1572868
  65.1 16.4 %copy-start.13 = (f32[8,128,128]{2,1,0:T(8,128)S(1)}, f32[8,128,128]{2,1,0:T(8,128)}, u32[]{:S(2)}) copy-start(f32[8,128,128]{2,1,0:T(8,128)} %down.5) | copy-start | bytes 1572868
  67.1 14.4 %collective-permute-start.2 = (f32[32,128]{1,0:T(8,128)S(1)}, f32[32,128]{1,0:T(8,128)S(1)}, u32[]{:S(2)}, u32[]{:S(2)}) collective-permute-start(f32[32,128]{1,0:T(8,128)S(1)} %get-tuple-element.35.s.s_in), channel_id=1, source_target_pairs={{0,16},{16,0},{32,48},{48,32},{64,80},{80,64},{96,112},{112,96},{1... | collective-permute-start | bytes 49160 | tf_op jit(solution)/shard_map/ppermute | solution.py:188
  67.3 14.1 %collective-permute-start.3 = (f32[32,128]{1,0:T(8,128)S(1)}, f32[32,128]{1,0:T(8,128)S(1)}, u32[]{:S(2)}, u32[]{:S(2)}) collective-permute-start(f32[32,128]{1,0:T(8,128)S(1)} %get-tuple-element.35.s.s_in), channel_id=1, source_target_pairs={{16,32},{48,64},{80,96},{32,16},{64,48},{96,80},{17,33},{49,65},{8... | collective-permute-start | bytes 49160 | tf_op jit(solution)/shard_map/ppermute | solution.py:190
  93.7 16.4 %copy-start.7 = (f32[32,128,128]{2,1,0:T(8,128)S(1)}, f32[32,128,128]{2,1,0:T(8,128)}, u32[]{:S(2)}) copy-start(f32[32,128,128]{2,1,0:T(8,128)} %diag.11) | copy-start | bytes 6291460
  96.1 14.0 %collective-permute-start.4 = (f32[32,128]{1,0:T(8,128)S(1)}, f32[32,128]{1,0:T(8,128)S(1)}, u32[]{:S(2)}, u32[]{:S(2)}) collective-permute-start(f32[32,128]{1,0:T(8,128)S(1)} %get-tuple-element.46.s), channel_id=1, source_target_pairs={{0,16},{16,0},{32,48},{48,32},{64,80},{80,64},{96,112},{112,96},{1... | collective-permute-start | bytes 49160 | tf_op jit(solution)/shard_map/ppermute | solution.py:188
  96.1 14.0 %collective-permute-start.5 = (f32[32,128]{1,0:T(8,128)S(1)}, f32[32,128]{1,0:T(8,128)S(1)}, u32[]{:S(2)}, u32[]{:S(2)}) collective-permute-start(f32[32,128]{1,0:T(8,128)S(1)} %get-tuple-element.46.s), channel_id=1, source_target_pairs={{16,32},{48,64},{80,96},{32,16},{64,48},{96,80},{17,33},{49,65},{8... | collective-permute-start | bytes 49160 | tf_op jit(solution)/shard_map/ppermute | solution.py:190

commit v2 on v1

--- a/solution.py
+++ b/solution.py
@@ -56,7 +56,7 @@
     )
 
 
-def first_kernel(fetch, pre, rhs, t_out, send):
+def first_kernel(fetch, count, pre, rhs, t_out, send):
     for g in range(NBD):
         t_out[g : g + 1, :] = product((pre[g], rhs[g : g + 1, :]))
     t = t_out[...]
@@ -112,15 +112,14 @@
     send[...] = pick(choice[...], s_out[...])
 
 
-def residual_rows(own, margin, vert, odd, cell, diag, off, down, s, table, core, chip, res, ur, r_out):
+def residual_rows(own, margin, vert, cell, diag, off, down, s, table, below, above, res, ur, r_out):
     r_out[...] = res[...]
     for r in range(RCAP):
         at = pl.ds(cell[r], 1)
         r_out[at, :] = r_out[at, :] - product((down[r], ur[r : r + 1, :]))
     for g in range(NBD):
         place = vert[g] % NBD
-        below = (vert[g] < NBD).astype(jnp.int32)
-        over = jnp.where(below == odd[0], row(core, place), row(chip, place))
+        over = jnp.where(vert[g] < NBD, row(below, place), row(above, place))
         r_out[g : g + 1, :] = r_out[g : g + 1, :] - product(
             (diag[g], s[g : g + 1, :]),
             (off[g, 0], row(s, own[0, g])),
@@ -131,12 +130,12 @@
 
 
 def residual_kernel(
-    keep, gain, own, margin, vert, odd, cell, count,
+    keep, gain, own, margin, vert, cell, count,
     diag, off, pre, root_diag, root_pre, root_up, down,
-    s, table, core, chip, res, ur, rr, root_x, choice,
+    s, table, below, above, res, ur, rr, root_x, choice,
     t_out, r_out, ur_out, rr_out, root_x_out, send,
 ):
-    residual_rows(own, margin, vert, odd, cell, diag, off, down, s, table, core, chip, res, ur, r_out)
+    residual_rows(own, margin, vert, cell, diag, off, down, s, table, below, above, res, ur, r_out)
     for g in range(NBD):
         t_out[g : g + 1, :] = product((pre[g], r_out[g : g + 1, :]))
     send[...] = pick(choice[...], t_out[...])
@@ -151,9 +150,9 @@
 
 
 def last_kernel(
-    own, margin, vert, odd, cell, diag, off, down, s, table, core, chip, res, ur, r_out
-):
-    residual_rows(own, margin, vert, odd, cell, diag, off, down, s, table, core, chip, res, ur, r_out)
+    own, margin, vert, cell, diag, off, down, s, table, below, above, res, ur, r_out
+):
+    residual_rows(own, margin, vert, cell, diag, off, down, s, table, below, above, res, ur, r_out)
 
 
 def call(kernel, name, scalars, arrays, outs, scratch=()):
@@ -176,7 +175,6 @@
     root_diag, root_pre, root_up, root_down, root_cell, root_count, root_rhs,
 ):
     slabs = lax.axis_size("slab")
-    odd = (lax.axis_index("slab") % 2).astype(jnp.int32).reshape(1)
     own_cols, fetch_rows = own_cols.T, jnp.swapaxes(fetch_rows, 1, 2)
     soil, root, table = (NBD, B), (RCAP, B), (SLOTS, B)
 
@@ -185,13 +183,11 @@
         return got.reshape(SLOTS, B)
 
     def vertical(s):
-        core = lax.ppermute(s, "slab", [(i, i ^ 1) for i in range(slabs)])
-        up = [(i, i + 1) for i in range(1, slabs - 1, 2)]
-        chip = lax.ppermute(s, "slab", up + [(j, i) for i, j in up])
-        return core, chip
+        up = [(i, (i + 1) % slabs) for i in range(slabs)]
+        return lax.ppermute(s, "slab", up), lax.ppermute(s, "slab", [(j, i) for i, j in up])
 
     t, send = call(
-        first_kernel, "first", (fetch_rows,), (soil_pre, soil_rhs), (soil, (TILES, PIECE, B))
+        first_kernel, "first", (fetch_rows, root_count), (soil_pre, soil_rhs), (soil, (TILES, PIECE, B))
     )
     got = lax.all_to_all(send, "tile", 0, 0)
     s, send, choice, ur = call(
@@ -203,13 +199,13 @@
     x, r, rr, root_x = s, soil_rhs, root_rhs, ur
     rho = 1.0 / SIGMA
     for sweep in range(SWEEPS):
-        core, chip = vertical(s)
+        below, above = vertical(s)
         got = exchange(send)
-        scalars = (own_cols, margin_slot, vertical_col, odd, root_cell)
+        scalars = (own_cols, margin_slot, vertical_col, root_cell)
         if sweep + 1 == SWEEPS:
             (r,) = call(
                 last_kernel, "last", scalars,
-                (soil_diag, soil_off, root_down, s, got, core, chip, r, ur), (soil,),
+                (soil_diag, soil_off, root_down, s, got, below, above, r, ur), (soil,),
             )
             break
         rho_new = 1.0 / (2.0 * SIGMA - rho)
@@ -219,7 +215,7 @@
             functools.partial(residual_kernel, keep, gain), f"residual{sweep}",
             scalars + (root_count,),
             (soil_diag, soil_off, soil_pre, root_diag, root_pre, root_up, root_down,
-             s, got, core, chip, r, ur, rr, root_x, choice),
+             s, got, below, above, r, ur, rr, root_x, choice),
             (soil, soil, root, root, root, table),
         )
         got = exchange(send)

time: 113 us -> 92.9 us (0.82)
  blocking collectives: 36.7 us -> 63.1 us
  starting transfers between devices: 26.9 us -> 9.39 us
  waiting for transfers between devices: 14.2 us -> 0.02 us
  local copies, waits for them, and re-layouts: 16.4 us -> 3.05 us
  Pallas kernels: 16.5 us -> 15.3 us
    all_to_all x0 -> x1, blocking collectives: none -> 17.1 us  [body(): got = lax.all_to_all(send, 'tile', 0, 0)]
    all_to_all x2 -> x0, waiting for transfers between devices: 14.2 us -> none  [the longest x1 7.83 us: body(): got = lax.all_to_all(send, 'tile', 0, 0)]
    unnamed x50 -> x32, local copies, waits for them, and re-layouts: 16.4 us -> 3.05 us
    all_to_all x2 -> x0, starting transfers between devices: 12.1 us -> none  [the longest x1 8.6 us: body(): got = lax.all_to_all(send, 'tile', 0, 0)]
    all_to_all x4 -> x5, blocking collectives: 36.7 us -> 46 us  [exchange(): got = lax.all_to_all(rows.reshape(TILES, CAP, B), 'tile', 0, 0)]
    ppermute x6, starting transfers between devices: 14.8 us -> 9.39 us  [the longest x3 6.74 us: vertical(): lax.ppermute(s, 'slab', [(j, i) for i, j in up])]
    pallas_call x7, Pallas kernels: 16.5 us -> 15.3 us  [call(): pl.pallas_call(kernel, out_shape=tuple((jax.ShapeDtypeStruct(shape, F32)...]
  transfers between devices with their start and end apart: 8 -> 6, of which waited for: 2 -> 0; matrix products, arithmetic and copies ran while one was open for 0% -> 0% of each run, Pallas kernels for 0% -> 0%
where the time goes in v2:
time: 92.9 us; the launch traced here: 92.4 us
  blocking collectives  63.1 us (68%)
  Pallas kernels  15.3 us (16%)
  starting transfers between devices  9.39 us (10%)
  local copies, waits for them, and re-layouts  3.05 us (3%)
  between operations  1.47 us (2%)
    all_to_all x5, blocking collectives, exchange(): got = lax.all_to_all(rows.reshape(TILES, CAP, B), 'tile', 0, 0)  46 us
    all_to_all x1, blocking collectives, body(): got = lax.all_to_all(send, 'tile', 0, 0)  17.1 us
    pallas_call x7, Pallas kernels, call(): pl.pallas_call(kernel, out_shape=tuple((jax.ShapeDtypeStruct(shape, F32)...  15.3 us
    ppermute x3, starting transfers between devices, vertical(): lax.ppermute(s, 'slab', [(j, i) for i, j in up])  6.74 us
    unnamed x32, local copies, waits for them, and re-layouts  3.05 us
    ppermute x3, starting transfers between devices, vertical(): lax.ppermute(s, 'slab', up)  2.66 us
  transfers between devices with their start and end apart: 6, of which 0 were waited for; matrix products, arithmetic and copies ran while one was open for 0% of the time, Pallas kernels for 0%

profile of v2, /device:TPU:1, one launch (start us, length us, event | category | flops | bytes accessed | tf_op | source)
XLA Modules:
  0.0 92.4 jit_solution(14145299289113819021)
XLA Ops:
  1.3 0.0 copy-start.1
  1.3 1.6 %copy-done.1 = f32[32,128,128]{2,1,0:T(8,128)S(1)} copy-done((f32[32,128,128]{2,1,0:T(8,128)S(1)}, f32[32,128,128]{2,1,0:T(8,128)}, u32[]{:S(2)}) %copy-start.1) | copy-done | bytes 2097176
  2.9 0.0 copy-start.8
  2.9 0.7 copy-done.8
  3.6 0.0 copy-start.11
  3.6 0.7 copy-done.11
  4.3 0.0 copy-start
  4.3 0.0 copy-start.3
  4.3 0.0 copy-start.5
  4.3 0.0 copy-start.10
  4.3 0.0 copy-start.12
  4.3 0.0 copy-start.13
  4.3 1.2 %first.1 = (f32[32,128]{1,0:T(8,128)S(1)}, f32[16,40,128]{2,1,0:T(8,128)S(1)}) custom-call(s32[1,2,16]{2,1,0:T(2,128)S(1)} %bitcast.22, s32[1]{0:T(128)S(6)} %copy.18.count, f32[32,128,128]{2,1,0:T(8,128)S(1)} %copy-done.1, f32[32,128]{1,0:T(8,128)S(1)} %copy-done.8), custom_call_target="tpu_custom_call" | custom-call | flops 20000000000 | bytes 40000000 | tf_op jit(solution)/shard_map/first/pallas_call | solution.py:159
  5.5 17.1 %all_to_all.30.table = f32[16,40,128]{2,1,0:T(8,128)S(1)} all-to-all(f32[16,40,128]{2,1,0:T(8,128)S(1)} %get-tuple-element.27), channel_id=1, replica_groups=mesh['slab'=8,'tile'=16] {'tile'}, dimensions={0} | all-to-all | bytes 655360 | tf_op jit(solution)/shard_map/all_to_all | solution.py:192
  22.6 0.0 copy-done
  22.6 0.0 copy-done.3
  22.6 0.0 copy-done.5
  22.6 0.0 copy-done.10
  22.6 0.0 copy-done.12
  22.7 0.0 copy-done.13
  22.7 0.0 copy-start.2
  22.7 0.0 copy-start.4
  22.7 0.0 copy-start.6
  22.7 0.0 copy-start.7
  22.7 0.0 copy-start.9
  22.7 0.0 copy-start.14
  22.7 0.0 copy-start.15
  22.7 2.0 %step0.1 = (f32[32,128]{1,0:T(8,128)S(1)}, f32[32,128]{1,0:T(8,128)S(1)}, f32[32,128]{1,0:T(8,128)S(1)}, f32[8,128]{1,0:T(8,128)S(1)}) custom-call(s32[2,32]{1,0:T(2,128)S(1)} %bitcast.24, s32[32]{0:T(128)S(1)} %copy-done.13, s32[1,2,16]{2,1,0:T(2,128)S(1)} %bitcast.23, s32[1]{0:T(128)S(6)} %copy.18.count, f32[32,128,128]{2,1,0:T(8,128)S(1)} %copy-done.3, ...), custom_call_target="tpu_custom_call" | custom-call | flops 20000000000 | bytes 40000000 | tf_op jit(solution)/shard_map/step0/pallas_call | solution.py:159
  24.8 1.9 %collective-permute-start.1 = (f32[32,128]{1,0:T(8,128)S(1)}, f32[32,128]{1,0:T(8,128)S(1)}, u32[]{:S(2)}, u32[]{:S(2)}) collective-permute-start(f32[32,128]{1,0:T(8,128)S(1)} %get-tuple-element.28.s.s_in.x_in), channel_id=1, source_target_pairs={{16,0},{32,16},{48,32},{64,48},{80,64},{96,80},{112,96},{0,112},{1... | collective-permute-start | bytes 49160 | tf_op jit(solution)/shard_map/ppermute | solution.py:187
  26.6 1.1 %collective-permute-start = (f32[32,128]{1,0:T(8,128)S(1)}, f32[32,128]{1,0:T(8,128)S(1)}, u32[]{:S(2)}, u32[]{:S(2)}) collective-permute-start(f32[32,128]{1,0:T(8,128)S(1)} %get-tuple-element.28.s.s_in.x_in), channel_id=1, source_target_pairs={{0,16},{16,32},{32,48},{48,64},{64,80},{80,96},{96,112},{112,0},{1... | collective-permute-start | bytes 49160 | tf_op jit(solution)/shard_map/ppermute | solution.py:187
  27.8 9.0 %all_to_all.31 = f32[16,2,128]{2,1,0:T(2,128)S(1)} all-to-all(f32[16,2,128]{2,1,0:T(2,128)S(1)} %bitcast.15), channel_id=1, replica_groups=mesh['slab'=8,'tile'=16] {'tile'}, dimensions={0} | all-to-all | bytes 32768 | tf_op jit(solution)/shard_map/all_to_all | solution.py:182
  36.8 0.0 collective-permute-done.1.above
  36.8 0.0 collective-permute-done.below
  36.8 0.0 copy-done.2
  36.8 0.0 copy-done.4
  36.8 0.0 copy-done.6
  36.8 0.0 copy-done.7
  36.8 0.0 copy-done.9
  36.8 0.0 copy-done.14
  36.8 0.0 copy-done.15
  36.8 2.5 %residual0.1 = (f32[32,128]{1,0:T(8,128)S(1)}, f32[32,128]{1,0:T(8,128)S(1)}, f32[8,128]{1,0:T(8,128)S(1)}, f32[8,128]{1,0:T(8,128)S(1)}, f32[8,128]{1,0:T(8,128)S(1)}, /*index=5*/f32[32,128]{1,0:T(8,128)S(1)}) custom-call(s32[2,32]{1,0:T(2,128)S(1)} %bitcast.25, s32[32]{0:T(128)S(1)} %copy-done.13, s32[32]{0:T(128)S(1)} %copy-done.14, s32[8]{0:T(128)S(1)} %copy-done.15, ...), custom_call_target="tpu_custom_call" | custom-call | flops 20000000000 | bytes 40000000 | tf_op jit(solution)/shard_map/residual0/pallas_call | solution.py:159
  39.3 9.3 %all_to_all.32 = f32[16,2,128]{2,1,0:T(2,128)S(1)} all-to-all(f32[16,2,128]{2,1,0:T(2,128)S(1)} %bitcast.19), channel_id=1, replica_groups=mesh['slab'=8,'tile'=16] {'tile'}, dimensions={0} | all-to-all | bytes 32768 | tf_op jit(solution)/shard_map/all_to_all | solution.py:182
  48.6 2.0 %step1.1 = (f32[32,128]{1,0:T(8,128)S(1)}, f32[32,128]{1,0:T(8,128)S(1)}, f32[32,128]{1,0:T(8,128)S(1)}) custom-call(s32[2,32]{1,0:T(2,128)S(1)} %bitcast.26, s32[32]{0:T(128)S(1)} %copy-done.13, f32[32,128,128]{2,1,0:T(8,128)S(1)} %copy-done.3, f32[32,4,128,128]{3,2,1,0:T(8,128)S(1)} %copy-done, f32[32,128,128]{2,1,0:T(8,128)S(1)} %copy-done.2, ...), custom_call_target="tpu_custom_call" | custom-call | flops 20000000000 | bytes 40000000 | tf_op jit(solution)/shard_map/step1/pallas_call | solution.py:159
  50.6 2.4 %collective-permute-start.3 = (f32[32,128]{1,0:T(8,128)S(1)}, f32[32,128]{1,0:T(8,128)S(1)}, u32[]{:S(2)}, u32[]{:S(2)}) collective-permute-start(f32[32,128]{1,0:T(8,128)S(1)} %get-tuple-element.35.s.s_in), channel_id=1, source_target_pairs={{16,0},{32,16},{48,32},{64,48},{80,64},{96,80},{112,96},{0,112},{1... | collective-permute-start | bytes 49160 | tf_op jit(solution)/shard_map/ppermute | solution.py:187
  53.0 0.8 collective-permute-start.2
  53.8 9.2 %all_to_all.33 = f32[16,2,128]{2,1,0:T(2,128)S(1)} all-to-all(f32[16,2,128]{2,1,0:T(2,128)S(1)} %bitcast.16), channel_id=1, replica_groups=mesh['slab'=8,'tile'=16] {'tile'}, dimensions={0} | all-to-all | bytes 32768 | tf_op jit(solution)/shard_map/all_to_all | solution.py:182
  63.0 0.0 collective-permute-done.3.above
  63.0 0.0 collective-permute-done.2.below
  63.0 3.0 %residual1.1 = (f32[32,128]{1,0:T(8,128)S(1)}, f32[32,128]{1,0:T(8,128)S(1)}, f32[8,128]{1,0:T(8,128)S(1)}, f32[8,128]{1,0:T(8,128)}, f32[8,128]{1,0:T(8,128)}, /*index=5*/f32[32,128]{1,0:T(8,128)S(1)}) custom-call(s32[2,32]{1,0:T(2,128)S(1)} %bitcast.27, s32[32]{0:T(128)S(1)} %copy-done.13, s32[32]{0:T(128)S(1)} %copy-done.14, s32[8]{0:T(128)S(1)} %copy-done.15, ...), custom_call_target="tpu_custom_call" | custom-call | flops 20000000000 | bytes 40000000 | tf_op jit(solution)/shard_map/residual1/pallas_call | solution.py:159
  66.0 9.4 %all_to_all.34 = f32[16,2,128]{2,1,0:T(2,128)S(1)} all-to-all(f32[16,2,128]{2,1,0:T(2,128)S(1)} %bitcast.17), channel_id=1, replica_groups=mesh['slab'=8,'tile'=16] {'tile'}, dimensions={0} | all-to-all | bytes 32768 | tf_op jit(solution)/shard_map/all_to_all | solution.py:182
  75.4 2.5 %step2.1 = (f32[32,128]{1,0:T(8,128)S(1)}, f32[32,128]{1,0:T(8,128)}, f32[32,128]{1,0:T(8,128)S(1)}) custom-call(s32[2,32]{1,0:T(2,128)S(1)} %bitcast.28, s32[32]{0:T(128)S(1)} %copy-done.13, f32[32,128,128]{2,1,0:T(8,128)S(1)} %copy-done.3, f32[32,4,128,128]{3,2,1,0:T(8,128)S(1)} %copy-done, f32[32,128,128]{2,1,0:T(8,128)S(1)} %copy-done.2, ...), custom_call_target="tpu_custom_call" | custom-call | flops 20000000000 | bytes 40000000 | tf_op jit(solution)/shard_map/step2/pallas_call | solution.py:159
  77.9 2.4 %collective-permute-start.5 = (f32[32,128]{1,0:T(8,128)S(1)}, f32[32,128]{1,0:T(8,128)S(1)}, u32[]{:S(2)}, u32[]{:S(2)}) collective-permute-start(f32[32,128]{1,0:T(8,128)S(1)} %get-tuple-element.46.s), channel_id=1, source_target_pairs={{16,0},{32,16},{48,32},{64,48},{80,64},{96,80},{112,96},{0,112},{1... | collective-permute-start | bytes 49160 | tf_op jit(solution)/shard_map/ppermute | solution.py:187
  80.3 0.7 collective-permute-start.4
  81.0 9.2 %all_to_all.35 = f32[16,2,128]{2,1,0:T(2,128)S(1)} all-to-all(f32[16,2,128]{2,1,0:T(2,128)S(1)} %bitcast.14), channel_id=1, replica_groups=mesh['slab'=8,'tile'=16] {'tile'}, dimensions={0} | all-to-all | bytes 32768 | tf_op jit(solution)/shard_map/all_to_all | solution.py:182
  90.2 0.0 collective-permute-done.5.above
  90.2 0.0 collective-permute-done.4.below
  90.2 2.2 %last.1 = f32[32,128]{1,0:T(8,128)} custom-call(s32[2,32]{1,0:T(2,128)S(1)} %bitcast.29, s32[32]{0:T(128)S(1)} %copy-done.13, s32[32]{0:T(128)S(1)} %copy-done.14, s32[8]{0:T(128)S(1)} %copy-done.15, f32[32,128,128]{2,1,0:T(8,128)S(1)} %copy-done.3, f32[32,4,128,128]{3,2,1,0:T(8,128)S(1)} %copy-done, f32[8,128,128]{2,1,0:T(8,128)S(1)} %copy-done.7, ...), custom_call_target="tpu_custom_call" | custom-call | flops 20000000000 | bytes 40000000 | tf_op jit(solution)/shard_map/last/pallas_call | solution.py:159
Async XLA Ops:
  1.3 1.6 %copy-start.1 = (f32[32,128,128]{2,1,0:T(8,128)S(1)}, f32[32,128,128]{2,1,0:T(8,128)}, u32[]{:S(2)}) copy-start(f32[32,128,128]{2,1,0:T(8,128)} %pre.11) | copy-start | bytes 6291460
  2.9 0.7 copy-start.8
  3.6 0.7 copy-start.11
  4.3 18.4 %copy-start = (f32[32,4,128,128]{3,2,1,0:T(8,128)S(1)}, f32[32,4,128,128]{3,2,1,0:T(8,128)}, u32[]{:S(2)}) copy-start(f32[32,4,128,128]{3,2,1,0:T(8,128)} %off.11) | copy-start | bytes 25165828
  4.3 18.4 %copy-start.3 = (f32[32,128,128]{2,1,0:T(8,128)S(1)}, f32[32,128,128]{2,1,0:T(8,128)}, u32[]{:S(2)}) copy-start(f32[32,128,128]{2,1,0:T(8,128)} %diag.11) | copy-start | bytes 6291460
  4.3 18.4 %copy-start.5 = (f32[8,128,128]{2,1,0:T(8,128)S(1)}, f32[8,128,128]{2,1,0:T(8,128)}, u32[]{:S(2)}) copy-start(f32[8,128,128]{2,1,0:T(8,128)} %root_pre.5) | copy-start | bytes 1572868
  4.3 18.4 %copy-start.10 = (f32[8,128]{1,0:T(8,128)S(1)}, f32[8,128]{1,0:T(8,128)}, u32[]{:S(2)}) copy-start(f32[8,128]{1,0:T(8,128)} %rr.1) | copy-start | bytes 12292
  4.3 18.4 %copy-start.12 = (s32[32,2]{0,1:T(2,128)S(1)}, s32[32,2]{0,1:T(2,128)}, u32[]{:S(2)}) copy-start(s32[32,2]{0,1:T(2,128)} %param.18) | copy-start | bytes 772
  4.3 18.4 %copy-start.13 = (s32[32]{0:T(128)S(1)}, s32[32]{0:T(128)}, u32[]{:S(2)}) copy-start(s32[32]{0:T(128)} %margin.11) | copy-start | bytes 388
  22.7 14.1 %copy-start.2 = (f32[32,128,128]{2,1,0:T(8,128)S(1)}, f32[32,128,128]{2,1,0:T(8,128)}, u32[]{:S(2)}) copy-start(f32[32,128,128]{2,1,0:T(8,128)} %pre.11) | copy-start | bytes 6291460
  22.7 14.1 %copy-start.4 = (f32[8,128,128]{2,1,0:T(8,128)S(1)}, f32[8,128,128]{2,1,0:T(8,128)}, u32[]{:S(2)}) copy-start(f32[8,128,128]{2,1,0:T(8,128)} %root_diag.3) | copy-start | bytes 1572868
  22.7 14.1 %copy-start.6 = (f32[8,128,128]{2,1,0:T(8,128)S(1)}, f32[8,128,128]{2,1,0:T(8,128)}, u32[]{:S(2)}) copy-start(f32[8,128,128]{2,1,0:T(8,128)} %root_up.3) | copy-start | bytes 1572868
  22.7 14.1 %copy-start.7 = (f32[8,128,128]{2,1,0:T(8,128)S(1)}, f32[8,128,128]{2,1,0:T(8,128)}, u32[]{:S(2)}) copy-start(f32[8,128,128]{2,1,0:T(8,128)} %down.5) | copy-start | bytes 1572868
  22.7 14.1 %copy-start.9 = (f32[32,128]{1,0:T(8,128)S(1)}, f32[32,128]{1,0:T(8,128)}, u32[]{:S(2)}) copy-start(f32[32,128]{1,0:T(8,128)} %res.1) | copy-start | bytes 49156
  22.7 14.1 %copy-start.14 = (s32[32]{0:T(128)S(1)}, s32[32]{0:T(128)}, u32[]{:S(2)}) copy-start(s32[32]{0:T(128)} %vert.5) | copy-start | bytes 388
  22.7 14.1 %copy-start.15 = (s32[8]{0:T(128)S(1)}, s32[8]{0:T(128)}, u32[]{:S(2)}) copy-start(s32[8]{0:T(128)} %cell.5) | copy-start | bytes 100
  24.8 12.0 %collective-permute-start.1 = (f32[32,128]{1,0:T(8,128)S(1)}, f32[32,128]{1,0:T(8,128)S(1)}, u32[]{:S(2)}, u32[]{:S(2)}) collective-permute-start(f32[32,128]{1,0:T(8,128)S(1)} %get-tuple-element.28.s.s_in.x_in), channel_id=1, source_target_pairs={{16,0},{32,16},{48,32},{64,48},{80,64},{96,80},{112,96},{0,112},{1... | collective-permute-start | bytes 49160 | tf_op jit(solution)/shard_map/ppermute | solution.py:187
  26.6 10.1 %collective-permute-start = (f32[32,128]{1,0:T(8,128)S(1)}, f32[32,128]{1,0:T(8,128)S(1)}, u32[]{:S(2)}, u32[]{:S(2)}) collective-permute-start(f32[32,128]{1,0:T(8,128)S(1)} %get-tuple-element.28.s.s_in.x_in), channel_id=1, source_target_pairs={{0,16},{16,32},{32,48},{48,64},{64,80},{80,96},{96,112},{112,0},{1... | collective-permute-start | bytes 49160 | tf_op jit(solution)/shard_map/ppermute | solution.py:187
  50.6 12.4 %collective-permute-start.3 = (f32[32,128]{1,0:T(8,128)S(1)}, f32[32,128]{1,0:T(8,128)S(1)}, u32[]{:S(2)}, u32[]{:S(2)}) collective-permute-start(f32[32,128]{1,0:T(8,128)S(1)} %get-tuple-element.35.s.s_in), channel_id=1, source_target_pairs={{16,0},{32,16},{48,32},{64,48},{80,64},{96,80},{112,96},{0,112},{1... | collective-permute-start | bytes 49160 | tf_op jit(solution)/shard_map/ppermute | solution.py:187
  53.0 10.0 %collective-permute-start.2 = (f32[32,128]{1,0:T(8,128)S(1)}, f32[32,128]{1,0:T(8,128)S(1)}, u32[]{:S(2)}, u32[]{:S(2)}) collective-permute-start(f32[32,128]{1,0:T(8,128)S(1)} %get-tuple-element.35.s.s_in), channel_id=1, source_target_pairs={{0,16},{16,32},{32,48},{48,64},{64,80},{80,96},{96,112},{112,0},{1... | collective-permute-start | bytes 49160 | tf_op jit(solution)/shard_map/ppermute | solution.py:187
  77.9 12.3 %collective-permute-start.5 = (f32[32,128]{1,0:T(8,128)S(1)}, f32[32,128]{1,0:T(8,128)S(1)}, u32[]{:S(2)}, u32[]{:S(2)}) collective-permute-start(f32[32,128]{1,0:T(8,128)S(1)} %get-tuple-element.46.s), channel_id=1, source_target_pairs={{16,0},{32,16},{48,32},{64,48},{80,64},{96,80},{112,96},{0,112},{1... | collective-permute-start | bytes 49160 | tf_op jit(solution)/shard_map/ppermute | solution.py:187
  80.3 9.9 %collective-permute-start.4 = (f32[32,128]{1,0:T(8,128)S(1)}, f32[32,128]{1,0:T(8,128)S(1)}, u32[]{:S(2)}, u32[]{:S(2)}) collective-permute-start(f32[32,128]{1,0:T(8,128)S(1)} %get-tuple-element.46.s), channel_id=1, source_target_pairs={{0,16},{16,32},{32,48},{48,64},{64,80},{80,96},{96,112},{112,0},{1... | collective-permute-start | bytes 49160 | tf_op jit(solution)/shard_map/ppermute | solution.py:187

commit v3 on v2

v3 whole, which is shorter than its diff:
```python
import functools

import jax
import jax.numpy as jnp
from jax import lax
from jax.experimental import pallas as pl
from jax.experimental.pallas import tpu as pltpu
from jax.sharding import PartitionSpec as P

SWEEPS = 3
LOW_BOUND = 0.25
HIGH_BOUND = 2.0
THETA = (HIGH_BOUND + LOW_BOUND) / 2.0
DELTA = (HIGH_BOUND - LOW_BOUND) / 2.0
SIGMA = THETA / DELTA

B = 128
NBD = 32
RCAP = 8
TILES = 16
CAP = 2
SLOTS = TILES * CAP
PIECE = NBD + 8
F32 = jnp.float32
OWN, MARGIN, VERT, CELL = 0, 2 * NBD, 3 * NBD, 4 * NBD
ENTRIES = CELL + RCAP

VMEM = pl.BlockSpec(memory_space=pltpu.VMEM)
SMEM = pl.BlockSpec(memory_space=pltpu.SMEM)


def row_sum(acc):
    lane = lax.broadcasted_iota(jnp.int32, (8, B), 1)
    sub = lax.broadcasted_iota(jnp.int32, (8, B), 0)
    ahead = lane - sub
    sums = jnp.sum(acc.reshape(B // 8, 8, B), axis=2, keepdims=True)
    out = jnp.zeros((8, B), F32)
    for k in range(B // 8):
        out = jnp.where(ahead == 8 * k, sums[k], out)
    return jnp.sum(out, axis=0, keepdims=True)


def product(*pairs):
    acc = None
    for mat, vec in pairs:
        term = mat * vec
        acc = term if acc is None else acc + term
    return row_sum(acc)


def row(ref, index):
    return ref[pl.ds(index, 1), :]


def at(ref, g):
    return ref[g : g + 1, :]


def pick(choice, values):
    return jnp.dot(
        choice[:, :NBD], values, precision=lax.Precision.HIGHEST, preferred_element_type=F32
    )


def anchor_kernel(out):
    out[...] = jnp.zeros_like(out)


def first_kernel(count, anchor, fetch, pre, rhs, t_out, send):
    for g in range(NBD):
        t_out[g : g + 1, :] = product((pre[g], at(rhs, g)))
    t = t_out[...]
    asked = fetch[0].astype(F32)
    lane = lax.broadcasted_iota(jnp.int32, asked.shape, 1)
    for p in range(TILES):
        send[p, :NBD, :] = t
        mine = jnp.sum(jnp.where(lane == p, asked, 0.0), axis=1, keepdims=True)
        send[p, NBD : NBD + CAP, :] = jnp.broadcast_to(mine, (CAP, B))


def extended_rows(own, near_row, diag, off, pre, t, res, w):
    for g in range(NBD):
        w[g : g + 1, :] = at(res, g) - product(
            (diag[g], at(t, g)),
            (off[g, 0], row(t, own(0, g))),
            (off[g, 1], row(t, own(1, g))),
            (off[g, 2], near_row(g)),
        )


def first_step_kernel(
    own, margin, vert, cell, fetch, count, diag, off, pre, t, table, rhs, root_pre, root_rhs,
    s_out, send, choice, index, live, ur_out, w,
):
    def near_row(g):
        peer = margin[g] // CAP
        return table[peer, pl.ds(fetch[0, margin[g] % CAP, peer], 1), :]

    def note(entry, value):
        index[entry : entry + 1, :] = jnp.full((1, B), value, jnp.int32)

    for g in range(NBD):
        note(OWN + g, own[0, g])
        note(OWN + NBD + g, own[1, g])
        note(MARGIN + g, margin[g])
        note(VERT + g, vert[g])
    for r in range(RCAP):
        note(CELL + r, cell[r])
    extended_rows(lambda k, g: own[k, g], near_row, diag, off, pre, t, rhs, w)
    for g in range(NBD):
        z = at(t, g) + product((pre[g], at(w, g)))
        s_out[g : g + 1, :] = z * (1.0 / THETA)
    lane = lax.broadcasted_iota(jnp.int32, (CAP, B), 1).astype(F32)
    for p in range(TILES):
        choice[CAP * p : CAP * (p + 1), :] = (table[p, NBD : NBD + CAP, :] == lane).astype(F32)
    send[...] = pick(choice[...], s_out[...])
    slot = lax.broadcasted_iota(jnp.int32, (RCAP, B), 0)
    live[...] = (slot < count[0]).astype(F32)
    for r in range(RCAP):
        z = product((root_pre[r], at(root_rhs, r)))
        ur_out[r : r + 1, :] = jnp.where(at(live, r) > 0.0, z * (1.0 / THETA), 0.0)


def step_kernel(
    keep, gain, index, diag, off, pre, t, table, res, s_in, choice, s_out, send, w,
):
    def own(k, g):
        return index[OWN + k * NBD + g, 0]

    extended_rows(own, lambda g: row(table, index[MARGIN + g, 0]), diag, off, pre, t, res, w)
    for g in range(NBD):
        z = at(t, g) + product((pre[g], at(w, g)))
        s_out[g : g + 1, :] = keep * at(s_in, g) + gain * z
    send[...] = pick(choice[...], s_out[...])


def residual_rows(index, diag, off, down, s, table, below, above, res, ur, r_out):
    r_out[...] = res[...]
    for r in range(RCAP):
        spot = pl.ds(index[CELL + r, 0], 1)
        r_out[spot, :] = r_out[spot, :] - product((down[r], at(ur, r)))
    for g in range(NBD):
        vert = index[VERT + g, 0]
        over = jnp.where(vert < NBD, row(below, vert % NBD), row(above, vert % NBD))
        r_out[g : g + 1, :] = at(r_out, g) - product(
            (diag[g], at(s, g)),
            (off[g, 0], row(s, index[OWN + g, 0])),
            (off[g, 1], row(s, index[OWN + NBD + g, 0])),
            (off[g, 2], row(table, index[MARGIN + g, 0])),
            (off[g, 3], over),
        )


def residual_kernel(
    keep, gain, index, diag, off, pre, root_diag, root_pre, root_up, down,
    s, table, below, above, res, ur, rr, live, choice,
    t_out, r_out, ur_out, send, rr_out,
):
    residual_rows(index, diag, off, down, s, table, below, above, res, ur, r_out)
    for g in range(NBD):
        t_out[g : g + 1, :] = product((pre[g], at(r_out, g)))
    send[...] = pick(choice[...], t_out[...])
    for r in range(RCAP):
        change = product(
            (root_diag[r], at(ur, r)), (root_up[r], row(s, index[CELL + r, 0]))
        )
        rr_out[r : r + 1, :] = at(rr, r) - change
    for r in range(RCAP):
        z = product((root_pre[r], at(rr_out, r)))
        ur_out[r : r + 1, :] = jnp.where(
            at(live, r) > 0.0, keep * at(ur, r) + gain * z, 0.0
        )


def last_kernel(
    index, diag, off, down, s, table, below, above, res, ur, s_first, s_before, ur_first, ur_before,
    r_out, x_out, root_x,
):
    x_out[...] = s_first[...] + s_before[...] + s[...]
    root_x[...] = ur_first[...] + ur_before[...] + ur[...]
    residual_rows(index, diag, off, down, s, table, below, above, res, ur, r_out)


def call(kernel, name, scalars, arrays, outs, scratch=()):
    shapes = [s if isinstance(s, jax.ShapeDtypeStruct) else jax.ShapeDtypeStruct(s, F32) for s in outs]
    return pl.pallas_call(
        kernel,
        out_shape=tuple(shapes),
        in_specs=[SMEM] * len(scalars) + [VMEM] * len(arrays),
        out_specs=(VMEM,) * len(outs),
        scratch_shapes=[pltpu.VMEM(shape, F32) for shape in scratch],
        compiler_params=pltpu.CompilerParams(vmem_limit_bytes=4 * 2**20),
        cost_estimate=pl.CostEstimate(
            flops=20_000_000_000, transcendentals=0, bytes_accessed=40_000_000
        ),
        name=name,
    )(*scalars, *arrays)


def body(
    soil_diag, soil_off, soil_pre, own_cols, margin_slot, vertical_col, fetch_rows, soil_rhs,
    root_diag, root_pre, root_up, root_down, root_cell, root_count, root_rhs,
):
    slabs = lax.axis_size("slab")
    own_cols, fetch_rows = own_cols.T, jnp.swapaxes(fetch_rows, 1, 2)
    soil, root, table = (NBD, B), (RCAP, B), (SLOTS, B)

    def exchange(rows):
        got = lax.all_to_all(rows.reshape(TILES, CAP, B), "tile", 0, 0)
        return got.reshape(SLOTS, B)

    def vertical(s):
        up = [(i, (i + 1) % slabs) for i in range(slabs)]
        above = lax.ppermute(s, "slab", [(j, i) for i, j in up])
        return lax.ppermute(s, "slab", up), above

    (anchor,) = call(anchor_kernel, "anchor", (), (), (root,))
    t, send = call(
        first_kernel, "first", (root_count,), (anchor, fetch_rows, soil_pre, soil_rhs), (soil, (TILES, PIECE, B))
    )
    got = lax.all_to_all(send, "tile", 0, 0)
    s, send, choice, index, live, ur = call(
        first_step_kernel, "step0",
        (own_cols, margin_slot, vertical_col, root_cell, fetch_rows, root_count),
        (soil_diag, soil_off, soil_pre, t, got, soil_rhs, root_pre, root_rhs),
        (soil, table, table, jax.ShapeDtypeStruct((ENTRIES, B), jnp.int32), root, root),
        (soil,),
    )
    r, rr, steps, urs = soil_rhs, root_rhs, [s], [ur]
    rho = 1.0 / SIGMA
    for sweep in range(SWEEPS):
        below, above = vertical(s)
        got = exchange(send)
        if sweep + 1 == SWEEPS:
            r, x, root_x = call(
                last_kernel, "last", (),
                (index, soil_diag, soil_off, root_down, s, got, below, above, r, ur, *steps[:2], *urs[:2]),
                (soil, soil, root),
            )
            break
        rho_new = 1.0 / (2.0 * SIGMA - rho)
        keep, gain = rho_new * rho, 2.0 * rho_new / DELTA
        rho = rho_new
        more = sweep + 2 < SWEEPS
        t, r, ur, send, *rest = call(
            functools.partial(residual_kernel, keep, gain), f"residual{sweep}", (),
            (index, soil_diag, soil_off, soil_pre, root_diag, root_pre, root_up, root_down,
             s, got, below, above, r, urs[-1], rr, live, choice),
            (soil, soil, root, table) + (root,) * more, (root,) * (not more),
        )
        rr = rest[0] if more else None
        urs.append(ur)
        got = exchange(send)
        s, send = call(
            functools.partial(step_kernel, keep, gain), f"step{sweep + 1}", (),
            (index, soil_diag, soil_off, soil_pre, t, got, r, s, choice),
            (soil, table), (soil,),
        )
        steps.append(s)
    return x, root_x, r


def solution(mesh):
    split = P(("slab", "tile"))
    return jax.shard_map(
        body, mesh=mesh, in_specs=(split,) * 15, out_specs=(split,) * 3, check_vma=False
    )
```

time: 92.9 us -> 86.7 us (0.933)
  Pallas kernels: 15.3 us -> 11.3 us
  local copies, waits for them, and re-layouts: 3.05 us -> 0.84 us
    pallas_call x7 -> x8, Pallas kernels: 15.3 us -> 11.3 us  [call(): pl.pallas_call(kernel, out_shape=tuple(shapes), in_specs=[SMEM] * len(sca...]
    unnamed x32 -> x30, local copies, waits for them, and re-layouts: 3.05 us -> 0.84 us
where the time goes in v3:
time: 86.7 us; the launch traced here: 86.3 us
  blocking collectives  63.1 us (73%)
  Pallas kernels  11.3 us (13%)
  starting transfers between devices  9.41 us (11%)
  between operations  1.66 us (2%)
    all_to_all x5, blocking collectives, exchange(): got = lax.all_to_all(rows.reshape(TILES, CAP, B), 'tile', 0, 0)  46 us
    all_to_all x1, blocking collectives, body(): got = lax.all_to_all(send, 'tile', 0, 0)  17.1 us
    pallas_call x8, Pallas kernels, call(): pl.pallas_call(kernel, out_shape=tuple(shapes), in_specs=[SMEM] * len(sca...  11.3 us
    ppermute x3, starting transfers between devices, vertical(): above = lax.ppermute(s, 'slab', [(j, i) for i, j in up])  6.76 us
    ppermute x3, starting transfers between devices, vertical(): return (lax.ppermute(s, 'slab', up), above)  2.65 us
  transfers between devices with their start and end apart: 6, of which 0 were waited for; matrix products, arithmetic and copies ran while one was open for 0% of the time, Pallas kernels for 0%

profile of v3, /device:TPU:1, one launch (start us, length us, event | category | flops | bytes accessed | tf_op | source)
XLA Modules:
  0.0 86.3 jit_solution(14685444506900807293)
XLA Ops:
  0.6 0.0 copy-start
  0.6 0.0 copy-start.6
  0.7 0.0 copy-start.9
  0.7 0.0 slice-start
  1.5 0.8 copy-done
  2.2 0.0 copy-done.6
  2.2 0.0 copy-done.9
  2.2 0.0 slice-start.1
  2.2 0.0 copy-start.1
  2.3 0.0 copy-start.2
  2.3 0.0 copy-start.7
  2.3 0.0 copy-start.8
  2.3 0.0 copy-start.10
  2.3 0.0 copy-start.11
  2.3 0.0 copy-start.12
  2.3 0.6 first.1
  3.0 17.1 %all_to_all.30.table = f32[16,40,128]{2,1,0:T(8,128)S(1)} all-to-all(f32[16,40,128]{2,1,0:T(8,128)S(1)} %get-tuple-element.28), channel_id=1, replica_groups=mesh['slab'=8,'tile'=16] {'tile'}, dimensions={0} | all-to-all | bytes 655360 | tf_op jit(solution)/shard_map/all_to_all | solution.py:221
  20.1 0.0 slice-done
  20.1 0.0 slice-done.1
  20.1 0.0 copy-done.1
  20.1 0.0 copy-done.2
  20.1 0.0 copy-done.7
  20.1 0.0 copy-done.8
  20.1 0.0 copy-done.10
  20.2 0.0 copy-done.11
  20.2 0.0 copy-done.12
  20.2 0.0 copy-start.3
  20.2 0.0 copy-start.4
  20.2 0.0 copy-start.5
  20.2 2.0 %step0.1 = (f32[32,128]{1,0:T(8,128)S(1)}, f32[32,128]{1,0:T(8,128)S(1)}, f32[32,128]{1,0:T(8,128)S(1)}, s32[136,128]{1,0:T(8,128)S(1)}, f32[8,128]{1,0:T(8,128)S(1)}, /*index=5*/f32[8,128]{1,0:T(8,128)S(1)}) custom-call(s32[2,32]{1,0:T(2,128)S(1)} %bitcast.24, s32[32]{0:T(128)S(1)} %copy-done.10, s32[32]{0:T(128)S(1)} %copy-done.11, s32[8]{0:T(128)S(1)} %copy-done.12, ...), custom_call_target="tpu_custom_call" | custom-call | flops 20000000000 | bytes 40000000 | tf_op jit(solution)/shard_map/step0/pallas_call | solution.py:186
  22.3 1.9 %collective-permute-start.1 = (f32[32,128]{1,0:T(8,128)S(1)}, f32[32,128]{1,0:T(8,128)S(1)}, u32[]{:S(2)}, u32[]{:S(2)}) collective-permute-start(f32[32,128]{1,0:T(8,128)S(1)} %get-tuple-element.30.s.s_in.s_first), channel_id=1, source_target_pairs={{16,0},{32,16},{48,32},{64,48},{80,64},{96,80},{112,96},{0,112},{1... | collective-permute-start | bytes 49160 | tf_op jit(solution)/shard_map/ppermute | solution.py:214
  24.1 1.1 %collective-permute-start = (f32[32,128]{1,0:T(8,128)S(1)}, f32[32,128]{1,0:T(8,128)S(1)}, u32[]{:S(2)}, u32[]{:S(2)}) collective-permute-start(f32[32,128]{1,0:T(8,128)S(1)} %get-tuple-element.30.s.s_in.s_first), channel_id=1, source_target_pairs={{0,16},{16,32},{32,48},{48,64},{64,80},{80,96},{96,112},{112,0},{1... | collective-permute-start | bytes 49160 | tf_op jit(solution)/shard_map/ppermute | solution.py:215
  25.3 9.0 %all_to_all.31 = f32[16,2,128]{2,1,0:T(2,128)S(1)} all-to-all(f32[16,2,128]{2,1,0:T(2,128)S(1)} %bitcast.13), channel_id=1, replica_groups=mesh['slab'=8,'tile'=16] {'tile'}, dimensions={0} | all-to-all | bytes 32768 | tf_op jit(solution)/shard_map/all_to_all | solution.py:209
  34.3 0.0 collective-permute-done.1.above
  34.3 0.0 collective-permute-done.below
  34.3 0.0 copy-done.3
  34.3 0.0 copy-done.4
  34.3 0.0 copy-done.5
  34.3 2.0 %residual0.1 = (f32[32,128]{1,0:T(8,128)S(1)}, f32[32,128]{1,0:T(8,128)S(1)}, f32[8,128]{1,0:T(8,128)S(1)}, f32[32,128]{1,0:T(8,128)S(1)}, f32[8,128]{1,0:T(8,128)S(1)}) custom-call(s32[136,128]{1,0:T(8,128)S(1)} %get-tuple-element.29.index, f32[32,128,128]{2,1,0:T(8,128)S(1)} %copy-done.1, f32[32,4,128,128]{3,2,1,0:T(8,128)S(1)} %bitcast.23, ...), custom_call_target="tpu_custom_call" | custom-call | flops 20000000000 | bytes 40000000 | tf_op jit(solution)/shard_map/residual0/pallas_call | solution.py:186
  36.3 9.3 %all_to_all.32 = f32[16,2,128]{2,1,0:T(2,128)S(1)} all-to-all(f32[16,2,128]{2,1,0:T(2,128)S(1)} %bitcast.19), channel_id=1, replica_groups=mesh['slab'=8,'tile'=16] {'tile'}, dimensions={0} | all-to-all | bytes 32768 | tf_op jit(solution)/shard_map/all_to_all | solution.py:209
  45.5 1.5 %step1.1 = (f32[32,128]{1,0:T(8,128)S(1)}, f32[32,128]{1,0:T(8,128)S(1)}) custom-call(s32[136,128]{1,0:T(8,128)S(1)} %get-tuple-element.29.index, f32[32,128,128]{2,1,0:T(8,128)S(1)} %copy-done.1, f32[32,4,128,128]{3,2,1,0:T(8,128)S(1)} %bitcast.23, f32[32,128,128]{2,1,0:T(8,128)S(1)} %copy-done, f32[32,128]{1,0:T(8,128)S(1)} %get-tuple-element.35.t, ...), custom_call_target="tpu_custom_call" | custom-call | flops 20000000000 | bytes 40000000 | tf_op jit(solution)/shard_map/step1/pallas_call | solution.py:186
  47.0 2.4 %collective-permute-start.3 = (f32[32,128]{1,0:T(8,128)S(1)}, f32[32,128]{1,0:T(8,128)S(1)}, u32[]{:S(2)}, u32[]{:S(2)}) collective-permute-start(f32[32,128]{1,0:T(8,128)S(1)} %get-tuple-element.38.s.s_in.s_before), channel_id=1, source_target_pairs={{16,0},{32,16},{48,32},{64,48},{80,64},{96,80},{112,96},{0,112},{1... | collective-permute-start | bytes 49160 | tf_op jit(solution)/shard_map/ppermute | solution.py:214
  49.5 0.8 collective-permute-start.2
  50.3 9.2 %all_to_all.33 = f32[16,2,128]{2,1,0:T(2,128)S(1)} all-to-all(f32[16,2,128]{2,1,0:T(2,128)S(1)} %bitcast.17), channel_id=1, replica_groups=mesh['slab'=8,'tile'=16] {'tile'}, dimensions={0} | all-to-all | bytes 32768 | tf_op jit(solution)/shard_map/all_to_all | solution.py:209
  59.5 0.0 collective-permute-done.3.above
  59.5 0.0 collective-permute-done.2.below
  59.5 2.0 %residual1.1 = (f32[32,128]{1,0:T(8,128)S(1)}, f32[32,128]{1,0:T(8,128)S(1)}, f32[8,128]{1,0:T(8,128)S(1)}, f32[32,128]{1,0:T(8,128)S(1)}) custom-call(s32[136,128]{1,0:T(8,128)S(1)} %get-tuple-element.29.index, f32[32,128,128]{2,1,0:T(8,128)S(1)} %copy-done.1, f32[32,4,128,128]{3,2,1,0:T(8,128)S(1)} %bitcast.23, f32[32,128,128]{2,1,0:T(8,128)S(1)} %copy-done, ...), custom_call_target="tpu_custom_call" | custom-call | flops 20000000000 | bytes 40000000 | tf_op jit(solution)/shard_map/residual1/pallas_call | solution.py:186
  61.4 9.4 %all_to_all.34 = f32[16,2,128]{2,1,0:T(2,128)S(1)} all-to-all(f32[16,2,128]{2,1,0:T(2,128)S(1)} %bitcast.18), channel_id=1, replica_groups=mesh['slab'=8,'tile'=16] {'tile'}, dimensions={0} | all-to-all | bytes 32768 | tf_op jit(solution)/shard_map/all_to_all | solution.py:209
  70.8 1.5 %step2.1 = (f32[32,128]{1,0:T(8,128)S(1)}, f32[32,128]{1,0:T(8,128)S(1)}) custom-call(s32[136,128]{1,0:T(8,128)S(1)} %get-tuple-element.29.index, f32[32,128,128]{2,1,0:T(8,128)S(1)} %copy-done.1, f32[32,4,128,128]{3,2,1,0:T(8,128)S(1)} %bitcast.23, f32[32,128,128]{2,1,0:T(8,128)S(1)} %copy-done, f32[32,128]{1,0:T(8,128)S(1)} %get-tuple-element.42.t, ...), custom_call_target="tpu_custom_call" | custom-call | flops 20000000000 | bytes 40000000 | tf_op jit(solution)/shard_map/step2/pallas_call | solution.py:186
  72.3 2.4 %collective-permute-start.5 = (f32[32,128]{1,0:T(8,128)S(1)}, f32[32,128]{1,0:T(8,128)S(1)}, u32[]{:S(2)}, u32[]{:S(2)}) collective-permute-start(f32[32,128]{1,0:T(8,128)S(1)} %get-tuple-element.45.s), channel_id=1, source_target_pairs={{16,0},{32,16},{48,32},{64,48},{80,64},{96,80},{112,96},{0,112},{1... | collective-permute-start | bytes 49160 | tf_op jit(solution)/shard_map/ppermute | solution.py:214
  74.8 0.7 collective-permute-start.4
  75.5 9.2 %all_to_all.35 = f32[16,2,128]{2,1,0:T(2,128)S(1)} all-to-all(f32[16,2,128]{2,1,0:T(2,128)S(1)} %bitcast.16), channel_id=1, replica_groups=mesh['slab'=8,'tile'=16] {'tile'}, dimensions={0} | all-to-all | bytes 32768 | tf_op jit(solution)/shard_map/all_to_all | solution.py:209
  84.6 0.0 collective-permute-done.5.above
  84.6 0.0 collective-permute-done.4.below
  84.6 1.7 %last.1 = (f32[32,128]{1,0:T(8,128)}, f32[32,128]{1,0:T(8,128)}, f32[8,128]{1,0:T(8,128)}) custom-call(s32[136,128]{1,0:T(8,128)S(1)} %get-tuple-element.29.index, f32[32,128,128]{2,1,0:T(8,128)S(1)} %copy-done.1, f32[32,4,128,128]{3,2,1,0:T(8,128)S(1)} %bitcast.23, f32[8,128,128]{2,1,0:T(8,128)S(1)} %copy-done.5, f32[32,128]{1,0:T(8,128)S(1)} %get-tuple-element.45.s, ...), custom_call_target="tpu_custom_call" | custom-call | flops 20000000000 | bytes 40000000 | tf_op jit(solution)/shard_map/last/pallas_call | solution.py:186
  (2 shorter events, 0.0 us)
Async XLA Ops:
  0.6 1.6 %copy-start = (f32[32,128,128]{2,1,0:T(8,128)S(1)}, f32[32,128,128]{2,1,0:T(8,128)}, u32[]{:S(2)}) copy-start(f32[32,128,128]{2,1,0:T(8,128)} %pre.11) | copy-start | bytes 6291460
  0.6 1.6 %copy-start.6 = (f32[32,128]{1,0:T(8,128)S(1)}, f32[32,128]{1,0:T(8,128)}, u32[]{:S(2)}) copy-start(f32[32,128]{1,0:T(8,128)} %res.1) | copy-start | bytes 49156
  0.7 1.6 %copy-start.9 = (s32[1,16,2]{1,2,0:T(2,128)S(1)}, s32[1,16,2]{1,2,0:T(2,128)}, u32[]{:S(2)}) copy-start(s32[1,16,2]{1,2,0:T(2,128)} %param.21) | copy-start | bytes 388
  0.7 19.4 %slice-start = ((s8[8388608]{0:T(1024)(128)(4,1)}), s8[4194304]{0:T(1024)(128)(4,1)S(1)}, s32[]{:S(2)}) async-start(s8[8388608]{0:T(1024)(128)(4,1)} %bitcast.22), calls=%async_computation.6 | async-start | bytes 8388608
  2.2 17.9 %slice-start.1 = ((s8[8388608]{0:T(1024)(128)(4,1)}), s8[4194304]{0:T(1024)(128)(4,1)S(1)}, s32[]{:S(2)}) async-start(s8[8388608]{0:T(1024)(128)(4,1)} %bitcast.22), calls=%async_computation.7 | async-start | bytes 8388608
  2.2 17.9 %copy-start.1 = (f32[32,128,128]{2,1,0:T(8,128)S(1)}, f32[32,128,128]{2,1,0:T(8,128)}, u32[]{:S(2)}) copy-start(f32[32,128,128]{2,1,0:T(8,128)} %diag.11) | copy-start | bytes 6291460
  2.3 17.9 %copy-start.2 = (f32[8,128,128]{2,1,0:T(8,128)S(1)}, f32[8,128,128]{2,1,0:T(8,128)}, u32[]{:S(2)}) copy-start(f32[8,128,128]{2,1,0:T(8,128)} %root_pre.5) | copy-start | bytes 1572868
  2.3 17.9 %copy-start.7 = (f32[8,128]{1,0:T(8,128)S(1)}, f32[8,128]{1,0:T(8,128)}, u32[]{:S(2)}) copy-start(f32[8,128]{1,0:T(8,128)} %rr.1) | copy-start | bytes 12292
  2.3 17.9 %copy-start.8 = (s32[32,2]{0,1:T(2,128)S(1)}, s32[32,2]{0,1:T(2,128)}, u32[]{:S(2)}) copy-start(s32[32,2]{0,1:T(2,128)} %param.18) | copy-start | bytes 772
  2.3 17.9 %copy-start.10 = (s32[32]{0:T(128)S(1)}, s32[32]{0:T(128)}, u32[]{:S(2)}) copy-start(s32[32]{0:T(128)} %margin.1) | copy-start | bytes 388
  2.3 17.9 %copy-start.11 = (s32[32]{0:T(128)S(1)}, s32[32]{0:T(128)}, u32[]{:S(2)}) copy-start(s32[32]{0:T(128)} %vert.1) | copy-start | bytes 388
  2.3 17.9 %copy-start.12 = (s32[8]{0:T(128)S(1)}, s32[8]{0:T(128)}, u32[]{:S(2)}) copy-start(s32[8]{0:T(128)} %cell.1) | copy-start | bytes 100
  20.2 14.1 %copy-start.3 = (f32[8,128,128]{2,1,0:T(8,128)S(1)}, f32[8,128,128]{2,1,0:T(8,128)}, u32[]{:S(2)}) copy-start(f32[8,128,128]{2,1,0:T(8,128)} %root_diag.3) | copy-start | bytes 1572868
  20.2 14.1 %copy-start.4 = (f32[8,128,128]{2,1,0:T(8,128)S(1)}, f32[8,128,128]{2,1,0:T(8,128)}, u32[]{:S(2)}) copy-start(f32[8,128,128]{2,1,0:T(8,128)} %root_up.3) | copy-start | bytes 1572868
  20.2 14.1 %copy-start.5 = (f32[8,128,128]{2,1,0:T(8,128)S(1)}, f32[8,128,128]{2,1,0:T(8,128)}, u32[]{:S(2)}) copy-start(f32[8,128,128]{2,1,0:T(8,128)} %down.5) | copy-start | bytes 1572868
  22.3 12.0 %collective-permute-start.1 = (f32[32,128]{1,0:T(8,128)S(1)}, f32[32,128]{1,0:T(8,128)S(1)}, u32[]{:S(2)}, u32[]{:S(2)}) collective-permute-start(f32[32,128]{1,0:T(8,128)S(1)} %get-tuple-element.30.s.s_in.s_first), channel_id=1, source_target_pairs={{16,0},{32,16},{48,32},{64,48},{80,64},{96,80},{112,96},{0,112},{1... | collective-permute-start | bytes 49160 | tf_op jit(solution)/shard_map/ppermute | solution.py:214
  24.1 10.1 %collective-permute-start = (f32[32,128]{1,0:T(8,128)S(1)}, f32[32,128]{1,0:T(8,128)S(1)}, u32[]{:S(2)}, u32[]{:S(2)}) collective-permute-start(f32[32,128]{1,0:T(8,128)S(1)} %get-tuple-element.30.s.s_in.s_first), channel_id=1, source_target_pairs={{0,16},{16,32},{32,48},{48,64},{64,80},{80,96},{96,112},{112,0},{1... | collective-permute-start | bytes 49160 | tf_op jit(solution)/shard_map/ppermute | solution.py:215
  47.0 12.4 %collective-permute-start.3 = (f32[32,128]{1,0:T(8,128)S(1)}, f32[32,128]{1,0:T(8,128)S(1)}, u32[]{:S(2)}, u32[]{:S(2)}) collective-permute-start(f32[32,128]{1,0:T(8,128)S(1)} %get-tuple-element.38.s.s_in.s_before), channel_id=1, source_target_pairs={{16,0},{32,16},{48,32},{64,48},{80,64},{96,80},{112,96},{0,112},{1... | collective-permute-start | bytes 49160 | tf_op jit(solution)/shard_map/ppermute | solution.py:214
  49.5 10.0 %collective-permute-start.2 = (f32[32,128]{1,0:T(8,128)S(1)}, f32[32,128]{1,0:T(8,128)S(1)}, u32[]{:S(2)}, u32[]{:S(2)}) collective-permute-start(f32[32,128]{1,0:T(8,128)S(1)} %get-tuple-element.38.s.s_in.s_before), channel_id=1, source_target_pairs={{0,16},{16,32},{32,48},{48,64},{64,80},{80,96},{96,112},{112,0},{1... | collective-permute-start | bytes 49160 | tf_op jit(solution)/shard_map/ppermute | solution.py:215
  72.3 12.3 %collective-permute-start.5 = (f32[32,128]{1,0:T(8,128)S(1)}, f32[32,128]{1,0:T(8,128)S(1)}, u32[]{:S(2)}, u32[]{:S(2)}) collective-permute-start(f32[32,128]{1,0:T(8,128)S(1)} %get-tuple-element.45.s), channel_id=1, source_target_pairs={{16,0},{32,16},{48,32},{64,48},{80,64},{96,80},{112,96},{0,112},{1... | collective-permute-start | bytes 49160 | tf_op jit(solution)/shard_map/ppermute | solution.py:214
  74.8 9.9 %collective-permute-start.4 = (f32[32,128]{1,0:T(8,128)S(1)}, f32[32,128]{1,0:T(8,128)S(1)}, u32[]{:S(2)}, u32[]{:S(2)}) collective-permute-start(f32[32,128]{1,0:T(8,128)S(1)} %get-tuple-element.45.s), channel_id=1, source_target_pairs={{0,16},{16,32},{32,48},{48,64},{64,80},{80,96},{96,112},{112,0},{1... | collective-permute-start | bytes 49160 | tf_op jit(solution)/shard_map/ppermute | solution.py:215

commit v4 on v3

v4 whole, which is shorter than its diff:
```python
import functools

import jax
import jax.numpy as jnp
from jax import lax
from jax.experimental import pallas as pl
from jax.experimental.pallas import tpu as pltpu
from jax.sharding import PartitionSpec as P

SWEEPS = 3
LOW_BOUND = 0.25
HIGH_BOUND = 2.0
THETA = (HIGH_BOUND + LOW_BOUND) / 2.0
DELTA = (HIGH_BOUND - LOW_BOUND) / 2.0
SIGMA = THETA / DELTA

B = 128
NBD = 32
RCAP = 8
TILES = 16
CAP = 2
SLOTS = TILES * CAP
PIECE = NBD + 8
F32 = jnp.float32
OWN, MARGIN, VERT, WIDE, CELL = 0, 2 * NBD, 3 * NBD, 4 * NBD, 5 * NBD
ENTRIES = CELL + RCAP
LAG = 6

VMEM = pl.BlockSpec(memory_space=pltpu.VMEM)
SMEM = pl.BlockSpec(memory_space=pltpu.SMEM)


def row_sum(acc):
    lane = lax.broadcasted_iota(jnp.int32, (8, B), 1)
    sub = lax.broadcasted_iota(jnp.int32, (8, B), 0)
    ahead = lane - sub
    sums = jnp.sum(acc.reshape(B // 8, 8, B), axis=2, keepdims=True)
    out = jnp.zeros((8, B), F32)
    for k in range(B // 8):
        out = jnp.where(ahead == 8 * k, sums[k], out)
    return jnp.sum(out, axis=0, keepdims=True)


def product(*pairs):
    acc = None
    for mat, vec in pairs:
        term = mat * vec
        acc = term if acc is None else acc + term
    return row_sum(acc)


def row(ref, index):
    return ref[pl.ds(index, 1), :]


def at(ref, g):
    return ref[g : g + 1, :]


def send_rows(asked, values, send):
    for q in range(SLOTS):
        send[q : q + 1, :] = row(values, asked[q, 0])


def anchor_kernel(out):
    out[...] = jnp.zeros_like(out)


def list_kernel(own, margin, vert, cell, fetch, count, anchor, index, wish, live):
    def note(entry, value):
        index[entry : entry + 1, :] = jnp.full((1, B), value, jnp.int32)

    for g in range(NBD):
        note(OWN + g, own[0, g])
        note(OWN + NBD + g, own[1, g])
        note(MARGIN + g, margin[g])
        note(VERT + g, vert[g])
        peer = margin[g] // CAP
        note(WIDE + g, peer * PIECE + fetch[0, margin[g] % CAP, peer])
    for r in range(RCAP):
        note(CELL + r, cell[r])
    for q in range(SLOTS):
        wish[q : q + 1, :] = jnp.full((1, B), fetch[0, q % CAP, q // CAP], jnp.int32).astype(F32)
    slot = lax.broadcasted_iota(jnp.int32, (RCAP, B), 0)
    live[...] = (slot < count[0]).astype(F32)


def first_kernel(wish, pre, rhs, t_out, send):
    for g in range(NBD):
        t_out[g : g + 1, :] = product((pre[g], at(rhs, g)))
    t = t_out[...]
    for p in range(TILES):
        send[p, :NBD, :] = t
        send[p, NBD : NBD + CAP, :] = wish[CAP * p : CAP * (p + 1), :]


def staggered(first, second):
    for g in range(NBD + LAG):
        if g < NBD:
            first(g)
        if g >= LAG:
            second(g - LAG)


def step_rows(index, near, near_at, diag, off, pre, t, res, w, finish):
    def extended(g):
        w[g : g + 1, :] = at(res, g) - product(
            (diag[g], at(t, g)),
            (off[g, 0], row(t, index[OWN + g, 0])),
            (off[g, 1], row(t, index[OWN + NBD + g, 0])),
            (off[g, 2], row(near, index[near_at + g, 0])),
        )

    def turn(g):
        finish(g, at(t, g) + product((pre[g], at(w, g))))

    staggered(extended, turn)


def first_step_kernel(
    index, live, diag, off, pre, t, table, rhs, root_pre, root_rhs,
    s_out, send, asked, ur_out, w,
):
    for p in range(TILES):
        asked[CAP * p : CAP * (p + 1), :] = table[
            PIECE * p + NBD : PIECE * p + NBD + CAP, :
        ].astype(jnp.int32)

    def finish(g, z):
        s_out[g : g + 1, :] = z * (1.0 / THETA)

    step_rows(index, table, WIDE, diag, off, pre, t, rhs, w, finish)
    for r in range(RCAP):
        z = product((root_pre[r], at(root_rhs, r)))
        ur_out[r : r + 1, :] = jnp.where(at(live, r) > 0.0, z * (1.0 / THETA), 0.0)
    send_rows(asked, s_out, send)


def step_kernel(keep, gain, index, diag, off, pre, t, table, res, s_in, asked, s_out, send, w):
    def finish(g, z):
        s_out[g : g + 1, :] = keep * at(s_in, g) + gain * z

    step_rows(index, table, MARGIN, diag, off, pre, t, res, w, finish)
    send_rows(asked, s_out, send)


def residual_rows(index, diag, off, down, s, table, below, above, res, ur, r_out, after=None):
    r_out[...] = res[...]
    for r in range(RCAP):
        spot = pl.ds(index[CELL + r, 0], 1)
        r_out[spot, :] = r_out[spot, :] - product((down[r], at(ur, r)))

    def applied(g):
        vert = index[VERT + g, 0]
        over = jnp.where(vert < NBD, row(below, vert % NBD), row(above, vert % NBD))
        r_out[g : g + 1, :] = at(r_out, g) - product(
            (diag[g], at(s, g)),
            (off[g, 0], row(s, index[OWN + g, 0])),
            (off[g, 1], row(s, index[OWN + NBD + g, 0])),
            (off[g, 2], row(table, index[MARGIN + g, 0])),
            (off[g, 3], over),
        )

    staggered(applied, after or (lambda g: None))


def residual_kernel(
    keep, gain, index, diag, off, pre, root_diag, root_pre, root_up, down,
    s, table, below, above, res, ur, rr, live, asked,
    t_out, r_out, ur_out, send, rr_out,
):
    for r in range(RCAP):
        change = product(
            (root_diag[r], at(ur, r)), (root_up[r], row(s, index[CELL + r, 0]))
        )
        rr_out[r : r + 1, :] = at(rr, r) - change

    def turn(g):
        t_out[g : g + 1, :] = product((pre[g], at(r_out, g)))

    residual_rows(index, diag, off, down, s, table, below, above, res, ur, r_out, turn)
    for r in range(RCAP):
        z = product((root_pre[r], at(rr_out, r)))
        ur_out[r : r + 1, :] = jnp.where(
            at(live, r) > 0.0, keep * at(ur, r) + gain * z, 0.0
        )
    send_rows(asked, t_out, send)


def last_kernel(
    index, diag, off, down, s, table, below, above, res, ur, s_first, s_before, ur_first, ur_before,
    r_out, x_out, root_x,
):
    x_out[...] = s_first[...] + s_before[...] + s[...]
    root_x[...] = ur_first[...] + ur_before[...] + ur[...]
    residual_rows(index, diag, off, down, s, table, below, above, res, ur, r_out)


def call(kernel, name, scalars, arrays, outs, scratch=(), work=20_000_000_000):
    shapes = [s if isinstance(s, jax.ShapeDtypeStruct) else jax.ShapeDtypeStruct(s, F32) for s in outs]
    return pl.pallas_call(
        kernel,
        out_shape=tuple(shapes),
        in_specs=[SMEM] * len(scalars) + [VMEM] * len(arrays),
        out_specs=(VMEM,) * len(outs),
        scratch_shapes=[pltpu.VMEM(shape, F32) for shape in scratch],
        compiler_params=pltpu.CompilerParams(vmem_limit_bytes=4 * 2**20),
        cost_estimate=pl.CostEstimate(
            flops=work, transcendentals=0, bytes_accessed=work // 500
        ),
        name=name,
    )(*scalars, *arrays)


def body(
    soil_diag, soil_off, soil_pre, own_cols, margin_slot, vertical_col, fetch_rows, soil_rhs,
    root_diag, root_pre, root_up, root_down, root_cell, root_count, root_rhs,
):
    slabs = lax.axis_size("slab")
    own_cols, fetch_rows = own_cols.T, jnp.swapaxes(fetch_rows, 1, 2)
    soil, root, table = (NBD, B), (RCAP, B), (SLOTS, B)

    def exchange(rows):
        got = lax.all_to_all(rows.reshape(TILES, CAP, B), "tile", 0, 0)
        return got.reshape(SLOTS, B)

    def vertical(s):
        up = [(i, (i + 1) % slabs) for i in range(slabs)]
        above = lax.ppermute(s, "slab", [(j, i) for i, j in up])
        return lax.ppermute(s, "slab", up), above

    (anchor,) = call(anchor_kernel, "anchor", (), (), (root,))
    entries = jax.ShapeDtypeStruct((ENTRIES, B), jnp.int32)
    index, wish, live = call(
        list_kernel, "lists",
        (own_cols, margin_slot, vertical_col, root_cell, fetch_rows, root_count),
        (anchor,), (entries, table, root), work=1000,
    )
    t, send = call(
        first_kernel, "first", (), (wish, soil_pre, soil_rhs), (soil, (TILES, PIECE, B))
    )
    got = lax.all_to_all(send, "tile", 0, 0).reshape(TILES * PIECE, B)
    s, send, asked, ur = call(
        first_step_kernel, "step0", (),
        (index, live, soil_diag, soil_off, soil_pre, t, got, soil_rhs, root_pre, root_rhs),
        (soil, table, jax.ShapeDtypeStruct(table, jnp.int32), root), (soil,),
    )
    r, rr, steps, urs = soil_rhs, root_rhs, [s], [ur]
    rho = 1.0 / SIGMA
    for sweep in range(SWEEPS):
        below, above = vertical(s)
        got = exchange(send)
        if sweep + 1 == SWEEPS:
            r, x, root_x = call(
                last_kernel, "last", (),
                (index, soil_diag, soil_off, root_down, s, got, below, above, r, ur, *steps[:2], *urs[:2]),
                (soil, soil, root),
            )
            break
        rho_new = 1.0 / (2.0 * SIGMA - rho)
        keep, gain = rho_new * rho, 2.0 * rho_new / DELTA
        rho = rho_new
        more = sweep + 2 < SWEEPS
        t, r, ur, send, *rest = call(
            functools.partial(residual_kernel, keep, gain), f"residual{sweep}", (),
            (index, soil_diag, soil_off, soil_pre, root_diag, root_pre, root_up, root_down,
             s, got, below, above, r, urs[-1], rr, live, asked),
            (soil, soil, root, table) + (root,) * more, (root,) * (not more),
        )
        rr = rest[0] if more else None
        urs.append(ur)
        got = exchange(send)
        s, send = call(
            functools.partial(step_kernel, keep, gain), f"step{sweep + 1}", (),
            (index, soil_diag, soil_off, soil_pre, t, got, r, s, asked),
            (soil, table), (soil,),
        )
        steps.append(s)
    return x, root_x, r


def solution(mesh):
    split = P(("slab", "tile"))
    return jax.shard_map(
        body, mesh=mesh, in_specs=(split,) * 15, out_specs=(split,) * 3, check_vma=False
    )
```

time: 86.7 us -> 86 us (level)
    pallas_call x8 -> x9, Pallas kernels: 11.3 us -> 11.3 us  [call(): pl.pallas_call(kernel, out_shape=tuple(shapes), in_specs=[SMEM] * len(sca...]
where the time goes in v4:
time: 86 us; the launch traced here: 85.7 us
  blocking collectives  63.1 us (73%)
  Pallas kernels  11.3 us (13%)
  starting transfers between devices  9.44 us (11%)
  between operations  1.69 us (2%)
    all_to_all x5, blocking collectives, exchange(): got = lax.all_to_all(rows.reshape(TILES, CAP, B), 'tile', 0, 0)  46 us
    all_to_all x1, blocking collectives, body(): got = lax.all_to_all(send, 'tile', 0, 0).reshape(TILES * PIECE, B)  17.1 us
    pallas_call x9, Pallas kernels, call(): pl.pallas_call(kernel, out_shape=tuple(shapes), in_specs=[SMEM] * len(sca...  11.3 us
    ppermute x3, starting transfers between devices, vertical(): above = lax.ppermute(s, 'slab', [(j, i) for i, j in up])  6.73 us
    ppermute x3, starting transfers between devices, vertical(): return (lax.ppermute(s, 'slab', up), above)  2.7 us
  transfers between devices with their start and end apart: 6, of which 0 were waited for; matrix products, arithmetic and copies ran while one was open for 0% of the time, Pallas kernels for 0%

profile of v4, /device:TPU:1, one launch (start us, length us, event | category | flops | bytes accessed | tf_op | source)
XLA Modules:
  0.0 85.7 jit_solution(3172643566655727103)
XLA Ops:
  0.6 0.0 copy-start.4
  0.6 0.0 copy-start.1
  0.7 0.0 copy-start.3
  0.7 0.0 copy-start.2
  0.7 0.0 copy-start
  0.7 0.0 copy-start.5
  0.7 0.0 copy-start.11
  0.7 0.0 slice-start
  1.5 0.0 copy-done.4
  1.5 0.0 copy-done.1
  1.5 0.0 copy-done.3
  1.6 0.0 copy-done.2
  1.6 0.0 copy-done
  1.6 0.9 %lists.1 = (s32[168,128]{1,0:T(8,128)S(1)}, f32[32,128]{1,0:T(8,128)S(1)}, f32[8,128]{1,0:T(8,128)S(1)}) custom-call(s32[2,32]{1,0:T(2,128)S(1)} %bitcast.24, s32[32]{0:T(128)S(1)} %copy-done.2, s32[32]{0:T(128)S(1)} %copy-done.3, s32[8]{0:T(128)S(1)} %copy-done.4, s32[1,2,16]{2,1,0:T(2,128)S(1)} %bitcast.25, s32[1]{0:T(128)S(6)} %copy.18.count, ...), custom_call_target="tpu_custom_call" | custom-call | flops 1000 | bytes 2 | tf_op jit(solution)/shard_map/lists/pallas_call | solution.py:201
  2.4 0.0 copy-done.5
  2.5 0.0 copy-done.11
  2.5 0.0 slice-start.1
  2.5 0.0 copy-start.6
  2.5 0.0 copy-start.8
  2.5 0.0 copy-start.12
  2.5 0.6 first.1
  3.2 17.1 %all_to_all.30 = f32[16,40,128]{2,1,0:T(8,128)S(1)} all-to-all(f32[16,40,128]{2,1,0:T(8,128)S(1)} %get-tuple-element.32), channel_id=1, replica_groups=mesh['slab'=8,'tile'=16] {'tile'}, dimensions={0} | all-to-all | bytes 655360 | tf_op jit(solution)/shard_map/all_to_all | solution.py:242
  20.3 0.0 slice-done
  20.3 0.0 slice-done.1
  20.3 0.0 copy-done.6
  20.3 0.0 copy-done.8
  20.3 0.0 copy-done.12
  20.3 0.0 copy-start.7
  20.3 0.0 copy-start.9
  20.4 0.0 copy-start.10
  20.4 1.5 %step0.1 = (f32[32,128]{1,0:T(8,128)S(1)}, f32[32,128]{1,0:T(8,128)S(1)}, s32[32,128]{1,0:T(8,128)S(1)}, f32[8,128]{1,0:T(8,128)S(1)}) custom-call(s32[168,128]{1,0:T(8,128)S(1)} %get-tuple-element.28.index, f32[8,128]{1,0:T(8,128)S(1)} %get-tuple-element.29.live, f32[32,128,128]{2,1,0:T(8,128)S(1)} %copy-done.6, f32[32,4,128,128]{3,2,1,0:T(8,128)S(1)} %bitcast.27, ...), custom_call_target="tpu_custom_call" | custom-call | flops 20000000000 | bytes 40000000 | tf_op jit(solution)/shard_map/step0/pallas_call | solution.py:201
  21.9 1.9 %collective-permute-start.1 = (f32[32,128]{1,0:T(8,128)S(1)}, f32[32,128]{1,0:T(8,128)S(1)}, u32[]{:S(2)}, u32[]{:S(2)}) collective-permute-start(f32[32,128]{1,0:T(8,128)S(1)} %get-tuple-element.33.s.s_in.s_first), channel_id=1, source_target_pairs={{16,0},{32,16},{48,32},{64,48},{80,64},{96,80},{112,96},{0,112},{1... | collective-permute-start | bytes 49160 | tf_op jit(solution)/shard_map/ppermute | solution.py:229
  23.8 1.1 %collective-permute-start = (f32[32,128]{1,0:T(8,128)S(1)}, f32[32,128]{1,0:T(8,128)S(1)}, u32[]{:S(2)}, u32[]{:S(2)}) collective-permute-start(f32[32,128]{1,0:T(8,128)S(1)} %get-tuple-element.33.s.s_in.s_first), channel_id=1, source_target_pairs={{0,16},{16,32},{32,48},{48,64},{64,80},{80,96},{96,112},{112,0},{1... | collective-permute-start | bytes 49160 | tf_op jit(solution)/shard_map/ppermute | solution.py:230
  24.9 9.0 %all_to_all.31 = f32[16,2,128]{2,1,0:T(2,128)S(1)} all-to-all(f32[16,2,128]{2,1,0:T(2,128)S(1)} %bitcast.17), channel_id=1, replica_groups=mesh['slab'=8,'tile'=16] {'tile'}, dimensions={0} | all-to-all | bytes 32768 | tf_op jit(solution)/shard_map/all_to_all | solution.py:224
  33.9 0.0 collective-permute-done.1.above
  33.9 0.0 collective-permute-done.below
  33.9 0.0 copy-done.7
  33.9 0.0 copy-done.9
  33.9 0.0 copy-done.10
  33.9 1.9 %residual0.1 = (f32[32,128]{1,0:T(8,128)S(1)}, f32[32,128]{1,0:T(8,128)S(1)}, f32[8,128]{1,0:T(8,128)S(1)}, f32[32,128]{1,0:T(8,128)S(1)}, f32[8,128]{1,0:T(8,128)S(1)}) custom-call(s32[168,128]{1,0:T(8,128)S(1)} %get-tuple-element.28.index, f32[32,128,128]{2,1,0:T(8,128)S(1)} %copy-done.6, f32[32,4,128,128]{3,2,1,0:T(8,128)S(1)} %bitcast.27, ...), custom_call_target="tpu_custom_call" | custom-call | flops 20000000000 | bytes 40000000 | tf_op jit(solution)/shard_map/residual0/pallas_call | solution.py:201
  35.8 9.3 %all_to_all.32 = f32[16,2,128]{2,1,0:T(2,128)S(1)} all-to-all(f32[16,2,128]{2,1,0:T(2,128)S(1)} %bitcast.21), channel_id=1, replica_groups=mesh['slab'=8,'tile'=16] {'tile'}, dimensions={0} | all-to-all | bytes 32768 | tf_op jit(solution)/shard_map/all_to_all | solution.py:224
  45.1 1.4 %step1.1 = (f32[32,128]{1,0:T(8,128)S(1)}, f32[32,128]{1,0:T(8,128)S(1)}) custom-call(s32[168,128]{1,0:T(8,128)S(1)} %get-tuple-element.28.index, f32[32,128,128]{2,1,0:T(8,128)S(1)} %copy-done.6, f32[32,4,128,128]{3,2,1,0:T(8,128)S(1)} %bitcast.27, f32[32,128,128]{2,1,0:T(8,128)S(1)} %copy-done.5, f32[32,128]{1,0:T(8,128)S(1)} %get-tuple-element.37.t, ...), custom_call_target="tpu_custom_call" | custom-call | flops 20000000000 | bytes 40000000 | tf_op jit(solution)/shard_map/step1/pallas_call | solution.py:201
  46.5 2.4 %collective-permute-start.3 = (f32[32,128]{1,0:T(8,128)S(1)}, f32[32,128]{1,0:T(8,128)S(1)}, u32[]{:S(2)}, u32[]{:S(2)}) collective-permute-start(f32[32,128]{1,0:T(8,128)S(1)} %get-tuple-element.40.s.s_in.s_before), channel_id=1, source_target_pairs={{16,0},{32,16},{48,32},{64,48},{80,64},{96,80},{112,96},{0,112},{1... | collective-permute-start | bytes 49160 | tf_op jit(solution)/shard_map/ppermute | solution.py:229
  49.0 0.8 collective-permute-start.2
  49.8 9.2 %all_to_all.33 = f32[16,2,128]{2,1,0:T(2,128)S(1)} all-to-all(f32[16,2,128]{2,1,0:T(2,128)S(1)} %bitcast.19), channel_id=1, replica_groups=mesh['slab'=8,'tile'=16] {'tile'}, dimensions={0} | all-to-all | bytes 32768 | tf_op jit(solution)/shard_map/all_to_all | solution.py:224
  59.0 0.0 collective-permute-done.3.above
  59.0 0.0 collective-permute-done.2.below
  59.0 1.9 %residual1.1 = (f32[32,128]{1,0:T(8,128)S(1)}, f32[32,128]{1,0:T(8,128)S(1)}, f32[8,128]{1,0:T(8,128)S(1)}, f32[32,128]{1,0:T(8,128)S(1)}) custom-call(s32[168,128]{1,0:T(8,128)S(1)} %get-tuple-element.28.index, f32[32,128,128]{2,1,0:T(8,128)S(1)} %copy-done.6, f32[32,4,128,128]{3,2,1,0:T(8,128)S(1)} %bitcast.27, f32[32,128,128]{2,1,0:T(8,128)S(1)} %copy-done.5, ...), custom_call_target="tpu_custom_call" | custom-call | flops 20000000000 | bytes 40000000 | tf_op jit(solution)/shard_map/residual1/pallas_call | solution.py:201
  60.8 9.4 %all_to_all.34 = f32[16,2,128]{2,1,0:T(2,128)S(1)} all-to-all(f32[16,2,128]{2,1,0:T(2,128)S(1)} %bitcast.20), channel_id=1, replica_groups=mesh['slab'=8,'tile'=16] {'tile'}, dimensions={0} | all-to-all | bytes 32768 | tf_op jit(solution)/shard_map/all_to_all | solution.py:224
  70.2 1.4 %step2.1 = (f32[32,128]{1,0:T(8,128)S(1)}, f32[32,128]{1,0:T(8,128)S(1)}) custom-call(s32[168,128]{1,0:T(8,128)S(1)} %get-tuple-element.28.index, f32[32,128,128]{2,1,0:T(8,128)S(1)} %copy-done.6, f32[32,4,128,128]{3,2,1,0:T(8,128)S(1)} %bitcast.27, f32[32,128,128]{2,1,0:T(8,128)S(1)} %copy-done.5, f32[32,128]{1,0:T(8,128)S(1)} %get-tuple-element.44.t, ...), custom_call_target="tpu_custom_call" | custom-call | flops 20000000000 | bytes 40000000 | tf_op jit(solution)/shard_map/step2/pallas_call | solution.py:201
  71.7 2.4 %collective-permute-start.5 = (f32[32,128]{1,0:T(8,128)S(1)}, f32[32,128]{1,0:T(8,128)S(1)}, u32[]{:S(2)}, u32[]{:S(2)}) collective-permute-start(f32[32,128]{1,0:T(8,128)S(1)} %get-tuple-element.47.s), channel_id=1, source_target_pairs={{16,0},{32,16},{48,32},{64,48},{80,64},{96,80},{112,96},{0,112},{1... | collective-permute-start | bytes 49160 | tf_op jit(solution)/shard_map/ppermute | solution.py:229
  74.1 0.7 collective-permute-start.4
  74.8 9.2 %all_to_all.35 = f32[16,2,128]{2,1,0:T(2,128)S(1)} all-to-all(f32[16,2,128]{2,1,0:T(2,128)S(1)} %bitcast.18), channel_id=1, replica_groups=mesh['slab'=8,'tile'=16] {'tile'}, dimensions={0} | all-to-all | bytes 32768 | tf_op jit(solution)/shard_map/all_to_all | solution.py:224
  84.0 0.0 collective-permute-done.5.above
  84.0 0.0 collective-permute-done.4.below
  84.0 1.7 %last.1 = (f32[32,128]{1,0:T(8,128)}, f32[32,128]{1,0:T(8,128)}, f32[8,128]{1,0:T(8,128)}) custom-call(s32[168,128]{1,0:T(8,128)S(1)} %get-tuple-element.28.index, f32[32,128,128]{2,1,0:T(8,128)S(1)} %copy-done.6, f32[32,4,128,128]{3,2,1,0:T(8,128)S(1)} %bitcast.27, f32[8,128,128]{2,1,0:T(8,128)S(1)} %copy-done.10, f32[32,128]{1,0:T(8,128)S(1)} %get-tuple-element.47.s, ...), custom_call_target="tpu_custom_call" | custom-call | flops 20000000000 | bytes 40000000 | tf_op jit(solution)/shard_map/last/pallas_call | solution.py:201
  (2 shorter events, 0.0 us)
Async XLA Ops:
  0.6 0.9 %copy-start.4 = (s32[8]{0:T(128)S(1)}, s32[8]{0:T(128)}, u32[]{:S(2)}) copy-start(s32[8]{0:T(128)} %cell.1) | copy-start | bytes 100
  0.6 0.9 %copy-start.1 = (s32[1,16,2]{1,2,0:T(2,128)S(1)}, s32[1,16,2]{1,2,0:T(2,128)}, u32[]{:S(2)}) copy-start(s32[1,16,2]{1,2,0:T(2,128)} %param.21) | copy-start | bytes 388
  0.7 0.9 %copy-start.3 = (s32[32]{0:T(128)S(1)}, s32[32]{0:T(128)}, u32[]{:S(2)}) copy-start(s32[32]{0:T(128)} %vert.1) | copy-start | bytes 388
  0.7 0.9 %copy-start.2 = (s32[32]{0:T(128)S(1)}, s32[32]{0:T(128)}, u32[]{:S(2)}) copy-start(s32[32]{0:T(128)} %margin.1) | copy-start | bytes 388
  0.7 0.9 %copy-start = (s32[32,2]{0,1:T(2,128)S(1)}, s32[32,2]{0,1:T(2,128)}, u32[]{:S(2)}) copy-start(s32[32,2]{0,1:T(2,128)} %param.18) | copy-start | bytes 772
  0.7 1.8 %copy-start.5 = (f32[32,128,128]{2,1,0:T(8,128)S(1)}, f32[32,128,128]{2,1,0:T(8,128)}, u32[]{:S(2)}) copy-start(f32[32,128,128]{2,1,0:T(8,128)} %pre.11) | copy-start | bytes 6291460
  0.7 1.8 %copy-start.11 = (f32[32,128]{1,0:T(8,128)S(1)}, f32[32,128]{1,0:T(8,128)}, u32[]{:S(2)}) copy-start(f32[32,128]{1,0:T(8,128)} %res.1) | copy-start | bytes 49156
  0.7 19.6 %slice-start = ((s8[8388608]{0:T(1024)(128)(4,1)}), s8[4194304]{0:T(1024)(128)(4,1)S(1)}, s32[]{:S(2)}) async-start(s8[8388608]{0:T(1024)(128)(4,1)} %bitcast.26), calls=%async_computation.6 | async-start | bytes 8388608
  2.5 17.8 %slice-start.1 = ((s8[8388608]{0:T(1024)(128)(4,1)}), s8[4194304]{0:T(1024)(128)(4,1)S(1)}, s32[]{:S(2)}) async-start(s8[8388608]{0:T(1024)(128)(4,1)} %bitcast.26), calls=%async_computation.7 | async-start | bytes 8388608
  2.5 17.8 %copy-start.6 = (f32[32,128,128]{2,1,0:T(8,128)S(1)}, f32[32,128,128]{2,1,0:T(8,128)}, u32[]{:S(2)}) copy-start(f32[32,128,128]{2,1,0:T(8,128)} %diag.11) | copy-start | bytes 6291460
  2.5 17.8 %copy-start.8 = (f32[8,128,128]{2,1,0:T(8,128)S(1)}, f32[8,128,128]{2,1,0:T(8,128)}, u32[]{:S(2)}) copy-start(f32[8,128,128]{2,1,0:T(8,128)} %root_pre.5) | copy-start | bytes 1572868
  2.5 17.8 %copy-start.12 = (f32[8,128]{1,0:T(8,128)S(1)}, f32[8,128]{1,0:T(8,128)}, u32[]{:S(2)}) copy-start(f32[8,128]{1,0:T(8,128)} %rr.1) | copy-start | bytes 12292
  20.3 13.6 %copy-start.7 = (f32[8,128,128]{2,1,0:T(8,128)S(1)}, f32[8,128,128]{2,1,0:T(8,128)}, u32[]{:S(2)}) copy-start(f32[8,128,128]{2,1,0:T(8,128)} %root_diag.3) | copy-start | bytes 1572868
  20.3 13.6 %copy-start.9 = (f32[8,128,128]{2,1,0:T(8,128)S(1)}, f32[8,128,128]{2,1,0:T(8,128)}, u32[]{:S(2)}) copy-start(f32[8,128,128]{2,1,0:T(8,128)} %root_up.3) | copy-start | bytes 1572868
  20.4 13.6 %copy-start.10 = (f32[8,128,128]{2,1,0:T(8,128)S(1)}, f32[8,128,128]{2,1,0:T(8,128)}, u32[]{:S(2)}) copy-start(f32[8,128,128]{2,1,0:T(8,128)} %down.5) | copy-start | bytes 1572868
  21.9 12.0 %collective-permute-start.1 = (f32[32,128]{1,0:T(8,128)S(1)}, f32[32,128]{1,0:T(8,128)S(1)}, u32[]{:S(2)}, u32[]{:S(2)}) collective-permute-start(f32[32,128]{1,0:T(8,128)S(1)} %get-tuple-element.33.s.s_in.s_first), channel_id=1, source_target_pairs={{16,0},{32,16},{48,32},{64,48},{80,64},{96,80},{112,96},{0,112},{1... | collective-permute-start | bytes 49160 | tf_op jit(solution)/shard_map/ppermute | solution.py:229
  23.8 10.1 %collective-permute-start = (f32[32,128]{1,0:T(8,128)S(1)}, f32[32,128]{1,0:T(8,128)S(1)}, u32[]{:S(2)}, u32[]{:S(2)}) collective-permute-start(f32[32,128]{1,0:T(8,128)S(1)} %get-tuple-element.33.s.s_in.s_first), channel_id=1, source_target_pairs={{0,16},{16,32},{32,48},{48,64},{64,80},{80,96},{96,112},{112,0},{1... | collective-permute-start | bytes 49160 | tf_op jit(solution)/shard_map/ppermute | solution.py:230
  46.5 12.4 %collective-permute-start.3 = (f32[32,128]{1,0:T(8,128)S(1)}, f32[32,128]{1,0:T(8,128)S(1)}, u32[]{:S(2)}, u32[]{:S(2)}) collective-permute-start(f32[32,128]{1,0:T(8,128)S(1)} %get-tuple-element.40.s.s_in.s_before), channel_id=1, source_target_pairs={{16,0},{32,16},{48,32},{64,48},{80,64},{96,80},{112,96},{0,112},{1... | collective-permute-start | bytes 49160 | tf_op jit(solution)/shard_map/ppermute | solution.py:229
  49.0 10.0 %collective-permute-start.2 = (f32[32,128]{1,0:T(8,128)S(1)}, f32[32,128]{1,0:T(8,128)S(1)}, u32[]{:S(2)}, u32[]{:S(2)}) collective-permute-start(f32[32,128]{1,0:T(8,128)S(1)} %get-tuple-element.40.s.s_in.s_before), channel_id=1, source_target_pairs={{0,16},{16,32},{32,48},{48,64},{64,80},{80,96},{96,112},{112,0},{1... | collective-permute-start | bytes 49160 | tf_op jit(solution)/shard_map/ppermute | solution.py:230
  71.7 12.3 %collective-permute-start.5 = (f32[32,128]{1,0:T(8,128)S(1)}, f32[32,128]{1,0:T(8,128)S(1)}, u32[]{:S(2)}, u32[]{:S(2)}) collective-permute-start(f32[32,128]{1,0:T(8,128)S(1)} %get-tuple-element.47.s), channel_id=1, source_target_pairs={{16,0},{32,16},{48,32},{64,48},{80,64},{96,80},{112,96},{0,112},{1... | collective-permute-start | bytes 49160 | tf_op jit(solution)/shard_map/ppermute | solution.py:229
  74.1 9.9 %collective-permute-start.4 = (f32[32,128]{1,0:T(8,128)S(1)}, f32[32,128]{1,0:T(8,128)S(1)}, u32[]{:S(2)}, u32[]{:S(2)}) collective-permute-start(f32[32,128]{1,0:T(8,128)S(1)} %get-tuple-element.47.s), channel_id=1, source_target_pairs={{0,16},{16,32},{32,48},{48,64},{64,80},{80,96},{96,112},{112,0},{1... | collective-permute-start | bytes 49160 | tf_op jit(solution)/shard_map/ppermute | solution.py:230

commit v5 on v4

--- a/solution.py
+++ b/solution.py
@@ -20,11 +20,11 @@
 TILES = 16
 CAP = 2
 SLOTS = TILES * CAP
-PIECE = NBD + 8
+PIECE = NBD + CAP
 F32 = jnp.float32
 OWN, MARGIN, VERT, WIDE, CELL = 0, 2 * NBD, 3 * NBD, 4 * NBD, 5 * NBD
 ENTRIES = CELL + RCAP
-LAG = 6
+LAG = 8
 
 VMEM = pl.BlockSpec(memory_space=pltpu.VMEM)
 SMEM = pl.BlockSpec(memory_space=pltpu.SMEM)
@@ -90,8 +90,8 @@
         t_out[g : g + 1, :] = product((pre[g], at(rhs, g)))
     t = t_out[...]
     for p in range(TILES):
-        send[p, :NBD, :] = t
-        send[p, NBD : NBD + CAP, :] = wish[CAP * p : CAP * (p + 1), :]
+        send[PIECE * p : PIECE * p + NBD, :] = t
+        send[PIECE * p + NBD : PIECE * (p + 1), :] = wish[CAP * p : CAP * (p + 1), :]
 
 
 def staggered(first, second):
@@ -221,8 +221,8 @@
     soil, root, table = (NBD, B), (RCAP, B), (SLOTS, B)
 
     def exchange(rows):
-        got = lax.all_to_all(rows.reshape(TILES, CAP, B), "tile", 0, 0)
-        return got.reshape(SLOTS, B)
+        pieces = rows.reshape(TILES, -1, CAP, B)
+        return lax.all_to_all(pieces, "tile", 0, 0).reshape(rows.shape)
 
     def vertical(s):
         up = [(i, (i + 1) % slabs) for i in range(slabs)]
@@ -237,9 +237,9 @@
         (anchor,), (entries, table, root), work=1000,
     )
     t, send = call(
-        first_kernel, "first", (), (wish, soil_pre, soil_rhs), (soil, (TILES, PIECE, B))
-    )
-    got = lax.all_to_all(send, "tile", 0, 0).reshape(TILES * PIECE, B)
+        first_kernel, "first", (), (wish, soil_pre, soil_rhs), (soil, (TILES * PIECE, B))
+    )
+    got = exchange(send)
     s, send, asked, ur = call(
         first_step_kernel, "step0", (),
         (index, live, soil_diag, soil_off, soil_pre, t, got, soil_rhs, root_pre, root_rhs),

time: 86 us -> 85.5 us (level)
  no operation moved by 1% of the time
where the time goes in v5:
time: 85.5 us; the launch traced here: 85.1 us
  blocking collectives  62.7 us (73%)
  Pallas kernels  11.3 us (13%)
  starting transfers between devices  9.38 us (11%)
  between operations  1.7 us (2%)
    all_to_all x6, blocking collectives, exchange(): return lax.all_to_all(pieces, 'tile', 0, 0).reshape(rows.shape)  62.7 us
    pallas_call x9, Pallas kernels, call(): pl.pallas_call(kernel, out_shape=tuple(shapes), in_specs=[SMEM] * len(sca...  11.3 us
    ppermute x3, starting transfers between devices, vertical(): above = lax.ppermute(s, 'slab', [(j, i) for i, j in up])  7.01 us
    ppermute x3, starting transfers between devices, vertical(): return (lax.ppermute(s, 'slab', up), above)  2.37 us
  transfers between devices with their start and end apart: 6, of which 0 were waited for; matrix products, arithmetic and copies ran while one was open for 0% of the time, Pallas kernels for 0%

profile of v5, /device:TPU:1, one launch (start us, length us, event | category | flops | bytes accessed | tf_op | source)
XLA Modules:
  0.0 85.1 jit_solution(1379226882489018144)
XLA Ops:
  0.6 0.0 copy-start.4
  0.6 0.0 copy-start.1
  0.7 0.0 copy-start.3
  0.7 0.0 copy-start.2
  0.7 0.0 copy-start
  0.7 0.0 copy-start.5
  0.7 0.0 copy-start.11
  0.7 0.0 slice-start
  1.5 0.0 copy-done.4
  1.5 0.0 copy-done.1
  1.5 0.0 copy-done.3
  1.6 0.0 copy-done.2
  1.6 0.0 copy-done
  1.6 0.9 %lists.1 = (s32[168,128]{1,0:T(8,128)S(1)}, f32[32,128]{1,0:T(8,128)S(1)}, f32[8,128]{1,0:T(8,128)S(1)}) custom-call(s32[2,32]{1,0:T(2,128)S(1)} %bitcast.36, s32[32]{0:T(128)S(1)} %copy-done.2, s32[32]{0:T(128)S(1)} %copy-done.3, s32[8]{0:T(128)S(1)} %copy-done.4, s32[1,2,16]{2,1,0:T(2,128)S(1)} %bitcast.37, s32[1]{0:T(128)S(6)} %copy.23.count, ...), custom_call_target="tpu_custom_call" | custom-call | flops 1000 | bytes 2 | tf_op jit(solution)/shard_map/lists/pallas_call | solution.py:201
  2.4 0.0 copy-done.5
  2.5 0.0 copy-done.11
  2.5 0.0 slice-start.1
  2.5 0.0 copy-start.6
  2.5 0.0 copy-start.8
  2.5 0.0 copy-start.12
  2.5 0.6 first.1
  3.2 16.4 %all_to_all.30 = f32[16,17,2,128]{3,2,1,0:T(2,128)S(1)} all-to-all(f32[16,17,2,128]{3,2,1,0:T(2,128)S(1)} %bitcast.25), channel_id=1, replica_groups=mesh['slab'=8,'tile'=16] {'tile'}, dimensions={0} | all-to-all | bytes 557056 | tf_op jit(solution)/shard_map/all_to_all | solution.py:225
  19.5 0.0 slice-done
  19.5 0.0 slice-done.1
  19.5 0.0 copy-done.6
  19.5 0.0 copy-done.8
  19.6 0.0 copy-done.12
  19.6 0.0 copy-start.7
  19.6 0.0 copy-start.9
  19.6 0.0 copy-start.10
  19.6 1.5 %step0.1 = (f32[32,128]{1,0:T(8,128)S(1)}, f32[32,128]{1,0:T(8,128)S(1)}, s32[32,128]{1,0:T(8,128)S(1)}, f32[8,128]{1,0:T(8,128)S(1)}) custom-call(s32[168,128]{1,0:T(8,128)S(1)} %get-tuple-element.28.index, f32[8,128]{1,0:T(8,128)S(1)} %get-tuple-element.29.live, f32[32,128,128]{2,1,0:T(8,128)S(1)} %copy-done.6, f32[32,4,128,128]{3,2,1,0:T(8,128)S(1)} %bitcast.39, ...), custom_call_target="tpu_custom_call" | custom-call | flops 20000000000 | bytes 40000000 | tf_op jit(solution)/shard_map/step0/pallas_call | solution.py:201
  21.1 2.1 %collective-permute-start.1 = (f32[32,128]{1,0:T(8,128)S(1)}, f32[32,128]{1,0:T(8,128)S(1)}, u32[]{:S(2)}, u32[]{:S(2)}) collective-permute-start(f32[32,128]{1,0:T(8,128)S(1)} %get-tuple-element.33.s.s_in.s_first), channel_id=1, source_target_pairs={{16,0},{32,16},{48,32},{64,48},{80,64},{96,80},{112,96},{0,112},{1... | collective-permute-start | bytes 49160 | tf_op jit(solution)/shard_map/ppermute | solution.py:229
  23.3 1.1 %collective-permute-start = (f32[32,128]{1,0:T(8,128)S(1)}, f32[32,128]{1,0:T(8,128)S(1)}, u32[]{:S(2)}, u32[]{:S(2)}) collective-permute-start(f32[32,128]{1,0:T(8,128)S(1)} %get-tuple-element.33.s.s_in.s_first), channel_id=1, source_target_pairs={{0,16},{16,32},{32,48},{48,64},{64,80},{80,96},{96,112},{112,0},{1... | collective-permute-start | bytes 49160 | tf_op jit(solution)/shard_map/ppermute | solution.py:230
  24.4 9.0 %all_to_all.31 = f32[16,1,2,128]{3,2,1,0:T(2,128)S(1)} all-to-all(f32[16,1,2,128]{3,2,1,0:T(2,128)S(1)} %bitcast.29), channel_id=1, replica_groups=mesh['slab'=8,'tile'=16] {'tile'}, dimensions={0} | all-to-all | bytes 32768 | tf_op jit(solution)/shard_map/all_to_all | solution.py:225
  33.4 0.0 collective-permute-done.1.above
  33.4 0.0 collective-permute-done.below
  33.4 0.0 copy-done.7
  33.4 0.0 copy-done.9
  33.4 0.0 copy-done.10
  33.4 1.9 %residual0.1 = (f32[32,128]{1,0:T(8,128)S(1)}, f32[32,128]{1,0:T(8,128)S(1)}, f32[8,128]{1,0:T(8,128)S(1)}, f32[32,128]{1,0:T(8,128)S(1)}, f32[8,128]{1,0:T(8,128)S(1)}) custom-call(s32[168,128]{1,0:T(8,128)S(1)} %get-tuple-element.28.index, f32[32,128,128]{2,1,0:T(8,128)S(1)} %copy-done.6, f32[32,4,128,128]{3,2,1,0:T(8,128)S(1)} %bitcast.39, ...), custom_call_target="tpu_custom_call" | custom-call | flops 20000000000 | bytes 40000000 | tf_op jit(solution)/shard_map/residual0/pallas_call | solution.py:201
  35.3 9.5 %all_to_all.32 = f32[16,1,2,128]{3,2,1,0:T(2,128)S(1)} all-to-all(f32[16,1,2,128]{3,2,1,0:T(2,128)S(1)} %bitcast.33), channel_id=1, replica_groups=mesh['slab'=8,'tile'=16] {'tile'}, dimensions={0} | all-to-all | bytes 32768 | tf_op jit(solution)/shard_map/all_to_all | solution.py:225
  44.8 1.4 %step1.1 = (f32[32,128]{1,0:T(8,128)S(1)}, f32[32,128]{1,0:T(8,128)S(1)}) custom-call(s32[168,128]{1,0:T(8,128)S(1)} %get-tuple-element.28.index, f32[32,128,128]{2,1,0:T(8,128)S(1)} %copy-done.6, f32[32,4,128,128]{3,2,1,0:T(8,128)S(1)} %bitcast.39, f32[32,128,128]{2,1,0:T(8,128)S(1)} %copy-done.5, f32[32,128]{1,0:T(8,128)S(1)} %get-tuple-element.37.t, ...), custom_call_target="tpu_custom_call" | custom-call | flops 20000000000 | bytes 40000000 | tf_op jit(solution)/shard_map/step1/pallas_call | solution.py:201
  46.2 2.5 %collective-permute-start.3 = (f32[32,128]{1,0:T(8,128)S(1)}, f32[32,128]{1,0:T(8,128)S(1)}, u32[]{:S(2)}, u32[]{:S(2)}) collective-permute-start(f32[32,128]{1,0:T(8,128)S(1)} %get-tuple-element.40.s.s_in.s_before), channel_id=1, source_target_pairs={{16,0},{32,16},{48,32},{64,48},{80,64},{96,80},{112,96},{0,112},{1... | collective-permute-start | bytes 49160 | tf_op jit(solution)/shard_map/ppermute | solution.py:229
  48.7 0.6 collective-permute-start.2
  49.3 9.2 %all_to_all.33 = f32[16,1,2,128]{3,2,1,0:T(2,128)S(1)} all-to-all(f32[16,1,2,128]{3,2,1,0:T(2,128)S(1)} %bitcast.31), channel_id=1, replica_groups=mesh['slab'=8,'tile'=16] {'tile'}, dimensions={0} | all-to-all | bytes 32768 | tf_op jit(solution)/shard_map/all_to_all | solution.py:225
  58.4 0.0 collective-permute-done.3.above
  58.4 0.0 collective-permute-done.2.below
  58.4 1.9 %residual1.1 = (f32[32,128]{1,0:T(8,128)S(1)}, f32[32,128]{1,0:T(8,128)S(1)}, f32[8,128]{1,0:T(8,128)S(1)}, f32[32,128]{1,0:T(8,128)S(1)}) custom-call(s32[168,128]{1,0:T(8,128)S(1)} %get-tuple-element.28.index, f32[32,128,128]{2,1,0:T(8,128)S(1)} %copy-done.6, f32[32,4,128,128]{3,2,1,0:T(8,128)S(1)} %bitcast.39, f32[32,128,128]{2,1,0:T(8,128)S(1)} %copy-done.5, ...), custom_call_target="tpu_custom_call" | custom-call | flops 20000000000 | bytes 40000000 | tf_op jit(solution)/shard_map/residual1/pallas_call | solution.py:201
  60.3 9.5 %all_to_all.34 = f32[16,1,2,128]{3,2,1,0:T(2,128)S(1)} all-to-all(f32[16,1,2,128]{3,2,1,0:T(2,128)S(1)} %bitcast.32), channel_id=1, replica_groups=mesh['slab'=8,'tile'=16] {'tile'}, dimensions={0} | all-to-all | bytes 32768 | tf_op jit(solution)/shard_map/all_to_all | solution.py:225
  69.8 1.4 %step2.1 = (f32[32,128]{1,0:T(8,128)S(1)}, f32[32,128]{1,0:T(8,128)S(1)}) custom-call(s32[168,128]{1,0:T(8,128)S(1)} %get-tuple-element.28.index, f32[32,128,128]{2,1,0:T(8,128)S(1)} %copy-done.6, f32[32,4,128,128]{3,2,1,0:T(8,128)S(1)} %bitcast.39, f32[32,128,128]{2,1,0:T(8,128)S(1)} %copy-done.5, f32[32,128]{1,0:T(8,128)S(1)} %get-tuple-element.44.t, ...), custom_call_target="tpu_custom_call" | custom-call | flops 20000000000 | bytes 40000000 | tf_op jit(solution)/shard_map/step2/pallas_call | solution.py:201
  71.2 2.5 %collective-permute-start.5 = (f32[32,128]{1,0:T(8,128)S(1)}, f32[32,128]{1,0:T(8,128)S(1)}, u32[]{:S(2)}, u32[]{:S(2)}) collective-permute-start(f32[32,128]{1,0:T(8,128)S(1)} %get-tuple-element.47.s), channel_id=1, source_target_pairs={{16,0},{32,16},{48,32},{64,48},{80,64},{96,80},{112,96},{0,112},{1... | collective-permute-start | bytes 49160 | tf_op jit(solution)/shard_map/ppermute | solution.py:229
  73.7 0.6 collective-permute-start.4
  74.3 9.2 %all_to_all.35 = f32[16,1,2,128]{3,2,1,0:T(2,128)S(1)} all-to-all(f32[16,1,2,128]{3,2,1,0:T(2,128)S(1)} %bitcast.30), channel_id=1, replica_groups=mesh['slab'=8,'tile'=16] {'tile'}, dimensions={0} | all-to-all | bytes 32768 | tf_op jit(solution)/shard_map/all_to_all | solution.py:225
  83.5 0.0 collective-permute-done.5.above
  83.5 0.0 collective-permute-done.4.below
  83.5 1.7 %last.1 = (f32[32,128]{1,0:T(8,128)}, f32[32,128]{1,0:T(8,128)}, f32[8,128]{1,0:T(8,128)}) custom-call(s32[168,128]{1,0:T(8,128)S(1)} %get-tuple-element.28.index, f32[32,128,128]{2,1,0:T(8,128)S(1)} %copy-done.6, f32[32,4,128,128]{3,2,1,0:T(8,128)S(1)} %bitcast.39, f32[8,128,128]{2,1,0:T(8,128)S(1)} %copy-done.10, f32[32,128]{1,0:T(8,128)S(1)} %get-tuple-element.47.s, ...), custom_call_target="tpu_custom_call" | custom-call | flops 20000000000 | bytes 40000000 | tf_op jit(solution)/shard_map/last/pallas_call | solution.py:201
  (2 shorter events, 0.0 us)
Async XLA Ops:
  0.6 0.9 %copy-start.4 = (s32[8]{0:T(128)S(1)}, s32[8]{0:T(128)}, u32[]{:S(2)}) copy-start(s32[8]{0:T(128)} %cell.1) | copy-start | bytes 100
  0.6 0.9 %copy-start.1 = (s32[1,16,2]{1,2,0:T(2,128)S(1)}, s32[1,16,2]{1,2,0:T(2,128)}, u32[]{:S(2)}) copy-start(s32[1,16,2]{1,2,0:T(2,128)} %param.21) | copy-start | bytes 388
  0.7 0.9 %copy-start.3 = (s32[32]{0:T(128)S(1)}, s32[32]{0:T(128)}, u32[]{:S(2)}) copy-start(s32[32]{0:T(128)} %vert.1) | copy-start | bytes 388
  0.7 0.9 %copy-start.2 = (s32[32]{0:T(128)S(1)}, s32[32]{0:T(128)}, u32[]{:S(2)}) copy-start(s32[32]{0:T(128)} %margin.1) | copy-start | bytes 388
  0.7 0.9 %copy-start = (s32[32,2]{0,1:T(2,128)S(1)}, s32[32,2]{0,1:T(2,128)}, u32[]{:S(2)}) copy-start(s32[32,2]{0,1:T(2,128)} %param.18) | copy-start | bytes 772
  0.7 1.8 %copy-start.5 = (f32[32,128,128]{2,1,0:T(8,128)S(1)}, f32[32,128,128]{2,1,0:T(8,128)}, u32[]{:S(2)}) copy-start(f32[32,128,128]{2,1,0:T(8,128)} %pre.11) | copy-start | bytes 6291460
  0.7 1.8 %copy-start.11 = (f32[32,128]{1,0:T(8,128)S(1)}, f32[32,128]{1,0:T(8,128)}, u32[]{:S(2)}) copy-start(f32[32,128]{1,0:T(8,128)} %res.1) | copy-start | bytes 49156
  0.7 18.8 %slice-start = ((s8[8388608]{0:T(1024)(128)(4,1)}), s8[4194304]{0:T(1024)(128)(4,1)S(1)}, s32[]{:S(2)}) async-start(s8[8388608]{0:T(1024)(128)(4,1)} %bitcast.38), calls=%async_computation.6 | async-start | bytes 8388608
  2.5 17.1 %slice-start.1 = ((s8[8388608]{0:T(1024)(128)(4,1)}), s8[4194304]{0:T(1024)(128)(4,1)S(1)}, s32[]{:S(2)}) async-start(s8[8388608]{0:T(1024)(128)(4,1)} %bitcast.38), calls=%async_computation.7 | async-start | bytes 8388608
  2.5 17.1 %copy-start.6 = (f32[32,128,128]{2,1,0:T(8,128)S(1)}, f32[32,128,128]{2,1,0:T(8,128)}, u32[]{:S(2)}) copy-start(f32[32,128,128]{2,1,0:T(8,128)} %diag.11) | copy-start | bytes 6291460
  2.5 17.1 %copy-start.8 = (f32[8,128,128]{2,1,0:T(8,128)S(1)}, f32[8,128,128]{2,1,0:T(8,128)}, u32[]{:S(2)}) copy-start(f32[8,128,128]{2,1,0:T(8,128)} %root_pre.5) | copy-start | bytes 1572868
  2.5 17.1 %copy-start.12 = (f32[8,128]{1,0:T(8,128)S(1)}, f32[8,128]{1,0:T(8,128)}, u32[]{:S(2)}) copy-start(f32[8,128]{1,0:T(8,128)} %rr.1) | copy-start | bytes 12292
  19.6 13.8 %copy-start.7 = (f32[8,128,128]{2,1,0:T(8,128)S(1)}, f32[8,128,128]{2,1,0:T(8,128)}, u32[]{:S(2)}) copy-start(f32[8,128,128]{2,1,0:T(8,128)} %root_diag.3) | copy-start | bytes 1572868
  19.6 13.8 %copy-start.9 = (f32[8,128,128]{2,1,0:T(8,128)S(1)}, f32[8,128,128]{2,1,0:T(8,128)}, u32[]{:S(2)}) copy-start(f32[8,128,128]{2,1,0:T(8,128)} %root_up.3) | copy-start | bytes 1572868
  19.6 13.8 %copy-start.10 = (f32[8,128,128]{2,1,0:T(8,128)S(1)}, f32[8,128,128]{2,1,0:T(8,128)}, u32[]{:S(2)}) copy-start(f32[8,128,128]{2,1,0:T(8,128)} %down.5) | copy-start | bytes 1572868
  21.1 12.2 %collective-permute-start.1 = (f32[32,128]{1,0:T(8,128)S(1)}, f32[32,128]{1,0:T(8,128)S(1)}, u32[]{:S(2)}, u32[]{:S(2)}) collective-permute-start(f32[32,128]{1,0:T(8,128)S(1)} %get-tuple-element.33.s.s_in.s_first), channel_id=1, source_target_pairs={{16,0},{32,16},{48,32},{64,48},{80,64},{96,80},{112,96},{0,112},{1... | collective-permute-start | bytes 49160 | tf_op jit(solution)/shard_map/ppermute | solution.py:229
  23.3 10.1 %collective-permute-start = (f32[32,128]{1,0:T(8,128)S(1)}, f32[32,128]{1,0:T(8,128)S(1)}, u32[]{:S(2)}, u32[]{:S(2)}) collective-permute-start(f32[32,128]{1,0:T(8,128)S(1)} %get-tuple-element.33.s.s_in.s_first), channel_id=1, source_target_pairs={{0,16},{16,32},{32,48},{48,64},{64,80},{80,96},{96,112},{112,0},{1... | collective-permute-start | bytes 49160 | tf_op jit(solution)/shard_map/ppermute | solution.py:230
  46.2 12.2 %collective-permute-start.3 = (f32[32,128]{1,0:T(8,128)S(1)}, f32[32,128]{1,0:T(8,128)S(1)}, u32[]{:S(2)}, u32[]{:S(2)}) collective-permute-start(f32[32,128]{1,0:T(8,128)S(1)} %get-tuple-element.40.s.s_in.s_before), channel_id=1, source_target_pairs={{16,0},{32,16},{48,32},{64,48},{80,64},{96,80},{112,96},{0,112},{1... | collective-permute-start | bytes 49160 | tf_op jit(solution)/shard_map/ppermute | solution.py:229
  48.7 9.8 %collective-permute-start.2 = (f32[32,128]{1,0:T(8,128)S(1)}, f32[32,128]{1,0:T(8,128)S(1)}, u32[]{:S(2)}, u32[]{:S(2)}) collective-permute-start(f32[32,128]{1,0:T(8,128)S(1)} %get-tuple-element.40.s.s_in.s_before), channel_id=1, source_target_pairs={{0,16},{16,32},{32,48},{48,64},{64,80},{80,96},{96,112},{112,0},{1... | collective-permute-start | bytes 49160 | tf_op jit(solution)/shard_map/ppermute | solution.py:230
  71.2 12.2 %collective-permute-start.5 = (f32[32,128]{1,0:T(8,128)S(1)}, f32[32,128]{1,0:T(8,128)S(1)}, u32[]{:S(2)}, u32[]{:S(2)}) collective-permute-start(f32[32,128]{1,0:T(8,128)S(1)} %get-tuple-element.47.s), channel_id=1, source_target_pairs={{16,0},{32,16},{48,32},{64,48},{80,64},{96,80},{112,96},{0,112},{1... | collective-permute-start | bytes 49160 | tf_op jit(solution)/shard_map/ppermute | solution.py:229
  73.7 9.8 %collective-permute-start.4 = (f32[32,128]{1,0:T(8,128)S(1)}, f32[32,128]{1,0:T(8,128)S(1)}, u32[]{:S(2)}, u32[]{:S(2)}) collective-permute-start(f32[32,128]{1,0:T(8,128)S(1)} %get-tuple-element.47.s), channel_id=1, source_target_pairs={{0,16},{16,32},{32,48},{48,64},{64,80},{80,96},{96,112},{112,0},{1... | collective-permute-start | bytes 49160 | tf_op jit(solution)/shard_map/ppermute | solution.py:230

commit v6 on v5

--- a/solution.py
+++ b/solution.py
@@ -25,28 +25,45 @@
 OWN, MARGIN, VERT, WIDE, CELL = 0, 2 * NBD, 3 * NBD, 4 * NBD, 5 * NBD
 ENTRIES = CELL + RCAP
 LAG = 8
+AHEAD = 4
 
 VMEM = pl.BlockSpec(memory_space=pltpu.VMEM)
 SMEM = pl.BlockSpec(memory_space=pltpu.SMEM)
 
 
-def row_sum(acc):
+def diagonal(rows):
     lane = lax.broadcasted_iota(jnp.int32, (8, B), 1)
     sub = lax.broadcasted_iota(jnp.int32, (8, B), 0)
-    ahead = lane - sub
+    bit = 8
+    while len(rows) > 1:
+        high = (lane & bit) != 0
+        rows = [jnp.where(high, b, a) for a, b in zip(rows[::2], rows[1::2])]
+        bit *= 2
+    return jnp.sum(jnp.where((lane & 7) == sub, rows[0], 0.0), axis=0, keepdims=True)
+
+
+def lane_sums(acc):
     sums = jnp.sum(acc.reshape(B // 8, 8, B), axis=2, keepdims=True)
-    out = jnp.zeros((8, B), F32)
-    for k in range(B // 8):
-        out = jnp.where(ahead == 8 * k, sums[k], out)
-    return jnp.sum(out, axis=0, keepdims=True)
-
-
-def product(*pairs):
+    return diagonal([jnp.broadcast_to(sums[k], (8, B)) for k in range(B // 8)])
+
+
+def matrix_sums(acc):
+    high = acc.astype(jnp.bfloat16)
+    low = (acc - high.astype(F32)).astype(jnp.bfloat16)
+    sums = jnp.dot(
+        jnp.concatenate([high, low], axis=1),
+        jnp.ones((2 * B, B), jnp.bfloat16),
+        preferred_element_type=F32,
+    )
+    return diagonal([sums[8 * k : 8 * k + 8] for k in range(B // 8)])
+
+
+def product(*pairs, sums=lane_sums):
     acc = None
     for mat, vec in pairs:
         term = mat * vec
         acc = term if acc is None else acc + term
-    return row_sum(acc)
+    return sums(acc)
 
 
 def row(ref, index):
@@ -87,34 +104,42 @@
 
 def first_kernel(wish, pre, rhs, t_out, send):
     for g in range(NBD):
-        t_out[g : g + 1, :] = product((pre[g], at(rhs, g)))
+        t_out[g : g + 1, :] = product(
+            (pre[g], at(rhs, g)), sums=matrix_sums if g % 2 else lane_sums
+        )
     t = t_out[...]
     for p in range(TILES):
         send[PIECE * p : PIECE * p + NBD, :] = t
         send[PIECE * p + NBD : PIECE * (p + 1), :] = wish[CAP * p : CAP * (p + 1), :]
 
 
-def staggered(first, second):
-    for g in range(NBD + LAG):
-        if g < NBD:
-            first(g)
+def staggered(fetch_row, first, second):
+    held = {}
+    for g in range(-AHEAD, NBD + LAG):
+        if g + AHEAD < NBD:
+            held[g + AHEAD] = fetch_row(g + AHEAD)
+        if 0 <= g < NBD:
+            first(g, held.pop(g))
         if g >= LAG:
             second(g - LAG)
 
 
 def step_rows(index, near, near_at, diag, off, pre, t, res, w, finish):
-    def extended(g):
+    def rows_of(g):
+        return index[OWN + g, 0], index[OWN + NBD + g, 0], index[near_at + g, 0]
+
+    def extended(g, at_rows):
         w[g : g + 1, :] = at(res, g) - product(
             (diag[g], at(t, g)),
-            (off[g, 0], row(t, index[OWN + g, 0])),
-            (off[g, 1], row(t, index[OWN + NBD + g, 0])),
-            (off[g, 2], row(near, index[near_at + g, 0])),
+            (off[g, 0], row(t, at_rows[0])),
+            (off[g, 1], row(t, at_rows[1])),
+            (off[g, 2], row(near, at_rows[2])),
         )
 
     def turn(g):
         finish(g, at(t, g) + product((pre[g], at(w, g))))
 
-    staggered(extended, turn)
+    staggered(rows_of, extended, turn)
 
 
 def first_step_kernel(
@@ -131,7 +156,7 @@
 
     step_rows(index, table, WIDE, diag, off, pre, t, rhs, w, finish)
     for r in range(RCAP):
-        z = product((root_pre[r], at(root_rhs, r)))
+        z = product((root_pre[r], at(root_rhs, r)), sums=matrix_sums)
         ur_out[r : r + 1, :] = jnp.where(at(live, r) > 0.0, z * (1.0 / THETA), 0.0)
     send_rows(asked, s_out, send)
 
@@ -148,20 +173,25 @@
     r_out[...] = res[...]
     for r in range(RCAP):
         spot = pl.ds(index[CELL + r, 0], 1)
-        r_out[spot, :] = r_out[spot, :] - product((down[r], at(ur, r)))
-
-    def applied(g):
-        vert = index[VERT + g, 0]
+        r_out[spot, :] = r_out[spot, :] - product((down[r], at(ur, r)), sums=matrix_sums if after else lane_sums)
+
+    def rows_of(g):
+        return (
+            index[OWN + g, 0], index[OWN + NBD + g, 0], index[MARGIN + g, 0], index[VERT + g, 0]
+        )
+
+    def applied(g, at_rows):
+        vert = at_rows[3]
         over = jnp.where(vert < NBD, row(below, vert % NBD), row(above, vert % NBD))
         r_out[g : g + 1, :] = at(r_out, g) - product(
             (diag[g], at(s, g)),
-            (off[g, 0], row(s, index[OWN + g, 0])),
-            (off[g, 1], row(s, index[OWN + NBD + g, 0])),
-            (off[g, 2], row(table, index[MARGIN + g, 0])),
+            (off[g, 0], row(s, at_rows[0])),
+            (off[g, 1], row(s, at_rows[1])),
+            (off[g, 2], row(table, at_rows[2])),
             (off[g, 3], over),
         )
 
-    staggered(applied, after or (lambda g: None))
+    staggered(rows_of, applied, after or (lambda g: None))
 
 
 def residual_kernel(
@@ -169,21 +199,27 @@
     s, table, below, above, res, ur, rr, live, asked,
     t_out, r_out, ur_out, send, rr_out,
 ):
-    for r in range(RCAP):
+    def change_root(r):
         change = product(
-            (root_diag[r], at(ur, r)), (root_up[r], row(s, index[CELL + r, 0]))
+            (root_diag[r], at(ur, r)), (root_up[r], row(s, index[CELL + r, 0])),
+            sums=matrix_sums,
         )
         rr_out[r : r + 1, :] = at(rr, r) - change
+
+    def turn_root(r):
+        z = product((root_pre[r], at(rr_out, r)), sums=matrix_sums)
+        ur_out[r : r + 1, :] = jnp.where(
+            at(live, r) > 0.0, keep * at(ur, r) + gain * z, 0.0
+        )
 
     def turn(g):
         t_out[g : g + 1, :] = product((pre[g], at(r_out, g)))
+        if g % 2 == 0 and g < 2 * RCAP:
+            change_root(g // 2)
+        if g % 2 == 0 and g >= 2 * RCAP:
+            turn_root(g // 2 - RCAP)
 
     residual_rows(index, diag, off, down, s, table, below, above, res, ur, r_out, turn)
-    for r in range(RCAP):
-        z = product((root_pre[r], at(rr_out, r)))
-        ur_out[r : r + 1, :] = jnp.where(
-            at(live, r) > 0.0, keep * at(ur, r) + gain * z, 0.0
-        )
     send_rows(asked, t_out, send)
 
 

time: 85.5 us -> 85.1 us (level)
  no operation moved by 1% of the time
where the time goes in v6:
time: 85.1 us; the launch traced here: 84.8 us
  blocking collectives  62.6 us (74%)
  Pallas kernels  10.9 us (13%)
  starting transfers between devices  9.39 us (11%)
  between operations  1.7 us (2%)
    all_to_all x6, blocking collectives, exchange(): return lax.all_to_all(pieces, 'tile', 0, 0).reshape(rows.shape)  62.6 us
    pallas_call x9, Pallas kernels, call(): pl.pallas_call(kernel, out_shape=tuple(shapes), in_specs=[SMEM] * len(sca...  10.9 us
    ppermute x3, starting transfers between devices, vertical(): above = lax.ppermute(s, 'slab', [(j, i) for i, j in up])  7.01 us
    ppermute x3, starting transfers between devices, vertical(): return (lax.ppermute(s, 'slab', up), above)  2.38 us
  transfers between devices with their start and end apart: 6, of which 0 were waited for; matrix products, arithmetic and copies ran while one was open for 0% of the time, Pallas kernels for 0%

profile of v6, /device:TPU:1, one launch (start us, length us, event | category | flops | bytes accessed | tf_op | source)
XLA Modules:
  0.0 84.8 jit_solution(7207847011225942882)
XLA Ops:
  0.6 0.0 copy-start.4
  0.6 0.0 copy-start.1
  0.7 0.0 copy-start.3
  0.7 0.0 copy-start.2
  0.7 0.0 copy-start
  0.7 0.0 copy-start.5
  0.7 0.0 copy-start.11
  0.7 0.0 slice-start
  1.5 0.0 copy-done.4
  1.5 0.0 copy-done.1
  1.5 0.0 copy-done.3
  1.6 0.0 copy-done.2
  1.6 0.0 copy-done
  1.6 0.9 %lists.1 = (s32[168,128]{1,0:T(8,128)S(1)}, f32[32,128]{1,0:T(8,128)S(1)}, f32[8,128]{1,0:T(8,128)S(1)}) custom-call(s32[2,32]{1,0:T(2,128)S(1)} %bitcast.36, s32[32]{0:T(128)S(1)} %copy-done.2, s32[32]{0:T(128)S(1)} %copy-done.3, s32[8]{0:T(128)S(1)} %copy-done.4, s32[1,2,16]{2,1,0:T(2,128)S(1)} %bitcast.37, s32[1]{0:T(128)S(6)} %copy.23.count, ...), custom_call_target="tpu_custom_call" | custom-call | flops 1000 | bytes 2 | tf_op jit(solution)/shard_map/lists/pallas_call | solution.py:237
  2.4 0.0 copy-done.5
  2.5 0.0 copy-done.11
  2.5 0.0 slice-start.1
  2.5 0.0 copy-start.6
  2.5 0.0 copy-start.8
  2.5 0.0 copy-start.12
  2.5 0.5 first.1
  3.0 16.4 %all_to_all.30 = f32[16,17,2,128]{3,2,1,0:T(2,128)S(1)} all-to-all(f32[16,17,2,128]{3,2,1,0:T(2,128)S(1)} %bitcast.25), channel_id=1, replica_groups=mesh['slab'=8,'tile'=16] {'tile'}, dimensions={0} | all-to-all | bytes 557056 | tf_op jit(solution)/shard_map/all_to_all | solution.py:261
  19.4 0.0 slice-done
  19.4 0.0 slice-done.1
  19.4 0.0 copy-done.6
  19.4 0.0 copy-done.8
  19.4 0.0 copy-done.12
  19.4 0.0 copy-start.7
  19.4 0.0 copy-start.9
  19.5 0.0 copy-start.10
  19.5 1.4 %step0.1 = (f32[32,128]{1,0:T(8,128)S(1)}, f32[32,128]{1,0:T(8,128)S(1)}, s32[32,128]{1,0:T(8,128)S(1)}, f32[8,128]{1,0:T(8,128)S(1)}) custom-call(s32[168,128]{1,0:T(8,128)S(1)} %get-tuple-element.28.index, f32[8,128]{1,0:T(8,128)S(1)} %get-tuple-element.29.live, f32[32,128,128]{2,1,0:T(8,128)S(1)} %copy-done.6, f32[32,4,128,128]{3,2,1,0:T(8,128)S(1)} %bitcast.39, ...), custom_call_target="tpu_custom_call" | custom-call | flops 20000000000 | bytes 40000000 | tf_op jit(solution)/shard_map/step0/pallas_call | solution.py:237
  20.9 2.1 %collective-permute-start.1 = (f32[32,128]{1,0:T(8,128)S(1)}, f32[32,128]{1,0:T(8,128)S(1)}, u32[]{:S(2)}, u32[]{:S(2)}) collective-permute-start(f32[32,128]{1,0:T(8,128)S(1)} %get-tuple-element.33.s.s_in.s_first), channel_id=1, source_target_pairs={{16,0},{32,16},{48,32},{64,48},{80,64},{96,80},{112,96},{0,112},{1... | collective-permute-start | bytes 49160 | tf_op jit(solution)/shard_map/ppermute | solution.py:265
  23.0 1.1 %collective-permute-start = (f32[32,128]{1,0:T(8,128)S(1)}, f32[32,128]{1,0:T(8,128)S(1)}, u32[]{:S(2)}, u32[]{:S(2)}) collective-permute-start(f32[32,128]{1,0:T(8,128)S(1)} %get-tuple-element.33.s.s_in.s_first), channel_id=1, source_target_pairs={{0,16},{16,32},{32,48},{48,64},{64,80},{80,96},{96,112},{112,0},{1... | collective-permute-start | bytes 49160 | tf_op jit(solution)/shard_map/ppermute | solution.py:266
  24.1 9.0 %all_to_all.31 = f32[16,1,2,128]{3,2,1,0:T(2,128)S(1)} all-to-all(f32[16,1,2,128]{3,2,1,0:T(2,128)S(1)} %bitcast.29), channel_id=1, replica_groups=mesh['slab'=8,'tile'=16] {'tile'}, dimensions={0} | all-to-all | bytes 32768 | tf_op jit(solution)/shard_map/all_to_all | solution.py:261
  33.2 0.0 collective-permute-done.1.above
  33.2 0.0 collective-permute-done.below
  33.2 0.0 copy-done.7
  33.2 0.0 copy-done.9
  33.2 0.0 copy-done.10
  33.2 1.8 %residual0.1 = (f32[32,128]{1,0:T(8,128)S(1)}, f32[32,128]{1,0:T(8,128)S(1)}, f32[8,128]{1,0:T(8,128)S(1)}, f32[32,128]{1,0:T(8,128)S(1)}, f32[8,128]{1,0:T(8,128)S(1)}) custom-call(s32[168,128]{1,0:T(8,128)S(1)} %get-tuple-element.28.index, f32[32,128,128]{2,1,0:T(8,128)S(1)} %copy-done.6, f32[32,4,128,128]{3,2,1,0:T(8,128)S(1)} %bitcast.39, ...), custom_call_target="tpu_custom_call" | custom-call | flops 20000000000 | bytes 40000000 | tf_op jit(solution)/shard_map/residual0/pallas_call | solution.py:237
  35.0 9.5 %all_to_all.32 = f32[16,1,2,128]{3,2,1,0:T(2,128)S(1)} all-to-all(f32[16,1,2,128]{3,2,1,0:T(2,128)S(1)} %bitcast.33), channel_id=1, replica_groups=mesh['slab'=8,'tile'=16] {'tile'}, dimensions={0} | all-to-all | bytes 32768 | tf_op jit(solution)/shard_map/all_to_all | solution.py:261
  44.5 1.4 %step1.1 = (f32[32,128]{1,0:T(8,128)S(1)}, f32[32,128]{1,0:T(8,128)S(1)}) custom-call(s32[168,128]{1,0:T(8,128)S(1)} %get-tuple-element.28.index, f32[32,128,128]{2,1,0:T(8,128)S(1)} %copy-done.6, f32[32,4,128,128]{3,2,1,0:T(8,128)S(1)} %bitcast.39, f32[32,128,128]{2,1,0:T(8,128)S(1)} %copy-done.5, f32[32,128]{1,0:T(8,128)S(1)} %get-tuple-element.37.t, ...), custom_call_target="tpu_custom_call" | custom-call | flops 20000000000 | bytes 40000000 | tf_op jit(solution)/shard_map/step1/pallas_call | solution.py:237
  45.9 2.5 %collective-permute-start.3 = (f32[32,128]{1,0:T(8,128)S(1)}, f32[32,128]{1,0:T(8,128)S(1)}, u32[]{:S(2)}, u32[]{:S(2)}) collective-permute-start(f32[32,128]{1,0:T(8,128)S(1)} %get-tuple-element.40.s.s_in.s_before), channel_id=1, source_target_pairs={{16,0},{32,16},{48,32},{64,48},{80,64},{96,80},{112,96},{0,112},{1... | collective-permute-start | bytes 49160 | tf_op jit(solution)/shard_map/ppermute | solution.py:265
  48.4 0.6 collective-permute-start.2
  49.0 9.2 %all_to_all.33 = f32[16,1,2,128]{3,2,1,0:T(2,128)S(1)} all-to-all(f32[16,1,2,128]{3,2,1,0:T(2,128)S(1)} %bitcast.31), channel_id=1, replica_groups=mesh['slab'=8,'tile'=16] {'tile'}, dimensions={0} | all-to-all | bytes 32768 | tf_op jit(solution)/shard_map/all_to_all | solution.py:261
  58.2 0.0 collective-permute-done.3.above
  58.2 0.0 collective-permute-done.2.below
  58.2 1.8 %residual1.1 = (f32[32,128]{1,0:T(8,128)S(1)}, f32[32,128]{1,0:T(8,128)S(1)}, f32[8,128]{1,0:T(8,128)S(1)}, f32[32,128]{1,0:T(8,128)S(1)}) custom-call(s32[168,128]{1,0:T(8,128)S(1)} %get-tuple-element.28.index, f32[32,128,128]{2,1,0:T(8,128)S(1)} %copy-done.6, f32[32,4,128,128]{3,2,1,0:T(8,128)S(1)} %bitcast.39, f32[32,128,128]{2,1,0:T(8,128)S(1)} %copy-done.5, ...), custom_call_target="tpu_custom_call" | custom-call | flops 20000000000 | bytes 40000000 | tf_op jit(solution)/shard_map/residual1/pallas_call | solution.py:237
  60.0 9.5 %all_to_all.34 = f32[16,1,2,128]{3,2,1,0:T(2,128)S(1)} all-to-all(f32[16,1,2,128]{3,2,1,0:T(2,128)S(1)} %bitcast.32), channel_id=1, replica_groups=mesh['slab'=8,'tile'=16] {'tile'}, dimensions={0} | all-to-all | bytes 32768 | tf_op jit(solution)/shard_map/all_to_all | solution.py:261
  69.4 1.4 %step2.1 = (f32[32,128]{1,0:T(8,128)S(1)}, f32[32,128]{1,0:T(8,128)S(1)}) custom-call(s32[168,128]{1,0:T(8,128)S(1)} %get-tuple-element.28.index, f32[32,128,128]{2,1,0:T(8,128)S(1)} %copy-done.6, f32[32,4,128,128]{3,2,1,0:T(8,128)S(1)} %bitcast.39, f32[32,128,128]{2,1,0:T(8,128)S(1)} %copy-done.5, f32[32,128]{1,0:T(8,128)S(1)} %get-tuple-element.44.t, ...), custom_call_target="tpu_custom_call" | custom-call | flops 20000000000 | bytes 40000000 | tf_op jit(solution)/shard_map/step2/pallas_call | solution.py:237
  70.9 2.4 %collective-permute-start.5 = (f32[32,128]{1,0:T(8,128)S(1)}, f32[32,128]{1,0:T(8,128)S(1)}, u32[]{:S(2)}, u32[]{:S(2)}) collective-permute-start(f32[32,128]{1,0:T(8,128)S(1)} %get-tuple-element.47.s), channel_id=1, source_target_pairs={{16,0},{32,16},{48,32},{64,48},{80,64},{96,80},{112,96},{0,112},{1... | collective-permute-start | bytes 49160 | tf_op jit(solution)/shard_map/ppermute | solution.py:265
  73.3 0.6 collective-permute-start.4
  74.0 9.2 %all_to_all.35 = f32[16,1,2,128]{3,2,1,0:T(2,128)S(1)} all-to-all(f32[16,1,2,128]{3,2,1,0:T(2,128)S(1)} %bitcast.30), channel_id=1, replica_groups=mesh['slab'=8,'tile'=16] {'tile'}, dimensions={0} | all-to-all | bytes 32768 | tf_op jit(solution)/shard_map/all_to_all | solution.py:261
  83.1 0.0 collective-permute-done.5.above
  83.1 0.0 collective-permute-done.4.below
  83.1 1.7 %last.1 = (f32[32,128]{1,0:T(8,128)}, f32[32,128]{1,0:T(8,128)}, f32[8,128]{1,0:T(8,128)}) custom-call(s32[168,128]{1,0:T(8,128)S(1)} %get-tuple-element.28.index, f32[32,128,128]{2,1,0:T(8,128)S(1)} %copy-done.6, f32[32,4,128,128]{3,2,1,0:T(8,128)S(1)} %bitcast.39, f32[8,128,128]{2,1,0:T(8,128)S(1)} %copy-done.10, f32[32,128]{1,0:T(8,128)S(1)} %get-tuple-element.47.s, ...), custom_call_target="tpu_custom_call" | custom-call | flops 20000000000 | bytes 40000000 | tf_op jit(solution)/shard_map/last/pallas_call | solution.py:237
  (2 shorter events, 0.0 us)
Async XLA Ops:
  0.6 0.9 %copy-start.4 = (s32[8]{0:T(128)S(1)}, s32[8]{0:T(128)}, u32[]{:S(2)}) copy-start(s32[8]{0:T(128)} %cell.1) | copy-start | bytes 100
  0.6 0.9 %copy-start.1 = (s32[1,16,2]{1,2,0:T(2,128)S(1)}, s32[1,16,2]{1,2,0:T(2,128)}, u32[]{:S(2)}) copy-start(s32[1,16,2]{1,2,0:T(2,128)} %param.21) | copy-start | bytes 388
  0.7 0.9 %copy-start.3 = (s32[32]{0:T(128)S(1)}, s32[32]{0:T(128)}, u32[]{:S(2)}) copy-start(s32[32]{0:T(128)} %vert.1) | copy-start | bytes 388
  0.7 0.9 %copy-start.2 = (s32[32]{0:T(128)S(1)}, s32[32]{0:T(128)}, u32[]{:S(2)}) copy-start(s32[32]{0:T(128)} %margin.1) | copy-start | bytes 388
  0.7 0.9 %copy-start = (s32[32,2]{0,1:T(2,128)S(1)}, s32[32,2]{0,1:T(2,128)}, u32[]{:S(2)}) copy-start(s32[32,2]{0,1:T(2,128)} %param.18) | copy-start | bytes 772
  0.7 1.8 %copy-start.5 = (f32[32,128,128]{2,1,0:T(8,128)S(1)}, f32[32,128,128]{2,1,0:T(8,128)}, u32[]{:S(2)}) copy-start(f32[32,128,128]{2,1,0:T(8,128)} %pre.11) | copy-start | bytes 6291460
  0.7 1.8 %copy-start.11 = (f32[32,128]{1,0:T(8,128)S(1)}, f32[32,128]{1,0:T(8,128)}, u32[]{:S(2)}) copy-start(f32[32,128]{1,0:T(8,128)} %res.1) | copy-start | bytes 49156
  0.7 18.7 %slice-start = ((s8[8388608]{0:T(1024)(128)(4,1)}), s8[4194304]{0:T(1024)(128)(4,1)S(1)}, s32[]{:S(2)}) async-start(s8[8388608]{0:T(1024)(128)(4,1)} %bitcast.38), calls=%async_computation.6 | async-start | bytes 8388608
  2.5 16.9 %slice-start.1 = ((s8[8388608]{0:T(1024)(128)(4,1)}), s8[4194304]{0:T(1024)(128)(4,1)S(1)}, s32[]{:S(2)}) async-start(s8[8388608]{0:T(1024)(128)(4,1)} %bitcast.38), calls=%async_computation.7 | async-start | bytes 8388608
  2.5 16.9 %copy-start.6 = (f32[32,128,128]{2,1,0:T(8,128)S(1)}, f32[32,128,128]{2,1,0:T(8,128)}, u32[]{:S(2)}) copy-start(f32[32,128,128]{2,1,0:T(8,128)} %diag.11) | copy-start | bytes 6291460
  2.5 16.9 %copy-start.8 = (f32[8,128,128]{2,1,0:T(8,128)S(1)}, f32[8,128,128]{2,1,0:T(8,128)}, u32[]{:S(2)}) copy-start(f32[8,128,128]{2,1,0:T(8,128)} %root_pre.5) | copy-start | bytes 1572868
  2.5 16.9 %copy-start.12 = (f32[8,128]{1,0:T(8,128)S(1)}, f32[8,128]{1,0:T(8,128)}, u32[]{:S(2)}) copy-start(f32[8,128]{1,0:T(8,128)} %rr.1) | copy-start | bytes 12292
  19.4 13.7 %copy-start.7 = (f32[8,128,128]{2,1,0:T(8,128)S(1)}, f32[8,128,128]{2,1,0:T(8,128)}, u32[]{:S(2)}) copy-start(f32[8,128,128]{2,1,0:T(8,128)} %root_diag.3) | copy-start | bytes 1572868
  19.4 13.7 %copy-start.9 = (f32[8,128,128]{2,1,0:T(8,128)S(1)}, f32[8,128,128]{2,1,0:T(8,128)}, u32[]{:S(2)}) copy-start(f32[8,128,128]{2,1,0:T(8,128)} %root_up.3) | copy-start | bytes 1572868
  19.5 13.7 %copy-start.10 = (f32[8,128,128]{2,1,0:T(8,128)S(1)}, f32[8,128,128]{2,1,0:T(8,128)}, u32[]{:S(2)}) copy-start(f32[8,128,128]{2,1,0:T(8,128)} %down.5) | copy-start | bytes 1572868
  20.9 12.2 %collective-permute-start.1 = (f32[32,128]{1,0:T(8,128)S(1)}, f32[32,128]{1,0:T(8,128)S(1)}, u32[]{:S(2)}, u32[]{:S(2)}) collective-permute-start(f32[32,128]{1,0:T(8,128)S(1)} %get-tuple-element.33.s.s_in.s_first), channel_id=1, source_target_pairs={{16,0},{32,16},{48,32},{64,48},{80,64},{96,80},{112,96},{0,112},{1... | collective-permute-start | bytes 49160 | tf_op jit(solution)/shard_map/ppermute | solution.py:265
  23.0 10.1 %collective-permute-start = (f32[32,128]{1,0:T(8,128)S(1)}, f32[32,128]{1,0:T(8,128)S(1)}, u32[]{:S(2)}, u32[]{:S(2)}) collective-permute-start(f32[32,128]{1,0:T(8,128)S(1)} %get-tuple-element.33.s.s_in.s_first), channel_id=1, source_target_pairs={{0,16},{16,32},{32,48},{48,64},{64,80},{80,96},{96,112},{112,0},{1... | collective-permute-start | bytes 49160 | tf_op jit(solution)/shard_map/ppermute | solution.py:266
  45.9 12.2 %collective-permute-start.3 = (f32[32,128]{1,0:T(8,128)S(1)}, f32[32,128]{1,0:T(8,128)S(1)}, u32[]{:S(2)}, u32[]{:S(2)}) collective-permute-start(f32[32,128]{1,0:T(8,128)S(1)} %get-tuple-element.40.s.s_in.s_before), channel_id=1, source_target_pairs={{16,0},{32,16},{48,32},{64,48},{80,64},{96,80},{112,96},{0,112},{1... | collective-permute-start | bytes 49160 | tf_op jit(solution)/shard_map/ppermute | solution.py:265
  48.4 9.8 %collective-permute-start.2 = (f32[32,128]{1,0:T(8,128)S(1)}, f32[32,128]{1,0:T(8,128)S(1)}, u32[]{:S(2)}, u32[]{:S(2)}) collective-permute-start(f32[32,128]{1,0:T(8,128)S(1)} %get-tuple-element.40.s.s_in.s_before), channel_id=1, source_target_pairs={{0,16},{16,32},{32,48},{48,64},{64,80},{80,96},{96,112},{112,0},{1... | collective-permute-start | bytes 49160 | tf_op jit(solution)/shard_map/ppermute | solution.py:266
  70.9 12.2 %collective-permute-start.5 = (f32[32,128]{1,0:T(8,128)S(1)}, f32[32,128]{1,0:T(8,128)S(1)}, u32[]{:S(2)}, u32[]{:S(2)}) collective-permute-start(f32[32,128]{1,0:T(8,128)S(1)} %get-tuple-element.47.s), channel_id=1, source_target_pairs={{16,0},{32,16},{48,32},{64,48},{80,64},{96,80},{112,96},{0,112},{1... | collective-permute-start | bytes 49160 | tf_op jit(solution)/shard_map/ppermute | solution.py:265
  73.3 9.8 %collective-permute-start.4 = (f32[32,128]{1,0:T(8,128)S(1)}, f32[32,128]{1,0:T(8,128)S(1)}, u32[]{:S(2)}, u32[]{:S(2)}) collective-permute-start(f32[32,128]{1,0:T(8,128)S(1)} %get-tuple-element.47.s), channel_id=1, source_target_pairs={{0,16},{16,32},{32,48},{48,64},{64,80},{80,96},{96,112},{112,0},{1... | collective-permute-start | bytes 49160 | tf_op jit(solution)/shard_map/ppermute | solution.py:266

commit v7 on v6

--- a/solution.py
+++ b/solution.py
@@ -137,7 +137,11 @@
         )
 
     def turn(g):
-        finish(g, at(t, g) + product((pre[g], at(w, g))))
+        finish(
+            g,
+            at(t, g)
+            + product((pre[g], at(w, g)), sums=matrix_sums if g % 4 == 1 else lane_sums),
+        )
 
     staggered(rows_of, extended, turn)
 

time: 85.1 us -> 84.7 us (level)
  no operation moved by 1% of the time
where the time goes in v7:
time: 84.7 us; the launch traced here: 84.4 us
  blocking collectives  62.6 us (74%)
  Pallas kernels  10.6 us (13%)
  starting transfers between devices  9.41 us (11%)
  between operations  1.7 us (2%)
    all_to_all x6, blocking collectives, exchange(): return lax.all_to_all(pieces, 'tile', 0, 0).reshape(rows.shape)  62.6 us
    pallas_call x9, Pallas kernels, call(): pl.pallas_call(kernel, out_shape=tuple(shapes), in_specs=[SMEM] * len(sca...  10.6 us
    ppermute x3, starting transfers between devices, vertical(): above = lax.ppermute(s, 'slab', [(j, i) for i, j in up])  7.02 us
    ppermute x3, starting transfers between devices, vertical(): return (lax.ppermute(s, 'slab', up), above)  2.39 us
  transfers between devices with their start and end apart: 6, of which 0 were waited for; matrix products, arithmetic and copies ran while one was open for 0% of the time, Pallas kernels for 0%

profile of v7, /device:TPU:1, one launch (start us, length us, event | category | flops | bytes accessed | tf_op | source)
XLA Modules:
  0.0 84.4 jit_solution(8041056444047321444)
XLA Ops:
  0.6 0.0 copy-start.4
  0.6 0.0 copy-start.1
  0.7 0.0 copy-start.3
  0.7 0.0 copy-start.2
  0.7 0.0 copy-start
  0.7 0.0 copy-start.5
  0.7 0.0 copy-start.11
  0.7 0.0 slice-start
  1.5 0.0 copy-done.4
  1.5 0.0 copy-done.1
  1.5 0.0 copy-done.3
  1.6 0.0 copy-done.2
  1.6 0.0 copy-done
  1.6 0.9 %lists.1 = (s32[168,128]{1,0:T(8,128)S(1)}, f32[32,128]{1,0:T(8,128)S(1)}, f32[8,128]{1,0:T(8,128)S(1)}) custom-call(s32[2,32]{1,0:T(2,128)S(1)} %bitcast.36, s32[32]{0:T(128)S(1)} %copy-done.2, s32[32]{0:T(128)S(1)} %copy-done.3, s32[8]{0:T(128)S(1)} %copy-done.4, s32[1,2,16]{2,1,0:T(2,128)S(1)} %bitcast.37, s32[1]{0:T(128)S(6)} %copy.23.count, ...), custom_call_target="tpu_custom_call" | custom-call | flops 1000 | bytes 2 | tf_op jit(solution)/shard_map/lists/pallas_call | solution.py:241
  2.4 0.0 copy-done.5
  2.5 0.0 copy-done.11
  2.5 0.0 slice-start.1
  2.5 0.0 copy-start.6
  2.5 0.0 copy-start.8
  2.5 0.0 copy-start.12
  2.5 0.5 first.1
  3.0 16.4 %all_to_all.30 = f32[16,17,2,128]{3,2,1,0:T(2,128)S(1)} all-to-all(f32[16,17,2,128]{3,2,1,0:T(2,128)S(1)} %bitcast.25), channel_id=1, replica_groups=mesh['slab'=8,'tile'=16] {'tile'}, dimensions={0} | all-to-all | bytes 557056 | tf_op jit(solution)/shard_map/all_to_all | solution.py:265
  19.4 0.0 slice-done
  19.4 0.0 slice-done.1
  19.4 0.0 copy-done.6
  19.4 0.0 copy-done.8
  19.4 0.0 copy-done.12
  19.4 0.0 copy-start.7
  19.4 0.0 copy-start.9
  19.5 0.0 copy-start.10
  19.5 1.3 %step0.1 = (f32[32,128]{1,0:T(8,128)S(1)}, f32[32,128]{1,0:T(8,128)S(1)}, s32[32,128]{1,0:T(8,128)S(1)}, f32[8,128]{1,0:T(8,128)S(1)}) custom-call(s32[168,128]{1,0:T(8,128)S(1)} %get-tuple-element.28.index, f32[8,128]{1,0:T(8,128)S(1)} %get-tuple-element.29.live, f32[32,128,128]{2,1,0:T(8,128)S(1)} %copy-done.6, f32[32,4,128,128]{3,2,1,0:T(8,128)S(1)} %bitcast.39, ...), custom_call_target="tpu_custom_call" | custom-call | flops 20000000000 | bytes 40000000 | tf_op jit(solution)/shard_map/step0/pallas_call | solution.py:241
  20.8 2.1 %collective-permute-start.1 = (f32[32,128]{1,0:T(8,128)S(1)}, f32[32,128]{1,0:T(8,128)S(1)}, u32[]{:S(2)}, u32[]{:S(2)}) collective-permute-start(f32[32,128]{1,0:T(8,128)S(1)} %get-tuple-element.33.s.s_in.s_first), channel_id=1, source_target_pairs={{16,0},{32,16},{48,32},{64,48},{80,64},{96,80},{112,96},{0,112},{1... | collective-permute-start | bytes 49160 | tf_op jit(solution)/shard_map/ppermute | solution.py:269
  22.9 1.1 %collective-permute-start = (f32[32,128]{1,0:T(8,128)S(1)}, f32[32,128]{1,0:T(8,128)S(1)}, u32[]{:S(2)}, u32[]{:S(2)}) collective-permute-start(f32[32,128]{1,0:T(8,128)S(1)} %get-tuple-element.33.s.s_in.s_first), channel_id=1, source_target_pairs={{0,16},{16,32},{32,48},{48,64},{64,80},{80,96},{96,112},{112,0},{1... | collective-permute-start | bytes 49160 | tf_op jit(solution)/shard_map/ppermute | solution.py:270
  24.0 9.0 %all_to_all.31 = f32[16,1,2,128]{3,2,1,0:T(2,128)S(1)} all-to-all(f32[16,1,2,128]{3,2,1,0:T(2,128)S(1)} %bitcast.29), channel_id=1, replica_groups=mesh['slab'=8,'tile'=16] {'tile'}, dimensions={0} | all-to-all | bytes 32768 | tf_op jit(solution)/shard_map/all_to_all | solution.py:265
  33.0 0.0 collective-permute-done.1.above
  33.0 0.0 collective-permute-done.below
  33.0 0.0 copy-done.7
  33.1 0.0 copy-done.9
  33.1 0.0 copy-done.10
  33.1 1.8 %residual0.1 = (f32[32,128]{1,0:T(8,128)S(1)}, f32[32,128]{1,0:T(8,128)S(1)}, f32[8,128]{1,0:T(8,128)S(1)}, f32[32,128]{1,0:T(8,128)S(1)}, f32[8,128]{1,0:T(8,128)S(1)}) custom-call(s32[168,128]{1,0:T(8,128)S(1)} %get-tuple-element.28.index, f32[32,128,128]{2,1,0:T(8,128)S(1)} %copy-done.6, f32[32,4,128,128]{3,2,1,0:T(8,128)S(1)} %bitcast.39, ...), custom_call_target="tpu_custom_call" | custom-call | flops 20000000000 | bytes 40000000 | tf_op jit(solution)/shard_map/residual0/pallas_call | solution.py:241
  34.9 9.5 %all_to_all.32 = f32[16,1,2,128]{3,2,1,0:T(2,128)S(1)} all-to-all(f32[16,1,2,128]{3,2,1,0:T(2,128)S(1)} %bitcast.33), channel_id=1, replica_groups=mesh['slab'=8,'tile'=16] {'tile'}, dimensions={0} | all-to-all | bytes 32768 | tf_op jit(solution)/shard_map/all_to_all | solution.py:265
  44.4 1.3 %step1.1 = (f32[32,128]{1,0:T(8,128)S(1)}, f32[32,128]{1,0:T(8,128)S(1)}) custom-call(s32[168,128]{1,0:T(8,128)S(1)} %get-tuple-element.28.index, f32[32,128,128]{2,1,0:T(8,128)S(1)} %copy-done.6, f32[32,4,128,128]{3,2,1,0:T(8,128)S(1)} %bitcast.39, f32[32,128,128]{2,1,0:T(8,128)S(1)} %copy-done.5, f32[32,128]{1,0:T(8,128)S(1)} %get-tuple-element.37.t, ...), custom_call_target="tpu_custom_call" | custom-call | flops 20000000000 | bytes 40000000 | tf_op jit(solution)/shard_map/step1/pallas_call | solution.py:241
  45.7 2.5 %collective-permute-start.3 = (f32[32,128]{1,0:T(8,128)S(1)}, f32[32,128]{1,0:T(8,128)S(1)}, u32[]{:S(2)}, u32[]{:S(2)}) collective-permute-start(f32[32,128]{1,0:T(8,128)S(1)} %get-tuple-element.40.s.s_in.s_before), channel_id=1, source_target_pairs={{16,0},{32,16},{48,32},{64,48},{80,64},{96,80},{112,96},{0,112},{1... | collective-permute-start | bytes 49160 | tf_op jit(solution)/shard_map/ppermute | solution.py:269
  48.1 0.6 collective-permute-start.2
  48.8 9.2 %all_to_all.33 = f32[16,1,2,128]{3,2,1,0:T(2,128)S(1)} all-to-all(f32[16,1,2,128]{3,2,1,0:T(2,128)S(1)} %bitcast.31), channel_id=1, replica_groups=mesh['slab'=8,'tile'=16] {'tile'}, dimensions={0} | all-to-all | bytes 32768 | tf_op jit(solution)/shard_map/all_to_all | solution.py:265
  57.9 0.0 collective-permute-done.3.above
  57.9 0.0 collective-permute-done.2.below
  57.9 1.8 %residual1.1 = (f32[32,128]{1,0:T(8,128)S(1)}, f32[32,128]{1,0:T(8,128)S(1)}, f32[8,128]{1,0:T(8,128)S(1)}, f32[32,128]{1,0:T(8,128)S(1)}) custom-call(s32[168,128]{1,0:T(8,128)S(1)} %get-tuple-element.28.index, f32[32,128,128]{2,1,0:T(8,128)S(1)} %copy-done.6, f32[32,4,128,128]{3,2,1,0:T(8,128)S(1)} %bitcast.39, f32[32,128,128]{2,1,0:T(8,128)S(1)} %copy-done.5, ...), custom_call_target="tpu_custom_call" | custom-call | flops 20000000000 | bytes 40000000 | tf_op jit(solution)/shard_map/residual1/pallas_call | solution.py:241
  59.8 9.5 %all_to_all.34 = f32[16,1,2,128]{3,2,1,0:T(2,128)S(1)} all-to-all(f32[16,1,2,128]{3,2,1,0:T(2,128)S(1)} %bitcast.32), channel_id=1, replica_groups=mesh['slab'=8,'tile'=16] {'tile'}, dimensions={0} | all-to-all | bytes 32768 | tf_op jit(solution)/shard_map/all_to_all | solution.py:265
  69.2 1.3 %step2.1 = (f32[32,128]{1,0:T(8,128)S(1)}, f32[32,128]{1,0:T(8,128)S(1)}) custom-call(s32[168,128]{1,0:T(8,128)S(1)} %get-tuple-element.28.index, f32[32,128,128]{2,1,0:T(8,128)S(1)} %copy-done.6, f32[32,4,128,128]{3,2,1,0:T(8,128)S(1)} %bitcast.39, f32[32,128,128]{2,1,0:T(8,128)S(1)} %copy-done.5, f32[32,128]{1,0:T(8,128)S(1)} %get-tuple-element.44.t, ...), custom_call_target="tpu_custom_call" | custom-call | flops 20000000000 | bytes 40000000 | tf_op jit(solution)/shard_map/step2/pallas_call | solution.py:241
  70.5 2.5 %collective-permute-start.5 = (f32[32,128]{1,0:T(8,128)S(1)}, f32[32,128]{1,0:T(8,128)S(1)}, u32[]{:S(2)}, u32[]{:S(2)}) collective-permute-start(f32[32,128]{1,0:T(8,128)S(1)} %get-tuple-element.47.s), channel_id=1, source_target_pairs={{16,0},{32,16},{48,32},{64,48},{80,64},{96,80},{112,96},{0,112},{1... | collective-permute-start | bytes 49160 | tf_op jit(solution)/shard_map/ppermute | solution.py:269
  73.0 0.6 collective-permute-start.4
  73.6 9.2 %all_to_all.35 = f32[16,1,2,128]{3,2,1,0:T(2,128)S(1)} all-to-all(f32[16,1,2,128]{3,2,1,0:T(2,128)S(1)} %bitcast.30), channel_id=1, replica_groups=mesh['slab'=8,'tile'=16] {'tile'}, dimensions={0} | all-to-all | bytes 32768 | tf_op jit(solution)/shard_map/all_to_all | solution.py:265
  82.8 0.0 collective-permute-done.5.above
  82.8 0.0 collective-permute-done.4.below
  82.8 1.6 %last.1 = (f32[32,128]{1,0:T(8,128)}, f32[32,128]{1,0:T(8,128)}, f32[8,128]{1,0:T(8,128)}) custom-call(s32[168,128]{1,0:T(8,128)S(1)} %get-tuple-element.28.index, f32[32,128,128]{2,1,0:T(8,128)S(1)} %copy-done.6, f32[32,4,128,128]{3,2,1,0:T(8,128)S(1)} %bitcast.39, f32[8,128,128]{2,1,0:T(8,128)S(1)} %copy-done.10, f32[32,128]{1,0:T(8,128)S(1)} %get-tuple-element.47.s, ...), custom_call_target="tpu_custom_call" | custom-call | flops 20000000000 | bytes 40000000 | tf_op jit(solution)/shard_map/last/pallas_call | solution.py:241
  (2 shorter events, 0.0 us)
Async XLA Ops:
  0.6 0.9 %copy-start.4 = (s32[8]{0:T(128)S(1)}, s32[8]{0:T(128)}, u32[]{:S(2)}) copy-start(s32[8]{0:T(128)} %cell.1) | copy-start | bytes 100
  0.6 0.9 %copy-start.1 = (s32[1,16,2]{1,2,0:T(2,128)S(1)}, s32[1,16,2]{1,2,0:T(2,128)}, u32[]{:S(2)}) copy-start(s32[1,16,2]{1,2,0:T(2,128)} %param.21) | copy-start | bytes 388
  0.7 0.9 %copy-start.3 = (s32[32]{0:T(128)S(1)}, s32[32]{0:T(128)}, u32[]{:S(2)}) copy-start(s32[32]{0:T(128)} %vert.1) | copy-start | bytes 388
  0.7 0.9 %copy-start.2 = (s32[32]{0:T(128)S(1)}, s32[32]{0:T(128)}, u32[]{:S(2)}) copy-start(s32[32]{0:T(128)} %margin.1) | copy-start | bytes 388
  0.7 0.9 %copy-start = (s32[32,2]{0,1:T(2,128)S(1)}, s32[32,2]{0,1:T(2,128)}, u32[]{:S(2)}) copy-start(s32[32,2]{0,1:T(2,128)} %param.18) | copy-start | bytes 772
  0.7 1.8 %copy-start.5 = (f32[32,128,128]{2,1,0:T(8,128)S(1)}, f32[32,128,128]{2,1,0:T(8,128)}, u32[]{:S(2)}) copy-start(f32[32,128,128]{2,1,0:T(8,128)} %pre.11) | copy-start | bytes 6291460
  0.7 1.8 %copy-start.11 = (f32[32,128]{1,0:T(8,128)S(1)}, f32[32,128]{1,0:T(8,128)}, u32[]{:S(2)}) copy-start(f32[32,128]{1,0:T(8,128)} %res.1) | copy-start | bytes 49156
  0.7 18.7 %slice-start = ((s8[8388608]{0:T(1024)(128)(4,1)}), s8[4194304]{0:T(1024)(128)(4,1)S(1)}, s32[]{:S(2)}) async-start(s8[8388608]{0:T(1024)(128)(4,1)} %bitcast.38), calls=%async_computation.6 | async-start | bytes 8388608
  2.5 16.9 %slice-start.1 = ((s8[8388608]{0:T(1024)(128)(4,1)}), s8[4194304]{0:T(1024)(128)(4,1)S(1)}, s32[]{:S(2)}) async-start(s8[8388608]{0:T(1024)(128)(4,1)} %bitcast.38), calls=%async_computation.7 | async-start | bytes 8388608
  2.5 16.9 %copy-start.6 = (f32[32,128,128]{2,1,0:T(8,128)S(1)}, f32[32,128,128]{2,1,0:T(8,128)}, u32[]{:S(2)}) copy-start(f32[32,128,128]{2,1,0:T(8,128)} %diag.11) | copy-start | bytes 6291460
  2.5 16.9 %copy-start.8 = (f32[8,128,128]{2,1,0:T(8,128)S(1)}, f32[8,128,128]{2,1,0:T(8,128)}, u32[]{:S(2)}) copy-start(f32[8,128,128]{2,1,0:T(8,128)} %root_pre.5) | copy-start | bytes 1572868
  2.5 16.9 %copy-start.12 = (f32[8,128]{1,0:T(8,128)S(1)}, f32[8,128]{1,0:T(8,128)}, u32[]{:S(2)}) copy-start(f32[8,128]{1,0:T(8,128)} %rr.1) | copy-start | bytes 12292
  19.4 13.6 %copy-start.7 = (f32[8,128,128]{2,1,0:T(8,128)S(1)}, f32[8,128,128]{2,1,0:T(8,128)}, u32[]{:S(2)}) copy-start(f32[8,128,128]{2,1,0:T(8,128)} %root_diag.3) | copy-start | bytes 1572868
  19.4 13.6 %copy-start.9 = (f32[8,128,128]{2,1,0:T(8,128)S(1)}, f32[8,128,128]{2,1,0:T(8,128)}, u32[]{:S(2)}) copy-start(f32[8,128,128]{2,1,0:T(8,128)} %root_up.3) | copy-start | bytes 1572868
  19.5 13.6 %copy-start.10 = (f32[8,128,128]{2,1,0:T(8,128)S(1)}, f32[8,128,128]{2,1,0:T(8,128)}, u32[]{:S(2)}) copy-start(f32[8,128,128]{2,1,0:T(8,128)} %down.5) | copy-start | bytes 1572868
  20.8 12.2 %collective-permute-start.1 = (f32[32,128]{1,0:T(8,128)S(1)}, f32[32,128]{1,0:T(8,128)S(1)}, u32[]{:S(2)}, u32[]{:S(2)}) collective-permute-start(f32[32,128]{1,0:T(8,128)S(1)} %get-tuple-element.33.s.s_in.s_first), channel_id=1, source_target_pairs={{16,0},{32,16},{48,32},{64,48},{80,64},{96,80},{112,96},{0,112},{1... | collective-permute-start | bytes 49160 | tf_op jit(solution)/shard_map/ppermute | solution.py:269
  22.9 10.1 %collective-permute-start = (f32[32,128]{1,0:T(8,128)S(1)}, f32[32,128]{1,0:T(8,128)S(1)}, u32[]{:S(2)}, u32[]{:S(2)}) collective-permute-start(f32[32,128]{1,0:T(8,128)S(1)} %get-tuple-element.33.s.s_in.s_first), channel_id=1, source_target_pairs={{0,16},{16,32},{32,48},{48,64},{64,80},{80,96},{96,112},{112,0},{1... | collective-permute-start | bytes 49160 | tf_op jit(solution)/shard_map/ppermute | solution.py:270
  45.7 12.2 %collective-permute-start.3 = (f32[32,128]{1,0:T(8,128)S(1)}, f32[32,128]{1,0:T(8,128)S(1)}, u32[]{:S(2)}, u32[]{:S(2)}) collective-permute-start(f32[32,128]{1,0:T(8,128)S(1)} %get-tuple-element.40.s.s_in.s_before), channel_id=1, source_target_pairs={{16,0},{32,16},{48,32},{64,48},{80,64},{96,80},{112,96},{0,112},{1... | collective-permute-start | bytes 49160 | tf_op jit(solution)/shard_map/ppermute | solution.py:269
  48.1 9.8 %collective-permute-start.2 = (f32[32,128]{1,0:T(8,128)S(1)}, f32[32,128]{1,0:T(8,128)S(1)}, u32[]{:S(2)}, u32[]{:S(2)}) collective-permute-start(f32[32,128]{1,0:T(8,128)S(1)} %get-tuple-element.40.s.s_in.s_before), channel_id=1, source_target_pairs={{0,16},{16,32},{32,48},{48,64},{64,80},{80,96},{96,112},{112,0},{1... | collective-permute-start | bytes 49160 | tf_op jit(solution)/shard_map/ppermute | solution.py:270
  70.5 12.3 %collective-permute-start.5 = (f32[32,128]{1,0:T(8,128)S(1)}, f32[32,128]{1,0:T(8,128)S(1)}, u32[]{:S(2)}, u32[]{:S(2)}) collective-permute-start(f32[32,128]{1,0:T(8,128)S(1)} %get-tuple-element.47.s), channel_id=1, source_target_pairs={{16,0},{32,16},{48,32},{64,48},{80,64},{96,80},{112,96},{0,112},{1... | collective-permute-start | bytes 49160 | tf_op jit(solution)/shard_map/ppermute | solution.py:269
  73.0 9.8 %collective-permute-start.4 = (f32[32,128]{1,0:T(8,128)S(1)}, f32[32,128]{1,0:T(8,128)S(1)}, u32[]{:S(2)}, u32[]{:S(2)}) collective-permute-start(f32[32,128]{1,0:T(8,128)S(1)} %get-tuple-element.47.s), channel_id=1, source_target_pairs={{0,16},{16,32},{32,48},{48,64},{64,80},{80,96},{96,112},{112,0},{1... | collective-permute-start | bytes 49160 | tf_op jit(solution)/shard_map/ppermute | solution.py:270
